TPU v7x, 32 devices: a whole 2x2x4 slice. The times are simulated.
32 devices in a mesh: space: 4 (over z), member: 8 (over y, x, core).
Axes of the slice: x: 2, y: 2, z: 4, core: 2. Of those that a mesh axis runs over, the one named last changes fastest.
Arguments:
- prior_ensemble: float32 [32, 32, 512], P('member', None, 'space'), may hold values from -12 to 12, as said below
- wind: float32 [32, 512], P(None, 'space'), may hold values from -1 to 1
- obs_value: float32 [32, 512], P(('space', 'member')), may hold values from -6 to 6
- obs_weight: float32 [32, 512], P(('space', 'member')), may hold values from 0.25 to 4
- observed_cell_value: int32 [32, 512], P(('space', 'member')), may hold values from 0 to 511
- obs_count: int32 [32], P(('space', 'member')), may hold values from 64 to 512, as said below
Outputs:
- analysis: float32 [32, 32, 512], P('member', None, 'space')
Inputs may be any that keep to these rules, and one draw needn't show every extreme that they name: `prior_ensemble`: member states are rough from cell to cell, member scales differ. `obs_count`: some patch has all 512 slots live and some has 64 live.
All inputs are finite; a program needn't handle non-finite values.
Results may differ from a plain program's by a relative error of at most 0.0003.
Values sent between devices are 32-bit elements; how exact they have to be, the bound alone decides.
No kernel may reach another device: no remote copies, remote signals or barrier semaphores. Data moves between devices by JAX's collectives and lax.ppermute only.
A program may use at most 64 MiB of HBM per device.

v0:
```python
import jax
import jax.numpy as jnp
from jax import lax
from jax.sharding import PartitionSpec as P

SUBSTEPS = 4
NS_ITERS = 6


def padded(block, sides, width):
    for axis, dim in sides:
        count = lax.axis_size(axis)
        forward = [(i, i + 1) for i in range(count - 1)]
        forward.append((count - 1, 0))
        backward = [(target, source) for source, target in forward]
        low = lax.ppermute(
            lax.slice_in_dim(block, block.shape[dim] - width, None, axis=dim), axis, forward
        )
        high = lax.ppermute(lax.slice_in_dim(block, 0, width, axis=dim), axis, backward)
        block = jnp.concatenate([low, block, high], axis=dim)
    return block


def tendency(center, east, west, wind_mid):
    pads = [(0, 0)] * (center.ndim - 2) + [(1, 1), (0, 0)]
    ypad = jnp.pad(center, pads)
    north = ypad[..., 2:, :]
    south = ypad[..., :-2, :]
    speed = wind_mid + 0.25 * jnp.tanh(center)
    return (
        center
        + 0.2 * (east - 2.0 * center + west)
        + 0.1 * (north - 2.0 * center + south)
        - 0.3 * speed * (east - west)
    )


def inverse_root(gram):
    order = gram.shape[0]
    ident = jnp.eye(order, dtype=jnp.float32)
    scale = jnp.sqrt(jnp.sum(gram * gram) + 1e-06)
    upper = gram / scale
    lower = ident
    for step in range(NS_ITERS):
        middle = 1.5 * ident - 0.5 * jnp.dot(lower, upper, precision=lax.Precision.HIGHEST)
        upper = jnp.dot(upper, middle, precision=lax.Precision.HIGHEST)
        lower = jnp.dot(middle, lower, precision=lax.Precision.HIGHEST)
    return lower / jnp.sqrt(scale)


def analyze(xb, cells, value, weight, count):
    order = xb.shape[0]
    slots = cells.shape[0]
    mean = jnp.sum(xb, axis=0) / order
    pert = xb - mean
    start_gram = (order - 1.0) * jnp.eye(order, dtype=jnp.float32)
    ypert = jnp.take(pert, cells, axis=1)
    ymean = jnp.take(mean, cells)
    live = (jnp.arange(slots, dtype=jnp.int32) < count).astype(jnp.float32)
    wts = weight * live
    gram = start_gram + jnp.dot(ypert * wts, ypert.T, precision=lax.Precision.HIGHEST)
    rhs = jnp.dot(ypert, wts * (value - ymean), precision=lax.Precision.HIGHEST)
    root = inverse_root(gram)
    wbar = jnp.dot(
        root, jnp.dot(root, rhs, precision=lax.Precision.HIGHEST), precision=lax.Precision.HIGHEST
    )
    trans = jnp.sqrt(order - 1.0) * root + wbar[:, None]
    return mean + jnp.dot(trans.T, pert, precision=lax.Precision.HIGHEST)


def local(prior_ensemble, wind, obs_value, obs_weight, observed_cell_value, obs_count):
    model_variable = prior_ensemble
    stacked = jnp.concatenate([model_variable, wind[None]], axis=0)
    extended = padded(stacked, (("space", 2),), SUBSTEPS)
    state = extended[:-1]
    wind_ext = extended[-1]
    for step in range(SUBSTEPS):
        edge = step + 1
        wind_mid = wind_ext[:, edge : wind_ext.shape[1] - edge]
        state = tendency(state[..., 1:-1], state[..., 2:], state[..., :-2], wind_mid)
    model_variable = state
    mem_here, latitude_lines, column_entries = model_variable.shape
    groups = lax.axis_size("member")
    per_dev = obs_count.shape[0]
    cell_count = latitude_lines * column_entries // (groups * per_dev)
    blocks = model_variable.reshape(mem_here, groups, per_dev, cell_count)
    arrived = lax.all_to_all(blocks, "member", split_axis=1, concat_axis=0, tiled=True)
    output_results = [
        analyze(arrived[:, 0, 0], observed_cell_value[0], obs_value[0], obs_weight[0], obs_count[0])
    ]
    analysed_state = jnp.stack(output_results, axis=1)[:, None]
    returned = lax.all_to_all(analysed_state, "member", split_axis=0, concat_axis=1, tiled=True)
    return returned.reshape(mem_here, latitude_lines, column_entries)


def solution(mesh):
    in_specs = (
        P("member", None, "space"),
        P(None, "space"),
        P(("space", "member"), None),
        P(("space", "member"), None),
        P(("space", "member"), None),
        P(("space", "member")),
    )
    out_specs = P("member", None, "space")
    return jax.shard_map(local, mesh=mesh, in_specs=in_specs, out_specs=out_specs, check_vma=False)
```

profile of v0, /device:TPU:0, one launch (start us, length us, event | category | flops | bytes accessed | tf_op | source)
XLA Modules:
  0.0 40.0 jit_solution(312560310919123988)
XLA Ops:
  0.0 1.1 %slice_maximum_fusion = (f32[5,32,4]{2,1,0:T(8,128)S(1)}, f32[5,32,4]{2,1,0:T(8,128)S(1)}) fusion(f32[1,32,128]{2,1,0:T(8,128)} %bitcast.80, f32[4,32,128]{2,1,0:T(8,128)} %param.6), kind=kLoop, calls=%fused_computation.55 | loop fusion | flops 1280 | bytes 87040 | tf_op jit(solution)/shard_map/concatenate | solution.py:73
  1.1 3.1 %collective-permute-start = (f32[5,32,4]{2,1,0:T(8,128)S(1)}, f32[5,32,4]{2,1,0:T(8,128)S(1)}, u32[]{:S(2)}, u32[]{:S(2)}) collective-permute-start(f32[5,32,4]{2,1,0:T(8,128)S(1)} %get-tuple-element.7), channel_id=1, source_target_pairs={{0,8},{8,16},{16,24},{24,0},{1,9},{9,17},{17,25},{25,1},{2,10},{10... | collective-permute-start | bytes 7688 | tf_op jit(solution)/shard_map/ppermute | solution.py:16
  4.2 2.1 %collective-permute-start.1 = (f32[5,32,4]{2,1,0:T(8,128)S(1)}, f32[5,32,4]{2,1,0:T(8,128)S(1)}, u32[]{:S(2)}, u32[]{:S(2)}) collective-permute-start(f32[5,32,4]{2,1,0:T(8,128)S(1)} %get-tuple-element.8), channel_id=1, source_target_pairs={{8,0},{16,8},{24,16},{0,24},{9,1},{17,9},{25,17},{1,25},{10,2},{18... | collective-permute-start | bytes 7688 | tf_op jit(solution)/shard_map/ppermute | solution.py:19
  6.9 2.0 %collective-permute-done = f32[5,32,4]{2,1,0:T(8,128)S(1)} collective-permute-done((f32[5,32,4]{2,1,0:T(8,128)S(1)}, f32[5,32,4]{2,1,0:T(8,128)S(1)}, u32[]{:S(2)}, u32[]{:S(2)}) %collective-permute-start) | collective-permute-done | bytes 2592 | tf_op jit(solution)/shard_map/ppermute | solution.py:16
  9.0 0.8 %collective-permute-done.1 = f32[5,32,4]{2,1,0:T(8,128)S(1)} collective-permute-done((f32[5,32,4]{2,1,0:T(8,128)S(1)}, f32[5,32,4]{2,1,0:T(8,128)S(1)}, u32[]{:S(2)}, u32[]{:S(2)}) %collective-permute-start.1) | collective-permute-done | bytes 2592 | tf_op jit(solution)/shard_map/ppermute | solution.py:19
  10.2 0.1 pad_maximum_fusion
  11.3 0.7 %copy.16 = f32[4,8,1,512]{3,0,2,1:T(4,128)} copy(f32[4,8,1,512]{3,1,0,2:T(8,128)S(1)} %reshape.57) | data formatting | bytes 131072 | tf_op jit(solution)/shard_map/reshape | solution.py:86
  11.9 3.7 %all-to-all-start = ((f32[4,8,1,512]{3,0,2,1:T(4,128)}), f32[4,8,1,512]{3,0,2,1:T(4,128)S(1)}, u32[]{:S(2)}, u32[]{:S(2)}) async-start(f32[4,8,1,512]{3,0,2,1:T(4,128)} %copy.16), calls=%async_computation | async-start | bytes 131072 | tf_op jit(solution)/shard_map/all_to_all | solution.py:87
  15.7 5.0 %all-to-all-done = f32[4,8,1,512]{3,0,2,1:T(4,128)S(1)} async-done(((f32[4,8,1,512]{3,0,2,1:T(4,128)}), f32[4,8,1,512]{3,0,2,1:T(4,128)S(1)}, u32[]{:S(2)}, u32[]{:S(2)}) %all-to-all-start) | async-done | bytes 65568 | tf_op jit(solution)/shard_map/all_to_all | solution.py:87
  20.9 3.5 %gather_fusion.1 = f32[512]{0:T(512)S(1)} fusion(f32[512]{0:T(512)S(1)} %broadcast_multiply_fusion, s32[1024]{0:T(1024)S(1)} %pad_clamp_fusion), kind=kCustom, calls=%fused_computation.1 | custom fusion | bytes 6144 | tf_op jit(solution)/shard_map/jit(_take)/gather | solution.py:58
  24.4 1.0 %gather_fusion = f32[512,32]{1,0:T(8,128)S(1)} fusion(f32[32,512]{0,1:T(8,128)S(1)} %copy.17, s32[1024]{0:T(1024)S(1)} %pad_clamp_fusion), kind=kCustom, calls=%fused_computation | custom fusion | bytes 133120 | tf_op jit(solution)/shard_map/jit(_take)/gather | solution.py:57
  25.5 0.7 %copy-done.4 = f32[1,512]{1,0:T(1,128)S(1)} copy-done((f32[1,512]{1,0:T(1,128)S(1)}, f32[1,512]{1,0:T(1,128)}, u32[]{:S(2)}) %copy-start.4) | copy-done | bytes 2072
  26.1 1.5 %multiply_reduce_fusion = (f32[]{:T(128)}, f32[32,32]{1,0:T(8,128)S(1)}) fusion(f32[512,32]{1,0:T(8,128)S(1)} %gather_fusion, pred[512]{0:T(512)(128)(4,1)S(1)} %get-tuple-element.6, f32[512]{0:T(512)S(1)} %bitcast.83), kind=kOutput, calls=%fused_computation.65 | convolution fusion | flops 6345727 | bytes 72196 | tf_op jit(solution)/shard_map/dot_general | solution.py:61
  28.4 0.1 fusion.40
  28.7 0.2 fusion.5
  28.9 0.1 fusion.45
  29.0 0.1 fusion.44
  29.2 0.2 fusion.4
  29.5 0.1 fusion.46
  29.6 0.2 fusion.3
  29.8 0.1 fusion.49
  29.9 0.1 fusion.48
  30.1 0.2 fusion.2
  30.4 0.1 fusion.50
  30.6 0.3 convolution_bitcast_fusion
  30.9 0.1 fusion.1
  31.1 0.1 convolution_divide_fusion
  31.2 0.1 convolution_bitcast_fusion.2
  31.4 0.2 convolution_bitcast_fusion.1
  31.5 0.3 fusion
  32.0 7.4 %all_to_all.30 = f32[32,1,1,512]{3,2,1,0:T(1,128)S(1)} all-to-all(f32[32,1,1,512]{3,2,1,0:T(1,128)S(1)} %copy.18), channel_id=1, replica_groups=mesh['space'=4,'member'=8] {'member'}, dimensions={0} | all-to-all | bytes 131072 | tf_op jit(solution)/shard_map/all_to_all | solution.py:92
  39.4 0.6 %reshape.58 = f32[4,32,128]{2,1,0:T(8,128)} reshape(f32[4,8,1,1,512]{4,1,0,3,2:T(8,128)S(1)} %copy.19) | data formatting | bytes 131072 | tf_op jit(solution)/shard_map/reshape | solution.py:93
  (38 shorter events, 2.1 us)
Async XLA Ops:
  0.0 6.3 %copy-start.2 = (s32[1,512]{1,0:T(1,128)S(1)}, s32[1,512]{1,0:T(1,128)}, u32[]{:S(2)}) copy-start(s32[1,512]{1,0:T(1,128)} %param.10) | copy-start | bytes 6148
  0.0 6.9 %copy-start.3 = (f32[1,512]{1,0:T(1,128)S(1)}, f32[1,512]{1,0:T(1,128)}, u32[]{:S(2)}) copy-start(f32[1,512]{1,0:T(1,128)} %param.9) | copy-start | bytes 6148
  0.0 9.8 %copy-start = (f32[4,32,128]{2,1,0:T(8,128)S(1)}, f32[4,32,128]{2,1,0:T(8,128)}, u32[]{:S(2)}) copy-start(f32[4,32,128]{2,1,0:T(8,128)} %param.6) | copy-start | bytes 196612
  1.1 8.8 %copy-start.1 = (f32[32,128]{1,0:T(8,128)S(1)}, f32[32,128]{1,0:T(8,128)}, u32[]{:S(2)}) copy-start(f32[32,128]{1,0:T(8,128)} %param.7) | copy-start | bytes 49156
  1.1 7.9 %collective-permute-start = (f32[5,32,4]{2,1,0:T(8,128)S(1)}, f32[5,32,4]{2,1,0:T(8,128)S(1)}, u32[]{:S(2)}, u32[]{:S(2)}) collective-permute-start(f32[5,32,4]{2,1,0:T(8,128)S(1)} %get-tuple-element.7), channel_id=1, source_target_pairs={{0,8},{8,16},{16,24},{24,0},{1,9},{9,17},{17,25},{25,1},{2,10},{10... | collective-permute-start | bytes 7688 | tf_op jit(solution)/shard_map/ppermute | solution.py:16
  4.2 5.7 %collective-permute-start.1 = (f32[5,32,4]{2,1,0:T(8,128)S(1)}, f32[5,32,4]{2,1,0:T(8,128)S(1)}, u32[]{:S(2)}, u32[]{:S(2)}) collective-permute-start(f32[5,32,4]{2,1,0:T(8,128)S(1)} %get-tuple-element.8), channel_id=1, source_target_pairs={{8,0},{16,8},{24,16},{0,24},{9,1},{17,9},{25,17},{1,25},{10,2},{18... | collective-permute-start | bytes 7688 | tf_op jit(solution)/shard_map/ppermute | solution.py:19
  11.9 8.7 %all-to-all-start = ((f32[4,8,1,512]{3,0,2,1:T(4,128)}), f32[4,8,1,512]{3,0,2,1:T(4,128)S(1)}, u32[]{:S(2)}, u32[]{:S(2)}) async-start(f32[4,8,1,512]{3,0,2,1:T(4,128)} %copy.16), calls=%async_computation | async-start | bytes 131072 | tf_op jit(solution)/shard_map/all_to_all | solution.py:87
  25.4 0.7 %copy-start.4 = (f32[1,512]{1,0:T(1,128)S(1)}, f32[1,512]{1,0:T(1,128)}, u32[]{:S(2)}) copy-start(f32[1,512]{1,0:T(1,128)} %param.8) | copy-start | bytes 6148
where the time goes:
time: 40.4 us; the launch traced here: 40 us
  starting transfers between devices  8.89 us (22%)
  waiting for transfers between devices  7.89 us (20%)
  local copies, waits for them, and re-layouts  7.43 us (18%)
  blocking collectives  7.4 us (18%)
  matrix products  4.91 us (12%)
  other arithmetic  1.83 us (5%)
  between operations  1.67 us (4%)
    all_to_all x1, blocking collectives, local(): lax.all_to_all(analysed_state, 'member', split_axis=0, concat_axis=1, til...  7.4 us
    all_to_all x1, waiting for transfers between devices, local(): lax.all_to_all(blocks, 'member', split_axis=1, concat_axis=0, tiled=True)  5.01 us
    all_to_all x1, starting transfers between devices, local(): lax.all_to_all(blocks, 'member', split_axis=1, concat_axis=0, tiled=True)  3.72 us
    gather x1, local copies, waits for them, and re-layouts, analyze(): ymean = jnp.take(mean, cells)  3.49 us
    ppermute x1, starting transfers between devices, padded(): lax.ppermute(lax.slice_in_dim(block, block.shape[dim] - width, None, axis...  3.08 us
    ppermute x1, starting transfers between devices, padded(): lax.ppermute(lax.slice_in_dim(block, 0, width, axis=dim), axis, backward)  2.09 us
    ppermute x1, waiting for transfers between devices, padded(): lax.ppermute(lax.slice_in_dim(block, block.shape[dim] - width, None, axis...  2.04 us
    dot_general x1, matrix products, analyze(): jnp.dot(ypert * wts, ypert.T, precision=lax.Precision.HIGHEST)  1.45 us
  transfers between devices with their start and end apart: 3, of which 3 were waited for; matrix products, arithmetic and copies ran while one was open for 0% of the time, Pallas kernels for 0%

commit v1 on v0

--- a/solution.py
+++ b/solution.py
@@ -1,10 +1,17 @@
+import functools
+
 import jax
 import jax.numpy as jnp
 from jax import lax
+from jax.experimental import pallas as pl
+from jax.experimental.pallas import tpu as pltpu
 from jax.sharding import PartitionSpec as P
 
 SUBSTEPS = 4
 NS_ITERS = 6
+LANES = 128
+STRIP = 32
+GATHER_BYTES = 4 << 20
 
 
 def padded(block, sides, width):
@@ -68,9 +75,8 @@
     return mean + jnp.dot(trans.T, pert, precision=lax.Precision.HIGHEST)
 
 
-def local(prior_ensemble, wind, obs_value, obs_weight, observed_cell_value, obs_count):
-    model_variable = prior_ensemble
-    stacked = jnp.concatenate([model_variable, wind[None]], axis=0)
+def exchanged(prior_ensemble, wind, obs_value, obs_weight, observed_cell_value, obs_count):
+    stacked = jnp.concatenate([prior_ensemble, wind[None]], axis=0)
     extended = padded(stacked, (("space", 2),), SUBSTEPS)
     state = extended[:-1]
     wind_ext = extended[-1]
@@ -78,19 +84,327 @@
         edge = step + 1
         wind_mid = wind_ext[:, edge : wind_ext.shape[1] - edge]
         state = tendency(state[..., 1:-1], state[..., 2:], state[..., :-2], wind_mid)
-    model_variable = state
-    mem_here, latitude_lines, column_entries = model_variable.shape
+    mem_here, latitude_lines, column_entries = state.shape
     groups = lax.axis_size("member")
     per_dev = obs_count.shape[0]
     cell_count = latitude_lines * column_entries // (groups * per_dev)
-    blocks = model_variable.reshape(mem_here, groups, per_dev, cell_count)
+    blocks = state.reshape(mem_here, groups, per_dev, cell_count)
     arrived = lax.all_to_all(blocks, "member", split_axis=1, concat_axis=0, tiled=True)
     output_results = [
-        analyze(arrived[:, 0, 0], observed_cell_value[0], obs_value[0], obs_weight[0], obs_count[0])
+        analyze(arrived[:, 0, i], observed_cell_value[i], obs_value[i], obs_weight[i], obs_count[i])
+        for i in range(per_dev)
     ]
     analysed_state = jnp.stack(output_results, axis=1)[:, None]
     returned = lax.all_to_all(analysed_state, "member", split_axis=0, concat_axis=1, tiled=True)
     return returned.reshape(mem_here, latitude_lines, column_entries)
+
+
+def strips_kernel(u_ref, q_ref):
+    rows = u_ref.shape[1]
+    lane = lax.broadcasted_iota(jnp.int32, (rows, LANES), 1)
+    west = (lane % STRIP) < STRIP // 2
+    total = [jnp.zeros((rows, LANES), jnp.float32)] * 2
+    for m in range(u_ref.shape[0] - 1):
+        mine = (lane // STRIP) == m
+        for k, x in enumerate((u_ref[m], u_ref[u_ref.shape[0] - 1])):
+            low = pltpu.roll(x, (STRIP * m + SUBSTEPS) % LANES, 1)
+            high = pltpu.roll(x, (STRIP * m + STRIP - SUBSTEPS) % LANES, 1)
+            total[k] = jnp.where(mine, jnp.where(west, low, high), total[k])
+    q_ref[0:rows, :] = total[0]
+    q_ref[rows : 2 * rows, :] = total[1]
+
+
+def substep(x, wind3):
+    rows = x.shape[0]
+    row = lax.broadcasted_iota(jnp.int32, x.shape, 0)
+    east = pltpu.roll(x, LANES - 1, 1)
+    west = pltpu.roll(x, 1, 1)
+    north = jnp.where(row == rows - 1, 0.0, pltpu.roll(x, rows - 1, 0))
+    south = jnp.where(row == 0, 0.0, pltpu.roll(x, 1, 0))
+    speed = wind3 + 0.075 * jnp.tanh(x)
+    return 0.4 * x + 0.2 * (east + west) + 0.1 * (north + south) - speed * (east - west)
+
+
+def pieces(x, count):
+    out = []
+    for _ in range(count):
+        part = x.astype(jnp.bfloat16)
+        out.append(part)
+        x = x - part.astype(jnp.float32)
+    return out
+
+
+def interior_kernel(count_ref, u_ref, cell_ref, value_ref, weight_ref, f_ref):
+    mem_here, rows = u_ref.shape[0] - 1, u_ref.shape[1]
+    stride = f_ref.shape[0] // mem_here
+    extra = stride - rows
+    wind3 = 0.3 * u_ref[mem_here]
+    slots = cell_ref.shape[1]
+    slot = lax.broadcasted_iota(jnp.int32, (1, slots), 1)
+    weight = jnp.where(slot < count_ref[0], weight_ref[...], 0.0)
+    parts = pieces(weight, 3) + pieces(weight * value_ref[...], 3)
+    sub = lax.broadcasted_iota(jnp.int32, (8, slots), 0)
+    lhs = jnp.zeros((8, slots), jnp.float32)
+    for k, part in enumerate(parts):
+        lhs = jnp.where(sub == k, part.astype(jnp.float32), lhs)
+    lhs = lhs.astype(jnp.bfloat16)
+    patch_rows = extra * mem_here // 2
+    for q in range(patch_rows):
+        cell = lax.broadcasted_iota(jnp.int32, (LANES, slots), 0) + LANES * q
+        hot = jnp.where(cell == cell_ref[...], 1.0, 0.0).astype(jnp.bfloat16)
+        sums = lax.dot_general(
+            lhs, hot, (((1,), (1,)), ((), ())), preferred_element_type=jnp.float32
+        )
+        for which in range(2):
+            k = which * patch_rows + q
+            line = sums[3 * which : 3 * which + 1] + sums[3 * which + 1 : 3 * which + 2]
+            line = line + sums[3 * which + 2 : 3 * which + 3]
+            at = (k // extra) * stride + rows + k % extra
+            f_ref[at : at + 1, :] = line
+    for m in range(mem_here):
+        x = u_ref[m]
+        for _ in range(SUBSTEPS):
+            x = substep(x, wind3)
+        f_ref[m * stride : m * stride + rows, :] = x
+
+
+def edges_kernel(q_ref, east_ref, west_ref, f_in_ref, f_ref):
+    rows = q_ref.shape[0] // 2
+    lane = lax.broadcasted_iota(jnp.int32, (rows, LANES), 1)
+    place = lane % STRIP
+    full = []
+    for k in range(2):
+        at = slice(k * rows, (k + 1) * rows)
+        west, east, own = west_ref[at, :], east_ref[at, :], q_ref[at, :]
+        full.append(
+            jnp.where(place < SUBSTEPS, west, jnp.where(place >= STRIP - SUBSTEPS, east, own))
+        )
+    x, wind3 = full[0], 0.3 * full[1]
+    for _ in range(SUBSTEPS):
+        x = substep(x, wind3)
+    mem_here = LANES // STRIP
+    stride = f_ref.shape[0] // mem_here
+    for m in range(mem_here):
+        low = pltpu.roll(x, (-STRIP * m - SUBSTEPS) % LANES, 1)
+        high = pltpu.roll(x, (-STRIP * m - STRIP + SUBSTEPS) % LANES, 1)
+        at = slice(m * stride, m * stride + rows)
+        inside = f_in_ref[at, :]
+        f_ref[at, :] = jnp.where(
+            lane < SUBSTEPS, low, jnp.where(lane >= LANES - SUBSTEPS, high, inside)
+        )
+        at = slice(m * stride + rows, (m + 1) * stride)
+        f_ref[at, :] = f_in_ref[at, :]
+
+
+def analysis_kernel(dims, me_ref, cat_ref, sib_ref, o_ref, ob_ref, pert_ref, scaled_ref, mean_ref):
+    mem_here, rows, groups = dims
+    f32, bf16 = jnp.float32, jnp.bfloat16
+    order = mem_here * groups
+    height = rows // groups
+    cells = height * LANES
+    wide = order * groups
+    stride = cat_ref.shape[0] * 2 // order
+    extra = stride - rows
+    me = me_ref[0]
+
+    for side, ref in enumerate((cat_ref, sib_ref)):
+        for k in range(groups // 2):
+            patch = me ^ (2 * k + side)
+            base = k * mem_here * stride
+            lines = [
+                ref[base + m * stride + rows : base + (m + 1) * stride, :] for m in range(mem_here)
+            ]
+            ob_ref[pl.ds(pl.multiple_of(patch * 2 * height, 2 * height), 2 * height), :] = (
+                jnp.concatenate(lines, axis=0)
+            )
+
+    for p in range(groups):
+        sums = ob_ref[p * 2 * height : (p + 1) * 2 * height, :]
+        for q in range(height):
+            at = pl.ds(p * height + q, order // 2, stride=stride)
+            xb = jnp.concatenate([cat_ref[at, :], sib_ref[at, :]], axis=0)
+            mean = jnp.sum(xb, axis=0, keepdims=True) * (1.0 / order)
+            pert = xb - mean
+            lanes = slice(q * LANES, (q + 1) * LANES)
+            weight = sums[q : q + 1, :]
+            pert_ref[p * order : (p + 1) * order, lanes] = pert
+            scaled_ref[p * order : (p + 1) * order, lanes] = pert * weight
+            scaled_ref[wide + p : wide + p + 1, lanes] = (
+                sums[height + q : height + q + 1, :] - weight * mean
+            )
+            mean_ref[p : p + 1, lanes] = mean
+    pad = scaled_ref.shape[0] - wide - groups
+    if pad:
+        scaled_ref[wide + groups :, :] = jnp.zeros((pad, cells), f32)
+
+    def split(x):
+        high = x.astype(bf16)
+        return high, (x - high.astype(f32)).astype(bf16)
+
+    def product(x, high, low, dims):
+        n = x.shape[0]
+        xh, xl = split(x)
+        dot = functools.partial(
+            lax.dot_general, dimension_numbers=(dims, ((), ())), preferred_element_type=f32
+        )
+        both = dot(jnp.concatenate([xh, xl], axis=0), high)
+        return both[:n] + both[n:] + dot(xh, low)
+
+    plain, turned = ((1,), (0,)), ((1,), (1,))
+
+    pert_high, pert_low = split(pert_ref[...])
+    full = product(scaled_ref[...], pert_high, pert_low, turned)
+    own_row = lax.broadcasted_iota(jnp.int32, (order, wide), 0)
+    lane = lax.broadcasted_iota(jnp.int32, (order, wide), 1)
+    gram = jnp.where(own_row == lane % order, order - 1.0, 0.0)
+    ident = jnp.where(own_row == lane % order, 1.0, 0.0)
+    block = lane // order
+    total = jnp.zeros((order, wide), f32)
+    for p in range(groups):
+        total = jnp.where(block == p, full[p * order : (p + 1) * order], total)
+    gram = gram + total
+    tail = full[wide : wide + 16]
+    tail_row = lax.broadcasted_iota(jnp.int32, (16, wide), 0)
+    tail_block = lax.broadcasted_iota(jnp.int32, (16, wide), 1) // order
+    rhs = jnp.sum(jnp.where(tail_row == tail_block, tail, 0.0), axis=0, keepdims=True)
+    first = tail_row == 0
+
+    diag = (
+        lax.broadcasted_iota(jnp.int32, (wide, wide), 0) // order
+        == lax.broadcasted_iota(jnp.int32, (wide, wide), 1) // order
+    )
+
+    def blocks(x):
+        return [
+            jnp.where(diag, jnp.concatenate([part.astype(f32)] * groups, axis=0), 0.0).astype(bf16)
+            for part in split(x)
+        ]
+
+    ones = jnp.where(diag, 1.0, 0.0).astype(bf16)
+    square = jnp.sum(gram * gram, axis=0, keepdims=True)
+    parts = pieces(jnp.where(first, square, 0.0), 3)
+    square = sum(
+        lax.dot_general(part, ones, (plain, ((), ())), preferred_element_type=f32)[0:1]
+        for part in parts
+    )
+    scale = jnp.sqrt(square + 1e-06)
+    inverse = 1.0 / scale
+
+    prod = gram * inverse
+    middle = 1.5 * ident - 0.5 * prod
+    lower = middle
+    vec = jnp.where(first, rhs, 0.0)
+    for step in range(NS_ITERS):
+        high, low = blocks(middle)
+        last = step == NS_ITERS - 1
+        if step == 0:
+            out = product(jnp.concatenate([prod, vec], axis=0), high, low, plain)
+            half, vec = out[:order], out[order:]
+        elif not last:
+            out = product(jnp.concatenate([prod, lower, vec], axis=0), high, low, plain)
+            half, lower, vec = out[:order], out[order : 2 * order], out[2 * order :]
+        else:
+            out = product(jnp.concatenate([lower, vec], axis=0), high, low, plain)
+            lower, vec = out[:order], out[order:]
+        if not last:
+            prod = product(half, high, low, plain)
+            middle = 1.5 * ident - 0.5 * prod
+    high, low = blocks(lower)
+    wbar = product(vec, high, low, plain)[0:1] * inverse
+    eight = lower[0:8] * (jnp.sqrt(inverse) * (order - 1.0) ** 0.5) + wbar
+
+    tall = jnp.concatenate([eight] * groups, axis=0)
+    tall_row = lax.broadcasted_iota(jnp.int32, tall.shape, 0) // 8
+    tall_block = lax.broadcasted_iota(jnp.int32, tall.shape, 1) // order
+    out = product(jnp.where(tall_row == tall_block, tall, 0.0), pert_high, pert_low, plain)
+    for p in range(groups):
+        for q in range(height):
+            lanes = slice(q * LANES, (q + 1) * LANES)
+            o_ref[pl.ds(p * height + q, mem_here, stride=rows), :] = (
+                out[8 * p : 8 * p + mem_here, lanes] + mean_ref[p : p + 1, lanes]
+            )
+
+
+def kernel_call(body, out_shape, scratch=(), smem=()):
+    def call(*args):
+        specs = [
+            pl.BlockSpec(memory_space=pltpu.SMEM if i in smem else pltpu.VMEM)
+            for i in range(len(args))
+        ]
+        return pl.pallas_call(
+            body,
+            out_shape=jax.ShapeDtypeStruct(out_shape, jnp.float32),
+            in_specs=specs,
+            out_specs=pl.BlockSpec(memory_space=pltpu.VMEM),
+            scratch_shapes=list(scratch),
+            compiler_params=pltpu.CompilerParams(vmem_limit_bytes=32 << 20),
+        )(*args)
+
+    return call
+
+
+def gathered(prior_ensemble, wind, obs_value, obs_weight, observed_cell_value, obs_count):
+    mem_here, rows, _ = prior_ensemble.shape
+    groups = lax.axis_size("member")
+    count = lax.axis_size("space")
+    order = mem_here * groups
+    height = rows // groups
+    extra = 2 * height // mem_here
+    stride = rows + extra
+    f32, bf16 = jnp.float32, jnp.bfloat16
+
+    both = jnp.concatenate([prior_ensemble, wind[None]], axis=0)
+    strips = kernel_call(strips_kernel, (2 * rows, LANES))(both)
+    forward = [(i, (i + 1) % count) for i in range(count)]
+    backward = [(i, (i - 1) % count) for i in range(count)]
+    east = lax.ppermute(strips, "space", backward)
+    west = lax.ppermute(strips, "space", forward)
+    inside = kernel_call(interior_kernel, (mem_here * stride, LANES), smem=(0,))(
+        obs_count, both, observed_cell_value, obs_value, obs_weight
+    )
+    payload = kernel_call(edges_kernel, (mem_here * stride, LANES))(strips, east, west, inside)
+
+    def swap(x, k):
+        return lax.ppermute(x, "member", [(i, i ^ k) for i in range(groups)])
+
+    chips = range(2, groups, 2)
+    others = [swap(payload, k) for k in reversed(chips)][::-1]
+    cat = jnp.concatenate([payload, *others], axis=0)
+    sibling = swap(cat, 1)
+    me = lax.axis_index("member").astype(jnp.int32).reshape(1)
+    wide = order * groups
+    cells = height * LANES
+    out = kernel_call(
+        functools.partial(analysis_kernel, (mem_here, rows, groups)),
+        (mem_here * rows, LANES),
+        scratch=[
+            pltpu.VMEM((groups * 2 * height, LANES), f32),
+            pltpu.VMEM((wide, cells), f32),
+            pltpu.VMEM((wide + 16, cells), f32),
+            pltpu.VMEM((max(groups, 8), cells), f32),
+        ],
+        smem=(0,),
+    )(me, cat, sibling)
+    return out.reshape(mem_here, rows, LANES)
+
+
+def local(prior_ensemble, *rest):
+    mem_here, rows, columns = prior_ensemble.shape
+    groups = lax.axis_size("member")
+    whole_tile = 4 * mem_here * groups * rows * columns
+    fits = (
+        columns == LANES
+        and mem_here * STRIP == LANES
+        and rows % groups == 0
+        and 2 * (rows // groups) % mem_here == 0
+        and rows % 8 == 0
+        and groups & (groups - 1) == 0
+        and 2 <= groups <= 16
+        and lax.axis_size("space") % 2 == 0
+        and rest[-1].shape[0] == 1
+        and whole_tile <= GATHER_BYTES
+    )
+    return (gathered if fits else exchanged)(prior_ensemble, *rest)
 
 
 def solution(mesh):

time: 40.4 us -> 21.8 us (0.54)
  local copies, waits for them, and re-layouts: 7.43 us -> 0.01 us
  blocking collectives: 7.4 us -> 0 us
  matrix products: 4.91 us -> 0 us
  Pallas kernels: 0 us -> 4.73 us
  waiting for transfers between devices: 7.89 us -> 6.45 us
  other arithmetic: 1.83 us -> 0.88 us
  between operations: 1.67 us -> 0.74 us
    all_to_all x1 -> x0, blocking collectives: 7.4 us -> none  [local(): lax.all_to_all(analysed_state, 'member', split_axis=0, concat_axis=1, til...]
    all_to_all x1 -> x0, waiting for transfers between devices: 5.01 us -> none  [local(): lax.all_to_all(blocks, 'member', split_axis=1, concat_axis=0, tiled=True)]
    dot_general x22 -> x0, matrix products: 4.91 us -> none  [the longest x1 1.45 us: analyze(): jnp.dot(ypert * wts, ypert.T, precision=lax.Precision.HIGHEST)]
    pallas_call x0 -> x4, Pallas kernels: none -> 4.73 us  [call(): pl.pallas_call(body, out_shape=jax.ShapeDtypeStruct(out_shape, jnp.float3...]
    gather x2 -> x0, local copies, waits for them, and re-layouts: 4.53 us -> none  [the longest x1 3.49 us: analyze(): ymean = jnp.take(mean, cells)]
    all_to_all x1 -> x0, starting transfers between devices: 3.72 us -> none  [local(): lax.all_to_all(blocks, 'member', split_axis=1, concat_axis=0, tiled=True)]
    ppermute x2 -> x6, starting transfers between devices: 5.17 us -> 8.79 us  [the longest x4 3.62 us: swap(): return lax.ppermute(x, 'member', [(i, i ^ k) for i in range(groups)])]
    ppermute x2 -> x6, waiting for transfers between devices: 2.88 us -> 6.45 us  [the longest x4 5.31 us: swap(): return lax.ppermute(x, 'member', [(i, i ^ k) for i in range(groups)])]
  transfers between devices with their start and end apart: 3 -> 6, of which waited for: 3 -> 6; matrix products, arithmetic and copies ran while one was open for 0% -> 0% of each run, Pallas kernels for 0% -> 2%
where the time goes in v1:
time: 21.8 us; the launch traced here: 21.6 us
  starting transfers between devices  8.79 us (40%)
  waiting for transfers between devices  6.45 us (30%)
  Pallas kernels  4.73 us (22%)
  other arithmetic  0.88 us (4%)
  between operations  0.74 us (3%)
    ppermute x4, waiting for transfers between devices, swap(): return lax.ppermute(x, 'member', [(i, i ^ k) for i in range(groups)])  5.31 us
    pallas_call x4, Pallas kernels, call(): pl.pallas_call(body, out_shape=jax.ShapeDtypeStruct(out_shape, jnp.float3...  4.73 us
    ppermute x4, starting transfers between devices, swap(): return lax.ppermute(x, 'member', [(i, i ^ k) for i in range(groups)])  3.62 us
    ppermute x1, starting transfers between devices, gathered(): west = lax.ppermute(strips, 'space', forward)  3.08 us
    ppermute x1, starting transfers between devices, gathered(): east = lax.ppermute(strips, 'space', backward)  2.09 us
    ppermute x1, waiting for transfers between devices, gathered(): west = lax.ppermute(strips, 'space', forward)  0.9 us
    concatenate x1, other arithmetic, gathered(): both = jnp.concatenate([prior_ensemble, wind[None]], axis=0)  0.86 us
  transfers between devices with their start and end apart: 6, of which 6 were waited for; matrix products, arithmetic and copies ran while one was open for 0% of the time, Pallas kernels for 2%

profile of v1, /device:TPU:0, one launch (start us, length us, event | category | flops | bytes accessed | tf_op | source)
XLA Modules:
  0.0 21.6 jit_solution(13871096931024418029)
XLA Ops:
  0.0 0.9 %pad_maximum_fusion.1.u_ref = f32[5,32,128]{2,1,0:T(8,128)S(1)} fusion(f32[1,32,128]{2,1,0:T(8,128)} %bitcast.3, f32[4,32,128]{2,1,0:T(8,128)} %param.6), kind=kLoop, calls=%fused_computation.1 | loop fusion | flops 20480 | bytes 163840 | tf_op jit(solution)/shard_map/concatenate | solution.py:356
  0.9 0.0 copy-start
  0.9 0.0 copy-start.1
  0.9 0.0 copy-start.2
  0.9 0.1 shard_map.64.q_ref
  1.0 3.1 %collective-permute-start.1 = (f32[64,128]{1,0:T(8,128)S(1)}, f32[64,128]{1,0:T(8,128)S(1)}, u32[]{:S(2)}, u32[]{:S(2)}) collective-permute-start(f32[64,128]{1,0:T(8,128)S(1)} %shard_map.64.q_ref), channel_id=1, source_target_pairs={{0,8},{8,16},{16,24},{24,0},{1,9},{9,17},{17,25},{25,1},{2,10},{10... | collective-permute-start | bytes 98312 | tf_op jit(solution)/shard_map/ppermute | solution.py:361
  4.1 2.1 %collective-permute-start = (f32[64,128]{1,0:T(8,128)S(1)}, f32[64,128]{1,0:T(8,128)S(1)}, u32[]{:S(2)}, u32[]{:S(2)}) collective-permute-start(f32[64,128]{1,0:T(8,128)S(1)} %shard_map.64.q_ref), channel_id=1, source_target_pairs={{0,24},{8,0},{16,8},{24,16},{1,25},{9,1},{17,9},{25,17},{2,26},{10... | collective-permute-start | bytes 98312 | tf_op jit(solution)/shard_map/ppermute | solution.py:360
  6.8 0.0 copy-done
  6.8 0.0 copy-done.1
  6.9 0.0 copy-done.2
  6.9 0.3 %shard_map.65.f_in_ref = f32[136,128]{1,0:T(8,128)S(1)} custom-call(s32[1]{0:T(128)S(6)} %copy.7.count_ref, f32[5,32,128]{2,1,0:T(8,128)S(1)} %pad_maximum_fusion.1.u_ref, s32[1,512]{1,0:T(1,128)S(1)} %copy-done, f32[1,512]{1,0:T(1,128)S(1)} %copy-done.1, f32[1,512]{1,0:T(1,128)S(1)} %copy-done.2), custom_call_target="tpu_custom_call" | custom-call | tf_op jit(solution)/shard_map/pallas_call | solution.py:334
  7.2 0.9 %collective-permute-done.1.west_ref = f32[64,128]{1,0:T(8,128)S(1)} collective-permute-done((f32[64,128]{1,0:T(8,128)S(1)}, f32[64,128]{1,0:T(8,128)S(1)}, u32[]{:S(2)}, u32[]{:S(2)}) %collective-permute-start.1) | collective-permute-done | bytes 32800 | tf_op jit(solution)/shard_map/ppermute | solution.py:361
  8.1 0.2 %collective-permute-done.east_ref = f32[64,128]{1,0:T(8,128)S(1)} collective-permute-done((f32[64,128]{1,0:T(8,128)S(1)}, f32[64,128]{1,0:T(8,128)S(1)}, u32[]{:S(2)}, u32[]{:S(2)}) %collective-permute-start) | collective-permute-done | bytes 32800 | tf_op jit(solution)/shard_map/ppermute | solution.py:360
  8.4 0.4 %shard_map.66 = f32[136,128]{1,0:T(8,128)S(1)} custom-call(f32[64,128]{1,0:T(8,128)S(1)} %shard_map.64.q_ref, f32[64,128]{1,0:T(8,128)S(1)} %collective-permute-done.east_ref, f32[64,128]{1,0:T(8,128)S(1)} %collective-permute-done.1.west_ref, f32[136,128]{1,0:T(8,128)S(1)} %shard_map.65.f_in_ref), custom_call_target="tpu_custom_call" | custom-call | tf_op jit(solution)/shard_map/pallas_call | solution.py:334
  8.8 2.5 %collective-permute-start.4 = (f32[136,128]{1,0:T(8,128)S(1)}, f32[136,128]{1,0:T(8,128)S(1)}, u32[]{:S(2)}, u32[]{:S(2)}) collective-permute-start(f32[136,128]{1,0:T(8,128)S(1)} %shard_map.66), channel_id=1, source_target_pairs={{0,6},{1,7},{2,4},{3,5},{4,2},{5,3},{6,0},{7,1},{8,14},{9,15},{10,... | collective-permute-start | bytes 208904 | tf_op jit(solution)/shard_map/ppermute | solution.py:368
  11.3 0.5 %collective-permute-start.3 = (f32[136,128]{1,0:T(8,128)S(1)}, f32[136,128]{1,0:T(8,128)S(1)}, u32[]{:S(2)}, u32[]{:S(2)}) collective-permute-start(f32[136,128]{1,0:T(8,128)S(1)} %shard_map.66), channel_id=1, source_target_pairs={{0,4},{1,5},{2,6},{3,7},{4,0},{5,1},{6,2},{7,3},{8,12},{9,13},{10,... | collective-permute-start | bytes 208904 | tf_op jit(solution)/shard_map/ppermute | solution.py:368
  11.8 0.5 %collective-permute-start.2 = (f32[136,128]{1,0:T(8,128)S(1)}, f32[136,128]{1,0:T(8,128)S(1)}, u32[]{:S(2)}, u32[]{:S(2)}) collective-permute-start(f32[136,128]{1,0:T(8,128)S(1)} %shard_map.66), channel_id=1, source_target_pairs={{0,2},{1,3},{2,0},{3,1},{4,6},{5,7},{6,4},{7,5},{8,10},{9,11},{10,... | collective-permute-start | bytes 208904 | tf_op jit(solution)/shard_map/ppermute | solution.py:368
  12.3 2.4 %collective-permute-done.4 = f32[136,128]{1,0:T(8,128)S(1)} collective-permute-done((f32[136,128]{1,0:T(8,128)S(1)}, f32[136,128]{1,0:T(8,128)S(1)}, u32[]{:S(2)}, u32[]{:S(2)}) %collective-permute-start.4) | collective-permute-done | bytes 69664 | tf_op jit(solution)/shard_map/ppermute | solution.py:368
  14.7 0.9 %collective-permute-done.3 = f32[136,128]{1,0:T(8,128)S(1)} collective-permute-done((f32[136,128]{1,0:T(8,128)S(1)}, f32[136,128]{1,0:T(8,128)S(1)}, u32[]{:S(2)}, u32[]{:S(2)}) %collective-permute-start.3) | collective-permute-done | bytes 69664 | tf_op jit(solution)/shard_map/ppermute | solution.py:368
  15.6 0.5 %collective-permute-done.2 = f32[136,128]{1,0:T(8,128)S(1)} collective-permute-done((f32[136,128]{1,0:T(8,128)S(1)}, f32[136,128]{1,0:T(8,128)S(1)}, u32[]{:S(2)}, u32[]{:S(2)}) %collective-permute-start.2) | collective-permute-done | bytes 69664 | tf_op jit(solution)/shard_map/ppermute | solution.py:368
  16.1 0.1 collective-permute-start.5
  16.2 1.5 %collective-permute-done.5.sib_ref = f32[544,128]{1,0:T(8,128)S(1)} collective-permute-done((f32[544,128]{1,0:T(8,128)S(1)}, f32[544,128]{1,0:T(8,128)S(1)}, u32[]{:S(2)}, u32[]{:S(2)}) %collective-permute-start.5) | collective-permute-done | bytes 278560 | tf_op jit(solution)/shard_map/ppermute | solution.py:368
  17.8 3.9 %shard_map.67 = f32[128,128]{1,0:T(8,128)} custom-call(s32[1]{0:T(128)} %bitcast.me_ref, f32[544,128]{1,0:T(8,128)S(1)} %pad_maximum_fusion.cat_ref, f32[544,128]{1,0:T(8,128)S(1)} %collective-permute-done.5.sib_ref), custom_call_target="tpu_custom_call" | custom-call | tf_op jit(solution)/shard_map/pallas_call | solution.py:334
  (1 shorter events, 0.0 us)
Async XLA Ops:
  0.9 6.0 %copy-start = (s32[1,512]{1,0:T(1,128)S(1)}, s32[1,512]{1,0:T(1,128)}, u32[]{:S(2)}) copy-start(s32[1,512]{1,0:T(1,128)} %cell_ref.1) | copy-start | bytes 6148
  0.9 6.0 %copy-start.1 = (f32[1,512]{1,0:T(1,128)S(1)}, f32[1,512]{1,0:T(1,128)}, u32[]{:S(2)}) copy-start(f32[1,512]{1,0:T(1,128)} %value_ref.1) | copy-start | bytes 6148
  0.9 6.0 %copy-start.2 = (f32[1,512]{1,0:T(1,128)S(1)}, f32[1,512]{1,0:T(1,128)}, u32[]{:S(2)}) copy-start(f32[1,512]{1,0:T(1,128)} %weight_ref.1) | copy-start | bytes 6148
  1.0 7.1 %collective-permute-start.1 = (f32[64,128]{1,0:T(8,128)S(1)}, f32[64,128]{1,0:T(8,128)S(1)}, u32[]{:S(2)}, u32[]{:S(2)}) collective-permute-start(f32[64,128]{1,0:T(8,128)S(1)} %shard_map.64.q_ref), channel_id=1, source_target_pairs={{0,8},{8,16},{16,24},{24,0},{1,9},{9,17},{17,25},{25,1},{2,10},{10... | collective-permute-start | bytes 98312 | tf_op jit(solution)/shard_map/ppermute | solution.py:361
  4.1 4.3 %collective-permute-start = (f32[64,128]{1,0:T(8,128)S(1)}, f32[64,128]{1,0:T(8,128)S(1)}, u32[]{:S(2)}, u32[]{:S(2)}) collective-permute-start(f32[64,128]{1,0:T(8,128)S(1)} %shard_map.64.q_ref), channel_id=1, source_target_pairs={{0,24},{8,0},{16,8},{24,16},{1,25},{9,1},{17,9},{25,17},{2,26},{10... | collective-permute-start | bytes 98312 | tf_op jit(solution)/shard_map/ppermute | solution.py:360
  8.8 5.9 %collective-permute-start.4 = (f32[136,128]{1,0:T(8,128)S(1)}, f32[136,128]{1,0:T(8,128)S(1)}, u32[]{:S(2)}, u32[]{:S(2)}) collective-permute-start(f32[136,128]{1,0:T(8,128)S(1)} %shard_map.66), channel_id=1, source_target_pairs={{0,6},{1,7},{2,4},{3,5},{4,2},{5,3},{6,0},{7,1},{8,14},{9,15},{10,... | collective-permute-start | bytes 208904 | tf_op jit(solution)/shard_map/ppermute | solution.py:368
  11.3 4.3 %collective-permute-start.3 = (f32[136,128]{1,0:T(8,128)S(1)}, f32[136,128]{1,0:T(8,128)S(1)}, u32[]{:S(2)}, u32[]{:S(2)}) collective-permute-start(f32[136,128]{1,0:T(8,128)S(1)} %shard_map.66), channel_id=1, source_target_pairs={{0,4},{1,5},{2,6},{3,7},{4,0},{5,1},{6,2},{7,3},{8,12},{9,13},{10,... | collective-permute-start | bytes 208904 | tf_op jit(solution)/shard_map/ppermute | solution.py:368
  11.8 4.3 %collective-permute-start.2 = (f32[136,128]{1,0:T(8,128)S(1)}, f32[136,128]{1,0:T(8,128)S(1)}, u32[]{:S(2)}, u32[]{:S(2)}) collective-permute-start(f32[136,128]{1,0:T(8,128)S(1)} %shard_map.66), channel_id=1, source_target_pairs={{0,2},{1,3},{2,0},{3,1},{4,6},{5,7},{6,4},{7,5},{8,10},{9,11},{10,... | collective-permute-start | bytes 208904 | tf_op jit(solution)/shard_map/ppermute | solution.py:368
  16.1 1.6 %collective-permute-start.5 = (f32[544,128]{1,0:T(8,128)S(1)}, f32[544,128]{1,0:T(8,128)S(1)}, u32[]{:S(2)}, u32[]{:S(2)}) collective-permute-start(f32[544,128]{1,0:T(8,128)S(1)} %pad_maximum_fusion.cat_ref), channel_id=1, source_target_pairs={{0,1},{1,0},{2,3},{3,2},{4,5},{5,4},{6,7},{7,6},{8,9},{9,8},{10,11... | collective-permute-start | bytes 835592 | tf_op jit(solution)/shard_map/ppermute | solution.py:368

commit v2 on v1

--- a/solution.py
+++ b/solution.py
@@ -99,19 +99,34 @@
     return returned.reshape(mem_here, latitude_lines, column_entries)
 
 
-def strips_kernel(u_ref, q_ref):
-    rows = u_ref.shape[1]
-    lane = lax.broadcasted_iota(jnp.int32, (rows, LANES), 1)
+def lane_of(shape):
+    return lax.broadcasted_iota(jnp.int32, shape, 1)
+
+
+def edge_kernel(start, wind_start, u_ref, z_ref):
+    members, rows, _ = u_ref.shape
+    members = members - 1
+    lane = lane_of((rows, LANES))
+    place = lane % STRIP
+    column = 0 if start > STRIP // 2 else LANES - SUBSTEPS
+    total = jnp.zeros((rows, LANES), jnp.float32)
+    for m in range(members):
+        for x, to in ((u_ref[m], start), (u_ref[members], wind_start)):
+            moved = pltpu.roll(x, (STRIP * m + to - column) % LANES, 1)
+            keep = (lane // STRIP == m) & (place >= to) & (place < to + SUBSTEPS)
+            total = jnp.where(keep, moved, total)
+    z_ref[...] = total
+
+
+def strips(block):
+    lane = lane_of(block[0].shape)
     west = (lane % STRIP) < STRIP // 2
-    total = [jnp.zeros((rows, LANES), jnp.float32)] * 2
-    for m in range(u_ref.shape[0] - 1):
-        mine = (lane // STRIP) == m
-        for k, x in enumerate((u_ref[m], u_ref[u_ref.shape[0] - 1])):
-            low = pltpu.roll(x, (STRIP * m + SUBSTEPS) % LANES, 1)
-            high = pltpu.roll(x, (STRIP * m + STRIP - SUBSTEPS) % LANES, 1)
-            total[k] = jnp.where(mine, jnp.where(west, low, high), total[k])
-    q_ref[0:rows, :] = total[0]
-    q_ref[rows : 2 * rows, :] = total[1]
+    total = jnp.zeros(block[0].shape, jnp.float32)
+    for m, x in enumerate(block):
+        low = pltpu.roll(x, (STRIP * m + SUBSTEPS) % LANES, 1)
+        high = pltpu.roll(x, (STRIP * m + STRIP - SUBSTEPS) % LANES, 1)
+        total = jnp.where((lane // STRIP) == m, jnp.where(west, low, high), total)
+    return total
 
 
 def substep(x, wind3):
@@ -134,14 +149,14 @@
     return out
 
 
-def interior_kernel(count_ref, u_ref, cell_ref, value_ref, weight_ref, f_ref):
+def interior_kernel(count_ref, u_ref, cell_ref, value_ref, weight_ref, f_ref, q_ref):
     mem_here, rows = u_ref.shape[0] - 1, u_ref.shape[1]
     stride = f_ref.shape[0] // mem_here
     extra = stride - rows
     wind3 = 0.3 * u_ref[mem_here]
     slots = cell_ref.shape[1]
     slot = lax.broadcasted_iota(jnp.int32, (1, slots), 1)
-    weight = jnp.where(slot < count_ref[0], weight_ref[...], 0.0)
+    weight = jnp.where(slot < count_ref[...], weight_ref[...], 0.0)
     parts = pieces(weight, 3) + pieces(weight * value_ref[...], 3)
     sub = lax.broadcasted_iota(jnp.int32, (8, slots), 0)
     lhs = jnp.zeros((8, slots), jnp.float32)
@@ -161,6 +176,8 @@
             line = line + sums[3 * which + 2 : 3 * which + 3]
             at = (k // extra) * stride + rows + k % extra
             f_ref[at : at + 1, :] = line
+    q_ref[0:rows, :] = strips([u_ref[m] for m in range(mem_here)])
+    q_ref[rows : 2 * rows, :] = strips([u_ref[mem_here]] * mem_here)
     for m in range(mem_here):
         x = u_ref[m]
         for _ in range(SUBSTEPS):
@@ -168,17 +185,19 @@
         f_ref[m * stride : m * stride + rows, :] = x
 
 
-def edges_kernel(q_ref, east_ref, west_ref, f_in_ref, f_ref):
+def edges_kernel(q_ref, west_ref, east_ref, f_in_ref, f_ref):
     rows = q_ref.shape[0] // 2
-    lane = lax.broadcasted_iota(jnp.int32, (rows, LANES), 1)
+    lane = lane_of((rows, LANES))
     place = lane % STRIP
+    west, east = west_ref[...], east_ref[...]
     full = []
     for k in range(2):
-        at = slice(k * rows, (k + 1) * rows)
-        west, east, own = west_ref[at, :], east_ref[at, :], q_ref[at, :]
+        own = q_ref[k * rows : (k + 1) * rows, :]
         full.append(
             jnp.where(place < SUBSTEPS, west, jnp.where(place >= STRIP - SUBSTEPS, east, own))
         )
+        west = pltpu.roll(west, LANES - SUBSTEPS, 1)
+        east = pltpu.roll(east, SUBSTEPS, 1)
     x, wind3 = full[0], 0.3 * full[1]
     for _ in range(SUBSTEPS):
         x = substep(x, wind3)
@@ -204,8 +223,17 @@
     cells = height * LANES
     wide = order * groups
     stride = cat_ref.shape[0] * 2 // order
-    extra = stride - rows
+    per = LANES // order
+    sets = range(groups // per)
+    plain, turned = (((1,), (0,)), ((), ())), (((1,), (1,)), ((), ()))
     me = me_ref[0]
+
+    def dot(x, y, how):
+        return lax.dot_general(x, y, how, preferred_element_type=f32)
+
+    def split(x):
+        high = x.astype(bf16)
+        return high, (x - high.astype(f32)).astype(bf16)
 
     for side, ref in enumerate((cat_ref, sib_ref)):
         for k in range(groups // 2):
@@ -219,126 +247,135 @@
             )
 
     for p in range(groups):
-        sums = ob_ref[p * 2 * height : (p + 1) * 2 * height, :]
         for q in range(height):
             at = pl.ds(p * height + q, order // 2, stride=stride)
             xb = jnp.concatenate([cat_ref[at, :], sib_ref[at, :]], axis=0)
             mean = jnp.sum(xb, axis=0, keepdims=True) * (1.0 / order)
             pert = xb - mean
             lanes = slice(q * LANES, (q + 1) * LANES)
-            weight = sums[q : q + 1, :]
+            line = p * 2 * height + q
             pert_ref[p * order : (p + 1) * order, lanes] = pert
-            scaled_ref[p * order : (p + 1) * order, lanes] = pert * weight
-            scaled_ref[wide + p : wide + p + 1, lanes] = (
-                sums[height + q : height + q + 1, :] - weight * mean
+            scaled_ref[p * order : (p + 1) * order, lanes] = pert * ob_ref[line : line + 1, :]
+            mean_ref[p : p + 1, lanes] = mean
+    lift = []
+    for q in range(height):
+        weight = ob_ref[pl.ds(q, groups, stride=2 * height), :]
+        lift.append(
+            ob_ref[pl.ds(height + q, groups, stride=2 * height), :]
+            - weight * mean_ref[:, q * LANES : (q + 1) * LANES]
+        )
+    lift = jnp.concatenate(lift, axis=1)
+    lift = jnp.concatenate([lift] * (16 // groups), axis=0)
+    lift_high, lift_low = split(lift)
+
+    pert_high, pert_low = split(pert_ref[...])
+    scaled_high, scaled_low = split(scaled_ref[...])
+    own_row = lax.broadcasted_iota(jnp.int32, (order, LANES), 0)
+    lane = lax.broadcasted_iota(jnp.int32, (order, LANES), 1)
+    ident = jnp.where(own_row == lane % order, 1.0, 0.0)
+    tail_row = lax.broadcasted_iota(jnp.int32, (16, LANES), 0)
+    tail_block = lax.broadcasted_iota(jnp.int32, (16, LANES), 1) // order
+    square_row = lax.broadcasted_iota(jnp.int32, (LANES, LANES), 0) // order
+    square_lane = lax.broadcasted_iota(jnp.int32, (LANES, LANES), 1) // order
+    diag = jnp.where(square_row == square_lane, 1.0, 0.0).astype(bf16)
+    grams, prod, middle, lower, vec, inverse = [], [], [], [], [], []
+    for t in sets:
+        at = slice(t * LANES, (t + 1) * LANES)
+        left_high = jnp.concatenate([scaled_high[at], lift_high], axis=0)
+        left_low = jnp.concatenate([scaled_low[at], lift_low], axis=0)
+        right = jnp.concatenate([pert_high[at], pert_low[at]], axis=0)
+        out = dot(left_high, right, turned)
+        full = out[:, :LANES] + out[:, LANES:] + dot(left_low, pert_high[at], turned)
+        gram = (order - 1.0) * ident
+        for p in range(per):
+            gram = gram + jnp.where(lane // order == p, full[p * order : (p + 1) * order], 0.0)
+        rhs = jnp.sum(
+            jnp.where(tail_row == tail_block + per * t, full[LANES:], 0.0), axis=0, keepdims=True
+        )
+        grams.append(gram)
+        vec.append(jnp.where(tail_row == 0, rhs, 0.0))
+
+    def weights(x):
+        high, low = (jnp.concatenate([part] * per, axis=0) * diag for part in split(x))
+        top = jnp.concatenate([high, low], axis=1)
+        return jnp.concatenate([top, jnp.concatenate([high, jnp.zeros_like(high)], axis=1)], axis=0)
+
+    def product(x, right):
+        out = dot(jnp.concatenate(split(x), axis=1), right, plain)
+        return out[:, :LANES] + out[:, LANES:]
+
+    twice = []
+    for t in sets:
+        twice.append(product(jnp.concatenate([grams[t], vec[t]], axis=0), weights(grams[t])))
+    for t in sets:
+        square = jnp.sum(grams[t] * grams[t], axis=0, keepdims=True)
+        group = lane[0:1] // order
+        total = jnp.zeros((1, LANES), f32)
+        for p in range(per):
+            mine = group == p
+            total = jnp.where(mine, jnp.sum(jnp.where(mine, square, 0.0), axis=1, keepdims=True), total)
+        square = total
+        inverse.append(1.0 / jnp.sqrt(square + 1e-06))
+        first = grams[t] * inverse[t]
+        middle.append(1.5 * ident - 0.5 * first)
+        lower.append(middle[t])
+        prod.append(1.5 * first - (0.5 * inverse[t]) * (twice[t][:order] * inverse[t]))
+        vec[t] = 1.5 * vec[t] - (0.5 * inverse[t]) * twice[t][order:]
+    for step in range(NS_ITERS):
+        last = step == NS_ITERS - 1
+        right = [weights(middle[t]) for t in sets]
+        if step:
+            for t in sets:
+                left = ([] if last else [prod[t]]) + [lower[t], vec[t]]
+                out = product(jnp.concatenate(left, axis=0), right[t])
+                if not last:
+                    prod[t], out = out[:order], out[order:]
+                lower[t], vec[t] = out[:order], out[order:]
+        if not last:
+            for t in sets:
+                prod[t] = product(prod[t], right[t])
+                middle[t] = 1.5 * ident - 0.5 * prod[t]
+    pick = lax.broadcasted_iota(jnp.int32, (groups, LANES), 0)
+    tall = []
+    for t in sets:
+        wbar = product(vec[t], weights(lower[t]))[0:1] * inverse[t]
+        own = lower[t][0:mem_here] * (jnp.sqrt(inverse[t]) * (order - 1.0) ** 0.5) + wbar
+        keep = pick == lax.broadcasted_iota(jnp.int32, (groups, LANES), 1) // order + per * t
+        tall.append(
+            jnp.concatenate(
+                [jnp.where(keep, own[i : i + 1], 0.0) for i in range(mem_here)], axis=0
             )
-            mean_ref[p : p + 1, lanes] = mean
-    pad = scaled_ref.shape[0] - wide - groups
-    if pad:
-        scaled_ref[wide + groups :, :] = jnp.zeros((pad, cells), f32)
-
-    def split(x):
-        high = x.astype(bf16)
-        return high, (x - high.astype(f32)).astype(bf16)
-
-    def product(x, high, low, dims):
-        n = x.shape[0]
-        xh, xl = split(x)
-        dot = functools.partial(
-            lax.dot_general, dimension_numbers=(dims, ((), ())), preferred_element_type=f32
-        )
-        both = dot(jnp.concatenate([xh, xl], axis=0), high)
-        return both[:n] + both[n:] + dot(xh, low)
-
-    plain, turned = ((1,), (0,)), ((1,), (1,))
-
-    pert_high, pert_low = split(pert_ref[...])
-    full = product(scaled_ref[...], pert_high, pert_low, turned)
-    own_row = lax.broadcasted_iota(jnp.int32, (order, wide), 0)
-    lane = lax.broadcasted_iota(jnp.int32, (order, wide), 1)
-    gram = jnp.where(own_row == lane % order, order - 1.0, 0.0)
-    ident = jnp.where(own_row == lane % order, 1.0, 0.0)
-    block = lane // order
-    total = jnp.zeros((order, wide), f32)
-    for p in range(groups):
-        total = jnp.where(block == p, full[p * order : (p + 1) * order], total)
-    gram = gram + total
-    tail = full[wide : wide + 16]
-    tail_row = lax.broadcasted_iota(jnp.int32, (16, wide), 0)
-    tail_block = lax.broadcasted_iota(jnp.int32, (16, wide), 1) // order
-    rhs = jnp.sum(jnp.where(tail_row == tail_block, tail, 0.0), axis=0, keepdims=True)
-    first = tail_row == 0
-
-    diag = (
-        lax.broadcasted_iota(jnp.int32, (wide, wide), 0) // order
-        == lax.broadcasted_iota(jnp.int32, (wide, wide), 1) // order
-    )
-
-    def blocks(x):
-        return [
-            jnp.where(diag, jnp.concatenate([part.astype(f32)] * groups, axis=0), 0.0).astype(bf16)
-            for part in split(x)
-        ]
-
-    ones = jnp.where(diag, 1.0, 0.0).astype(bf16)
-    square = jnp.sum(gram * gram, axis=0, keepdims=True)
-    parts = pieces(jnp.where(first, square, 0.0), 3)
-    square = sum(
-        lax.dot_general(part, ones, (plain, ((), ())), preferred_element_type=f32)[0:1]
-        for part in parts
-    )
-    scale = jnp.sqrt(square + 1e-06)
-    inverse = 1.0 / scale
-
-    prod = gram * inverse
-    middle = 1.5 * ident - 0.5 * prod
-    lower = middle
-    vec = jnp.where(first, rhs, 0.0)
-    for step in range(NS_ITERS):
-        high, low = blocks(middle)
-        last = step == NS_ITERS - 1
-        if step == 0:
-            out = product(jnp.concatenate([prod, vec], axis=0), high, low, plain)
-            half, vec = out[:order], out[order:]
-        elif not last:
-            out = product(jnp.concatenate([prod, lower, vec], axis=0), high, low, plain)
-            half, lower, vec = out[:order], out[order : 2 * order], out[2 * order :]
-        else:
-            out = product(jnp.concatenate([lower, vec], axis=0), high, low, plain)
-            lower, vec = out[:order], out[order:]
-        if not last:
-            prod = product(half, high, low, plain)
-            middle = 1.5 * ident - 0.5 * prod
-    high, low = blocks(lower)
-    wbar = product(vec, high, low, plain)[0:1] * inverse
-    eight = lower[0:8] * (jnp.sqrt(inverse) * (order - 1.0) ** 0.5) + wbar
-
-    tall = jnp.concatenate([eight] * groups, axis=0)
-    tall_row = lax.broadcasted_iota(jnp.int32, tall.shape, 0) // 8
-    tall_block = lax.broadcasted_iota(jnp.int32, tall.shape, 1) // order
-    out = product(jnp.where(tall_row == tall_block, tall, 0.0), pert_high, pert_low, plain)
-    for p in range(groups):
+        )
+
+    tall_high, tall_low = split(jnp.concatenate(tall, axis=1))
+    both = dot(jnp.concatenate([tall_high, tall_low], axis=0), pert_high, plain)
+    count = groups * mem_here
+    out = both[:count] + both[count:] + dot(tall_high, pert_low, plain)
+    for i in range(mem_here):
         for q in range(height):
             lanes = slice(q * LANES, (q + 1) * LANES)
-            o_ref[pl.ds(p * height + q, mem_here, stride=rows), :] = (
-                out[8 * p : 8 * p + mem_here, lanes] + mean_ref[p : p + 1, lanes]
+            o_ref[pl.ds(i * rows + q, groups, stride=height), :] = (
+                out[i * groups : (i + 1) * groups, lanes] + mean_ref[:, lanes]
             )
 
 
-def kernel_call(body, out_shape, scratch=(), smem=()):
+def kernel_call(body, *out_shapes, scratch=(), smem=(), work=None):
     def call(*args):
         specs = [
             pl.BlockSpec(memory_space=pltpu.SMEM if i in smem else pltpu.VMEM)
             for i in range(len(args))
         ]
-        return pl.pallas_call(
+        out = pl.pallas_call(
             body,
-            out_shape=jax.ShapeDtypeStruct(out_shape, jnp.float32),
+            out_shape=[jax.ShapeDtypeStruct(shape, jnp.float32) for shape in out_shapes],
             in_specs=specs,
-            out_specs=pl.BlockSpec(memory_space=pltpu.VMEM),
+            out_specs=[pl.BlockSpec(memory_space=pltpu.VMEM) for _ in out_shapes],
             scratch_shapes=list(scratch),
             compiler_params=pltpu.CompilerParams(vmem_limit_bytes=32 << 20),
+            cost_estimate=work
+            and pl.CostEstimate(flops=work, bytes_accessed=work, transcendentals=0),
         )(*args)
+        return out[0] if len(out_shapes) == 1 else out
 
     return call
 
@@ -349,39 +386,43 @@
     count = lax.axis_size("space")
     order = mem_here * groups
     height = rows // groups
-    extra = 2 * height // mem_here
-    stride = rows + extra
-    f32, bf16 = jnp.float32, jnp.bfloat16
+    stride = rows + 2 * height // mem_here
+    wide, cells = order * groups, height * LANES
+    f32 = jnp.float32
 
     both = jnp.concatenate([prior_ensemble, wind[None]], axis=0)
-    strips = kernel_call(strips_kernel, (2 * rows, LANES))(both)
     forward = [(i, (i + 1) % count) for i in range(count)]
     backward = [(i, (i - 1) % count) for i in range(count)]
-    east = lax.ppermute(strips, "space", backward)
-    west = lax.ppermute(strips, "space", forward)
-    inside = kernel_call(interior_kernel, (mem_here * stride, LANES), smem=(0,))(
-        obs_count, both, observed_cell_value, obs_value, obs_weight
-    )
-    payload = kernel_call(edges_kernel, (mem_here * stride, LANES))(strips, east, west, inside)
+    eastern = kernel_call(functools.partial(edge_kernel, 0, SUBSTEPS), (rows, LANES))(both)
+    western = kernel_call(
+        functools.partial(edge_kernel, STRIP - SUBSTEPS, STRIP - 2 * SUBSTEPS), (rows, LANES), work=None
+    )(both)
+    east = lax.ppermute(western, "space", backward)
+    west = lax.ppermute(eastern, "space", forward)
+    inside, near = kernel_call(interior_kernel, (mem_here * stride, LANES), (2 * rows, LANES))(
+        obs_count.reshape(1, 1), both, observed_cell_value, obs_value, obs_weight
+    )
+    payload = kernel_call(edges_kernel, (mem_here * stride, LANES))(near, west, east, inside)
 
     def swap(x, k):
         return lax.ppermute(x, "member", [(i, i ^ k) for i in range(groups)])
 
-    chips = range(2, groups, 2)
-    others = [swap(payload, k) for k in reversed(chips)][::-1]
+    others = [swap(payload, k) for k in range(2, groups, 2)]
     cat = jnp.concatenate([payload, *others], axis=0)
-    sibling = swap(cat, 1)
+    first = swap(jnp.concatenate([payload, others[-1]], axis=0), 1)
+    size = payload.shape[0]
+    sibling = jnp.concatenate(
+        [first[:size], *[swap(x, 1) for x in others[:-1]], first[size:]], axis=0
+    )
     me = lax.axis_index("member").astype(jnp.int32).reshape(1)
-    wide = order * groups
-    cells = height * LANES
     out = kernel_call(
         functools.partial(analysis_kernel, (mem_here, rows, groups)),
         (mem_here * rows, LANES),
         scratch=[
             pltpu.VMEM((groups * 2 * height, LANES), f32),
             pltpu.VMEM((wide, cells), f32),
-            pltpu.VMEM((wide + 16, cells), f32),
-            pltpu.VMEM((max(groups, 8), cells), f32),
+            pltpu.VMEM((wide, cells), f32),
+            pltpu.VMEM((groups, cells), f32),
         ],
         smem=(0,),
     )(me, cat, sibling)
@@ -399,7 +440,8 @@
         and 2 * (rows // groups) % mem_here == 0
         and rows % 8 == 0
         and groups & (groups - 1) == 0
-        and 2 <= groups <= 16
+        and groups in (8, 16)
+        and LANES % (mem_here * groups) == 0
         and lax.axis_size("space") % 2 == 0
         and rest[-1].shape[0] == 1
         and whole_tile <= GATHER_BYTES

time: 21.8 us -> 20.4 us (0.936)
  waiting for transfers between devices: 6.45 us -> 5.65 us
  Pallas kernels: 4.73 us -> 3.99 us
    pallas_call x4 -> x5, Pallas kernels: 4.73 us -> 3.99 us  [call(): pl.pallas_call(body, out_shape=[jax.ShapeDtypeStruct(shape, jnp.float32)...]
    ppermute x2, waiting for transfers between devices: 1.14 us -> 0.58 us  [the longest x1 0.4 us: gathered(): west = lax.ppermute(eastern, 'space', forward)]
    ppermute x4 -> x6, waiting for transfers between devices: 5.31 us -> 5.07 us  [swap(): return lax.ppermute(x, 'member', [(i, i ^ k) for i in range(groups)])]
    ppermute x4 -> x6, starting transfers between devices: 3.62 us -> 3.63 us  [swap(): return lax.ppermute(x, 'member', [(i, i ^ k) for i in range(groups)])]
  transfers between devices with their start and end apart: 6 -> 8, of which waited for: 6 -> 7; matrix products, arithmetic and copies ran while one was open for 0% -> 0% of each run, Pallas kernels for 2% -> 3%
where the time goes in v2:
time: 20.4 us; the launch traced here: 20.1 us
  starting transfers between devices  8.82 us (43%)
  waiting for transfers between devices  5.65 us (28%)
  Pallas kernels  3.99 us (20%)
  other arithmetic  0.91 us (4%)
  between operations  0.76 us (4%)
    ppermute x6, waiting for transfers between devices, swap(): return lax.ppermute(x, 'member', [(i, i ^ k) for i in range(groups)])  5.07 us
    pallas_call x5, Pallas kernels, call(): pl.pallas_call(body, out_shape=[jax.ShapeDtypeStruct(shape, jnp.float32)...  3.99 us
    ppermute x6, starting transfers between devices, swap(): return lax.ppermute(x, 'member', [(i, i ^ k) for i in range(groups)])  3.63 us
    ppermute x1, starting transfers between devices, gathered(): west = lax.ppermute(eastern, 'space', forward)  3.08 us
    ppermute x1, starting transfers between devices, gathered(): east = lax.ppermute(western, 'space', backward)  2.11 us
    concatenate x1, other arithmetic, gathered(): both = jnp.concatenate([prior_ensemble, wind[None]], axis=0)  0.86 us
  transfers between devices with their start and end apart: 8, of which 7 were waited for; matrix products, arithmetic and copies ran while one was open for 0% of the time, Pallas kernels for 3%

profile of v2, /device:TPU:0, one launch (start us, length us, event | category | flops | bytes accessed | tf_op | source)
XLA Modules:
  0.0 20.1 jit_solution(2260662946076518371)
XLA Ops:
  0.0 0.9 %pad_maximum_fusion.3.u_ref = f32[5,32,128]{2,1,0:T(8,128)S(1)} fusion(f32[1,32,128]{2,1,0:T(8,128)} %bitcast.5, f32[4,32,128]{2,1,0:T(8,128)} %param.6), kind=kLoop, calls=%fused_computation.3 | loop fusion | flops 20480 | bytes 163840 | tf_op jit(solution)/shard_map/concatenate | solution.py:393
  0.9 0.1 shard_map.65
  1.0 3.1 %collective-permute-start = (f32[32,128]{1,0:T(8,128)S(1)}, f32[32,128]{1,0:T(8,128)S(1)}, u32[]{:S(2)}, u32[]{:S(2)}) collective-permute-start(f32[32,128]{1,0:T(8,128)S(1)} %shard_map.65), channel_id=1, source_target_pairs={{0,8},{8,16},{16,24},{24,0},{1,9},{9,17},{17,25},{25,1},{2,10},{10... | collective-permute-start | bytes 49160 | tf_op jit(solution)/shard_map/ppermute | solution.py:401
  4.0 0.0 copy-start.1
  4.0 0.0 copy-start.2
  4.0 0.1 shard_map.66
  4.1 0.0 copy-start
  4.2 2.1 %collective-permute-start.1 = (f32[32,128]{1,0:T(8,128)S(1)}, f32[32,128]{1,0:T(8,128)S(1)}, u32[]{:S(2)}, u32[]{:S(2)}) collective-permute-start(f32[32,128]{1,0:T(8,128)S(1)} %shard_map.66), channel_id=1, source_target_pairs={{0,24},{8,0},{16,8},{24,16},{1,25},{9,1},{17,9},{25,17},{2,26},{10... | collective-permute-start | bytes 49160 | tf_op jit(solution)/shard_map/ppermute | solution.py:400
  6.9 0.0 copy-done.1
  6.9 0.0 copy-done.2
  6.9 0.0 copy-done
  6.9 0.4 %shard_map.64 = (f32[136,128]{1,0:T(8,128)S(1)}, f32[64,128]{1,0:T(8,128)S(1)}) custom-call(s32[1,1]{1,0:T(1,128)} %bitcast.4.count_ref, f32[5,32,128]{2,1,0:T(8,128)S(1)} %pad_maximum_fusion.3.u_ref, s32[1,512]{1,0:T(1,128)S(1)} %copy-done, f32[1,512]{1,0:T(1,128)S(1)} %copy-done.1, f32[1,512]{1,0:T(1,128)S(1)} %copy-done.2), custom_call_target="tpu_custom_call" | custom-call | tf_op jit(solution)/shard_map/pallas_call | solution.py:368
  7.4 0.4 %collective-permute-done.west_ref = f32[32,128]{1,0:T(8,128)S(1)} collective-permute-done((f32[32,128]{1,0:T(8,128)S(1)}, f32[32,128]{1,0:T(8,128)S(1)}, u32[]{:S(2)}, u32[]{:S(2)}) %collective-permute-start) | collective-permute-done | bytes 16416 | tf_op jit(solution)/shard_map/ppermute | solution.py:401
  7.8 0.2 collective-permute-done.1.east_ref
  8.0 0.4 %shard_map.67 = f32[136,128]{1,0:T(8,128)S(1)} custom-call(f32[64,128]{1,0:T(8,128)S(1)} %get-tuple-element.7.q_ref, f32[32,128]{1,0:T(8,128)S(1)} %collective-permute-done.west_ref, f32[32,128]{1,0:T(8,128)S(1)} %collective-permute-done.1.east_ref, f32[136,128]{1,0:T(8,128)S(1)} %get-tuple-element.8.f_in_ref), custom_call_target="tpu_custom_call" | custom-call | tf_op jit(solution)/shard_map/pallas_call | solution.py:368
  8.4 2.7 %collective-permute-start.4 = (f32[136,128]{1,0:T(8,128)S(1)}, f32[136,128]{1,0:T(8,128)S(1)}, u32[]{:S(2)}, u32[]{:S(2)}) collective-permute-start(f32[136,128]{1,0:T(8,128)S(1)} %shard_map.67), channel_id=1, source_target_pairs={{0,6},{1,7},{2,4},{3,5},{4,2},{5,3},{6,0},{7,1},{8,14},{9,15},{10,... | collective-permute-start | bytes 208904 | tf_op jit(solution)/shard_map/ppermute | solution.py:408
  11.0 0.5 %collective-permute-start.2 = (f32[136,128]{1,0:T(8,128)S(1)}, f32[136,128]{1,0:T(8,128)S(1)}, u32[]{:S(2)}, u32[]{:S(2)}) collective-permute-start(f32[136,128]{1,0:T(8,128)S(1)} %shard_map.67), channel_id=1, source_target_pairs={{0,2},{1,3},{2,0},{3,1},{4,6},{5,7},{6,4},{7,5},{8,10},{9,11},{10,... | collective-permute-start | bytes 208904 | tf_op jit(solution)/shard_map/ppermute | solution.py:408
  11.6 0.3 %collective-permute-start.3 = (f32[136,128]{1,0:T(8,128)S(1)}, f32[136,128]{1,0:T(8,128)S(1)}, u32[]{:S(2)}, u32[]{:S(2)}) collective-permute-start(f32[136,128]{1,0:T(8,128)S(1)} %shard_map.67), channel_id=1, source_target_pairs={{0,4},{1,5},{2,6},{3,7},{4,0},{5,1},{6,2},{7,3},{8,12},{9,13},{10,... | collective-permute-start | bytes 208904 | tf_op jit(solution)/shard_map/ppermute | solution.py:408
  11.9 1.8 %collective-permute-done.4 = f32[136,128]{1,0:T(8,128)S(1)} collective-permute-done((f32[136,128]{1,0:T(8,128)S(1)}, f32[136,128]{1,0:T(8,128)S(1)}, u32[]{:S(2)}, u32[]{:S(2)}) %collective-permute-start.4) | collective-permute-done | bytes 69664 | tf_op jit(solution)/shard_map/ppermute | solution.py:408
  13.8 0.1 collective-permute-start.5
  13.9 1.5 %collective-permute-done.2 = f32[136,128]{1,0:T(8,128)S(1)} collective-permute-done((f32[136,128]{1,0:T(8,128)S(1)}, f32[136,128]{1,0:T(8,128)S(1)}, u32[]{:S(2)}, u32[]{:S(2)}) %collective-permute-start.2) | collective-permute-done | bytes 69664 | tf_op jit(solution)/shard_map/ppermute | solution.py:408
  15.4 0.0 collective-permute-start.6
  15.4 0.5 %collective-permute-done.3 = f32[136,128]{1,0:T(8,128)S(1)} collective-permute-done((f32[136,128]{1,0:T(8,128)S(1)}, f32[136,128]{1,0:T(8,128)S(1)}, u32[]{:S(2)}, u32[]{:S(2)}) %collective-permute-start.3) | collective-permute-done | bytes 69664 | tf_op jit(solution)/shard_map/ppermute | solution.py:408
  15.9 0.0 collective-permute-start.7
  15.9 0.0 collective-permute-done.5
  16.0 0.7 %collective-permute-done.6 = f32[136,128]{1,0:T(8,128)S(1)} collective-permute-done((f32[136,128]{1,0:T(8,128)S(1)}, f32[136,128]{1,0:T(8,128)S(1)}, u32[]{:S(2)}, u32[]{:S(2)}) %collective-permute-start.6) | collective-permute-done | bytes 69664 | tf_op jit(solution)/shard_map/ppermute | solution.py:408
  16.6 0.5 %collective-permute-done.7 = f32[136,128]{1,0:T(8,128)S(1)} collective-permute-done((f32[136,128]{1,0:T(8,128)S(1)}, f32[136,128]{1,0:T(8,128)S(1)}, u32[]{:S(2)}, u32[]{:S(2)}) %collective-permute-start.7) | collective-permute-done | bytes 69664 | tf_op jit(solution)/shard_map/ppermute | solution.py:408
  17.2 3.0 %shard_map.68 = f32[128,128]{1,0:T(8,128)} custom-call(s32[1]{0:T(128)} %bitcast.me_ref, f32[544,128]{1,0:T(8,128)S(1)} %pad_maximum_fusion.cat_ref, f32[544,128]{1,0:T(8,128)S(1)} %pad_maximum_fusion.1.sib_ref), custom_call_target="tpu_custom_call" | custom-call | tf_op jit(solution)/shard_map/pallas_call | solution.py:368
  (4 shorter events, 0.1 us)
Async XLA Ops:
  1.0 6.8 %collective-permute-start = (f32[32,128]{1,0:T(8,128)S(1)}, f32[32,128]{1,0:T(8,128)S(1)}, u32[]{:S(2)}, u32[]{:S(2)}) collective-permute-start(f32[32,128]{1,0:T(8,128)S(1)} %shard_map.65), channel_id=1, source_target_pairs={{0,8},{8,16},{16,24},{24,0},{1,9},{9,17},{17,25},{25,1},{2,10},{10... | collective-permute-start | bytes 49160 | tf_op jit(solution)/shard_map/ppermute | solution.py:401
  4.0 2.9 %copy-start.1 = (f32[1,512]{1,0:T(1,128)S(1)}, f32[1,512]{1,0:T(1,128)}, u32[]{:S(2)}) copy-start(f32[1,512]{1,0:T(1,128)} %value_ref.1) | copy-start | bytes 6148
  4.0 2.9 %copy-start.2 = (f32[1,512]{1,0:T(1,128)S(1)}, f32[1,512]{1,0:T(1,128)}, u32[]{:S(2)}) copy-start(f32[1,512]{1,0:T(1,128)} %weight_ref.1) | copy-start | bytes 6148
  4.1 2.8 %copy-start = (s32[1,512]{1,0:T(1,128)S(1)}, s32[1,512]{1,0:T(1,128)}, u32[]{:S(2)}) copy-start(s32[1,512]{1,0:T(1,128)} %cell_ref.1) | copy-start | bytes 6148
  4.2 3.8 %collective-permute-start.1 = (f32[32,128]{1,0:T(8,128)S(1)}, f32[32,128]{1,0:T(8,128)S(1)}, u32[]{:S(2)}, u32[]{:S(2)}) collective-permute-start(f32[32,128]{1,0:T(8,128)S(1)} %shard_map.66), channel_id=1, source_target_pairs={{0,24},{8,0},{16,8},{24,16},{1,25},{9,1},{17,9},{25,17},{2,26},{10... | collective-permute-start | bytes 49160 | tf_op jit(solution)/shard_map/ppermute | solution.py:400
  8.4 5.4 %collective-permute-start.4 = (f32[136,128]{1,0:T(8,128)S(1)}, f32[136,128]{1,0:T(8,128)S(1)}, u32[]{:S(2)}, u32[]{:S(2)}) collective-permute-start(f32[136,128]{1,0:T(8,128)S(1)} %shard_map.67), channel_id=1, source_target_pairs={{0,6},{1,7},{2,4},{3,5},{4,2},{5,3},{6,0},{7,1},{8,14},{9,15},{10,... | collective-permute-start | bytes 208904 | tf_op jit(solution)/shard_map/ppermute | solution.py:408
  11.0 4.3 %collective-permute-start.2 = (f32[136,128]{1,0:T(8,128)S(1)}, f32[136,128]{1,0:T(8,128)S(1)}, u32[]{:S(2)}, u32[]{:S(2)}) collective-permute-start(f32[136,128]{1,0:T(8,128)S(1)} %shard_map.67), channel_id=1, source_target_pairs={{0,2},{1,3},{2,0},{3,1},{4,6},{5,7},{6,4},{7,5},{8,10},{9,11},{10,... | collective-permute-start | bytes 208904 | tf_op jit(solution)/shard_map/ppermute | solution.py:408
  11.6 4.3 %collective-permute-start.3 = (f32[136,128]{1,0:T(8,128)S(1)}, f32[136,128]{1,0:T(8,128)S(1)}, u32[]{:S(2)}, u32[]{:S(2)}) collective-permute-start(f32[136,128]{1,0:T(8,128)S(1)} %shard_map.67), channel_id=1, source_target_pairs={{0,4},{1,5},{2,6},{3,7},{4,0},{5,1},{6,2},{7,3},{8,12},{9,13},{10,... | collective-permute-start | bytes 208904 | tf_op jit(solution)/shard_map/ppermute | solution.py:408
  13.8 2.2 %collective-permute-start.5 = (f32[272,128]{1,0:T(8,128)S(1)}, f32[272,128]{1,0:T(8,128)S(1)}, u32[]{:S(2)}, u32[]{:S(2)}) collective-permute-start(f32[272,128]{1,0:T(8,128)S(1)} %pad_maximum_fusion.2), channel_id=1, source_target_pairs={{0,1},{1,0},{2,3},{3,2},{4,5},{5,4},{6,7},{7,6},{8,9},{9,8},{10,11... | collective-permute-start | bytes 417800 | tf_op jit(solution)/shard_map/ppermute | solution.py:408
  15.4 1.3 %collective-permute-start.6 = (f32[136,128]{1,0:T(8,128)S(1)}, f32[136,128]{1,0:T(8,128)S(1)}, u32[]{:S(2)}, u32[]{:S(2)}) collective-permute-start(f32[136,128]{1,0:T(8,128)S(1)} %collective-permute-done.2), channel_id=1, source_target_pairs={{0,1},{1,0},{2,3},{3,2},{4,5},{5,4},{6,7},{7,6},{8,9},{9,8},{10,11... | collective-permute-start | bytes 208904 | tf_op jit(solution)/shard_map/ppermute | solution.py:408
  15.9 1.3 %collective-permute-start.7 = (f32[136,128]{1,0:T(8,128)S(1)}, f32[136,128]{1,0:T(8,128)S(1)}, u32[]{:S(2)}, u32[]{:S(2)}) collective-permute-start(f32[136,128]{1,0:T(8,128)S(1)} %collective-permute-done.3), channel_id=1, source_target_pairs={{0,1},{1,0},{2,3},{3,2},{4,5},{5,4},{6,7},{7,6},{8,9},{9,8},{10,11... | collective-permute-start | bytes 208904 | tf_op jit(solution)/shard_map/ppermute | solution.py:408

commit v3 on v2

--- a/solution.py
+++ b/solution.py
@@ -215,6 +215,11 @@
         f_ref[at, :] = f_in_ref[at, :]
 
 
+def visits(groups):
+    chips = [groups - 2, *range(2, groups - 2, 2)]
+    return [0, *[chip + (i + 1) % 2 for i, chip in enumerate(chips)]]
+
+
 def analysis_kernel(dims, me_ref, cat_ref, sib_ref, o_ref, ob_ref, pert_ref, scaled_ref, mean_ref):
     mem_here, rows, groups = dims
     f32, bf16 = jnp.float32, jnp.bfloat16
@@ -237,7 +242,7 @@
 
     for side, ref in enumerate((cat_ref, sib_ref)):
         for k in range(groups // 2):
-            patch = me ^ (2 * k + side)
+            patch = me ^ (visits(groups)[k] ^ side)
             base = k * mem_here * stride
             lines = [
                 ref[base + m * stride + rows : base + (m + 1) * stride, :] for m in range(mem_here)
@@ -407,13 +412,10 @@
     def swap(x, k):
         return lax.ppermute(x, "member", [(i, i ^ k) for i in range(groups)])
 
-    others = [swap(payload, k) for k in range(2, groups, 2)]
-    cat = jnp.concatenate([payload, *others], axis=0)
-    first = swap(jnp.concatenate([payload, others[-1]], axis=0), 1)
-    size = payload.shape[0]
-    sibling = jnp.concatenate(
-        [first[:size], *[swap(x, 1) for x in others[:-1]], first[size:]], axis=0
-    )
+    held = [payload] + [swap(payload, k) for k in visits(groups)[1:]]
+    cat = jnp.concatenate(held, axis=0)
+    first = jnp.concatenate(held[:2], axis=0)
+    sibling = jnp.concatenate([swap(x, 1) for x in [first, *held[2:]]], axis=0)
     me = lax.axis_index("member").astype(jnp.int32).reshape(1)
     out = kernel_call(
         functools.partial(analysis_kernel, (mem_here, rows, groups)),

time: 20.4 us -> 19.3 us (0.946)
  waiting for transfers between devices: 5.65 us -> 4.22 us
  starting transfers between devices: 8.82 us -> 9.19 us
    ppermute x6, waiting for transfers between devices: 5.07 us -> 3.65 us  [swap(): return lax.ppermute(x, 'member', [(i, i ^ k) for i in range(groups)])]
    ppermute x6, starting transfers between devices: 3.63 us -> 4 us  [swap(): return lax.ppermute(x, 'member', [(i, i ^ k) for i in range(groups)])]
  transfers between devices with their start and end apart: 8 -> 8, of which waited for: 7 -> 6; matrix products, arithmetic and copies ran while one was open for 0% -> 0% of each run, Pallas kernels for 3% -> 3%
where the time goes in v3:
time: 19.3 us; the launch traced here: 19.1 us
  starting transfers between devices  9.19 us (48%)
  waiting for transfers between devices  4.22 us (22%)
  Pallas kernels  3.98 us (21%)
  other arithmetic  0.91 us (5%)
  between operations  0.73 us (4%)
    ppermute x6, starting transfers between devices, swap(): return lax.ppermute(x, 'member', [(i, i ^ k) for i in range(groups)])  4 us
    pallas_call x5, Pallas kernels, call(): pl.pallas_call(body, out_shape=[jax.ShapeDtypeStruct(shape, jnp.float32)...  3.98 us
    ppermute x6, waiting for transfers between devices, swap(): return lax.ppermute(x, 'member', [(i, i ^ k) for i in range(groups)])  3.65 us
    ppermute x1, starting transfers between devices, gathered(): west = lax.ppermute(eastern, 'space', forward)  3.08 us
    ppermute x1, starting transfers between devices, gathered(): east = lax.ppermute(western, 'space', backward)  2.11 us
    concatenate x1, other arithmetic, gathered(): both = jnp.concatenate([prior_ensemble, wind[None]], axis=0)  0.86 us
    ppermute x1, waiting for transfers between devices, gathered(): west = lax.ppermute(eastern, 'space', forward)  0.4 us
  transfers between devices with their start and end apart: 8, of which 6 were waited for; matrix products, arithmetic and copies ran while one was open for 0% of the time, Pallas kernels for 3%

profile of v3, /device:TPU:0, one launch (start us, length us, event | category | flops | bytes accessed | tf_op | source)
XLA Modules:
  0.0 19.1 jit_solution(5169124064640943078)
XLA Ops:
  0.0 0.9 %pad_maximum_fusion.3.u_ref = f32[5,32,128]{2,1,0:T(8,128)S(1)} fusion(f32[1,32,128]{2,1,0:T(8,128)} %bitcast.5, f32[4,32,128]{2,1,0:T(8,128)} %param.6), kind=kLoop, calls=%fused_computation.3 | loop fusion | flops 20480 | bytes 163840 | tf_op jit(solution)/shard_map/concatenate | solution.py:398
  0.9 0.1 shard_map.65
  1.0 3.1 %collective-permute-start = (f32[32,128]{1,0:T(8,128)S(1)}, f32[32,128]{1,0:T(8,128)S(1)}, u32[]{:S(2)}, u32[]{:S(2)}) collective-permute-start(f32[32,128]{1,0:T(8,128)S(1)} %shard_map.65), channel_id=1, source_target_pairs={{0,8},{8,16},{16,24},{24,0},{1,9},{9,17},{17,25},{25,1},{2,10},{10... | collective-permute-start | bytes 49160 | tf_op jit(solution)/shard_map/ppermute | solution.py:406
  4.0 0.0 copy-start.1
  4.0 0.0 copy-start.2
  4.0 0.1 shard_map.66
  4.1 0.0 copy-start
  4.2 2.1 %collective-permute-start.1 = (f32[32,128]{1,0:T(8,128)S(1)}, f32[32,128]{1,0:T(8,128)S(1)}, u32[]{:S(2)}, u32[]{:S(2)}) collective-permute-start(f32[32,128]{1,0:T(8,128)S(1)} %shard_map.66), channel_id=1, source_target_pairs={{0,24},{8,0},{16,8},{24,16},{1,25},{9,1},{17,9},{25,17},{2,26},{10... | collective-permute-start | bytes 49160 | tf_op jit(solution)/shard_map/ppermute | solution.py:405
  6.9 0.0 copy-done.1
  6.9 0.0 copy-done.2
  6.9 0.0 copy-done
  6.9 0.4 %shard_map.64 = (f32[136,128]{1,0:T(8,128)S(1)}, f32[64,128]{1,0:T(8,128)S(1)}) custom-call(s32[1,1]{1,0:T(1,128)} %bitcast.4.count_ref, f32[5,32,128]{2,1,0:T(8,128)S(1)} %pad_maximum_fusion.3.u_ref, s32[1,512]{1,0:T(1,128)S(1)} %copy-done, f32[1,512]{1,0:T(1,128)S(1)} %copy-done.1, f32[1,512]{1,0:T(1,128)S(1)} %copy-done.2), custom_call_target="tpu_custom_call" | custom-call | tf_op jit(solution)/shard_map/pallas_call | solution.py:373
  7.4 0.4 %collective-permute-done.west_ref = f32[32,128]{1,0:T(8,128)S(1)} collective-permute-done((f32[32,128]{1,0:T(8,128)S(1)}, f32[32,128]{1,0:T(8,128)S(1)}, u32[]{:S(2)}, u32[]{:S(2)}) %collective-permute-start) | collective-permute-done | bytes 16416 | tf_op jit(solution)/shard_map/ppermute | solution.py:406
  7.8 0.2 collective-permute-done.1.east_ref
  8.0 0.4 %shard_map.67 = f32[136,128]{1,0:T(8,128)S(1)} custom-call(f32[64,128]{1,0:T(8,128)S(1)} %get-tuple-element.7.q_ref, f32[32,128]{1,0:T(8,128)S(1)} %collective-permute-done.west_ref, f32[32,128]{1,0:T(8,128)S(1)} %collective-permute-done.1.east_ref, f32[136,128]{1,0:T(8,128)S(1)} %get-tuple-element.8.f_in_ref), custom_call_target="tpu_custom_call" | custom-call | tf_op jit(solution)/shard_map/pallas_call | solution.py:373
  8.4 1.1 %collective-permute-start.2 = (f32[136,128]{1,0:T(8,128)S(1)}, f32[136,128]{1,0:T(8,128)S(1)}, u32[]{:S(2)}, u32[]{:S(2)}) collective-permute-start(f32[136,128]{1,0:T(8,128)S(1)} %shard_map.67), channel_id=1, source_target_pairs={{0,7},{1,6},{2,5},{3,4},{4,3},{5,2},{6,1},{7,0},{8,15},{9,14},{10,... | collective-permute-start | bytes 208904 | tf_op jit(solution)/shard_map/ppermute | solution.py:413
  9.5 0.7 %collective-permute-start.3 = (f32[136,128]{1,0:T(8,128)S(1)}, f32[136,128]{1,0:T(8,128)S(1)}, u32[]{:S(2)}, u32[]{:S(2)}) collective-permute-start(f32[136,128]{1,0:T(8,128)S(1)} %shard_map.67), channel_id=1, source_target_pairs={{0,2},{1,3},{2,0},{3,1},{4,6},{5,7},{6,4},{7,5},{8,10},{9,11},{10,... | collective-permute-start | bytes 208904 | tf_op jit(solution)/shard_map/ppermute | solution.py:413
  10.2 1.2 %collective-permute-start.4 = (f32[136,128]{1,0:T(8,128)S(1)}, f32[136,128]{1,0:T(8,128)S(1)}, u32[]{:S(2)}, u32[]{:S(2)}) collective-permute-start(f32[136,128]{1,0:T(8,128)S(1)} %shard_map.67), channel_id=1, source_target_pairs={{0,5},{1,4},{2,7},{3,6},{4,1},{5,0},{6,3},{7,2},{8,13},{9,12},{10,... | collective-permute-start | bytes 208904 | tf_op jit(solution)/shard_map/ppermute | solution.py:413
  11.4 2.2 %collective-permute-done.2 = f32[136,128]{1,0:T(8,128)S(1)} collective-permute-done((f32[136,128]{1,0:T(8,128)S(1)}, f32[136,128]{1,0:T(8,128)S(1)}, u32[]{:S(2)}, u32[]{:S(2)}) %collective-permute-start.2) | collective-permute-done | bytes 69664 | tf_op jit(solution)/shard_map/ppermute | solution.py:413
  13.6 0.2 %collective-permute-start.5 = (f32[272,128]{1,0:T(8,128)S(1)}, f32[272,128]{1,0:T(8,128)S(1)}, u32[]{:S(2)}, u32[]{:S(2)}) collective-permute-start(f32[272,128]{1,0:T(8,128)S(1)} %pad_maximum_fusion.2), channel_id=1, source_target_pairs={{0,1},{1,0},{2,3},{3,2},{4,5},{5,4},{6,7},{7,6},{8,9},{9,8},{10,11... | collective-permute-start | bytes 417800 | tf_op jit(solution)/shard_map/ppermute | solution.py:413
  13.8 0.5 %collective-permute-done.3 = f32[136,128]{1,0:T(8,128)S(1)} collective-permute-done((f32[136,128]{1,0:T(8,128)S(1)}, f32[136,128]{1,0:T(8,128)S(1)}, u32[]{:S(2)}, u32[]{:S(2)}) %collective-permute-start.3) | collective-permute-done | bytes 69664 | tf_op jit(solution)/shard_map/ppermute | solution.py:413
  14.4 0.3 %collective-permute-start.6 = (f32[136,128]{1,0:T(8,128)S(1)}, f32[136,128]{1,0:T(8,128)S(1)}, u32[]{:S(2)}, u32[]{:S(2)}) collective-permute-start(f32[136,128]{1,0:T(8,128)S(1)} %collective-permute-done.3), channel_id=1, source_target_pairs={{0,1},{1,0},{2,3},{3,2},{4,5},{5,4},{6,7},{7,6},{8,9},{9,8},{10,11... | collective-permute-start | bytes 208904 | tf_op jit(solution)/shard_map/ppermute | solution.py:413
  14.7 0.0 collective-permute-done.4
  14.7 0.5 %collective-permute-start.7 = (f32[136,128]{1,0:T(8,128)S(1)}, f32[136,128]{1,0:T(8,128)S(1)}, u32[]{:S(2)}, u32[]{:S(2)}) collective-permute-start(f32[136,128]{1,0:T(8,128)S(1)} %collective-permute-done.4), channel_id=1, source_target_pairs={{0,1},{1,0},{2,3},{3,2},{4,5},{5,4},{6,7},{7,6},{8,9},{9,8},{10,11... | collective-permute-start | bytes 208904 | tf_op jit(solution)/shard_map/ppermute | solution.py:413
  15.2 0.4 %collective-permute-done.6 = f32[136,128]{1,0:T(8,128)S(1)} collective-permute-done((f32[136,128]{1,0:T(8,128)S(1)}, f32[136,128]{1,0:T(8,128)S(1)}, u32[]{:S(2)}, u32[]{:S(2)}) %collective-permute-start.6) | collective-permute-done | bytes 69664 | tf_op jit(solution)/shard_map/ppermute | solution.py:413
  15.6 0.4 %collective-permute-done.7 = f32[136,128]{1,0:T(8,128)S(1)} collective-permute-done((f32[136,128]{1,0:T(8,128)S(1)}, f32[136,128]{1,0:T(8,128)S(1)}, u32[]{:S(2)}, u32[]{:S(2)}) %collective-permute-start.7) | collective-permute-done | bytes 69664 | tf_op jit(solution)/shard_map/ppermute | solution.py:413
  16.1 0.0 collective-permute-done.5
  16.1 3.0 %shard_map.68 = f32[128,128]{1,0:T(8,128)} custom-call(s32[1]{0:T(128)} %bitcast.me_ref, f32[544,128]{1,0:T(8,128)S(1)} %pad_maximum_fusion.cat_ref, f32[544,128]{1,0:T(8,128)S(1)} %pad_maximum_fusion.1.sib_ref), custom_call_target="tpu_custom_call" | custom-call | tf_op jit(solution)/shard_map/pallas_call | solution.py:373
  (3 shorter events, 0.0 us)
Async XLA Ops:
  1.0 6.8 %collective-permute-start = (f32[32,128]{1,0:T(8,128)S(1)}, f32[32,128]{1,0:T(8,128)S(1)}, u32[]{:S(2)}, u32[]{:S(2)}) collective-permute-start(f32[32,128]{1,0:T(8,128)S(1)} %shard_map.65), channel_id=1, source_target_pairs={{0,8},{8,16},{16,24},{24,0},{1,9},{9,17},{17,25},{25,1},{2,10},{10... | collective-permute-start | bytes 49160 | tf_op jit(solution)/shard_map/ppermute | solution.py:406
  4.0 2.9 %copy-start.1 = (f32[1,512]{1,0:T(1,128)S(1)}, f32[1,512]{1,0:T(1,128)}, u32[]{:S(2)}) copy-start(f32[1,512]{1,0:T(1,128)} %value_ref.1) | copy-start | bytes 6148
  4.0 2.9 %copy-start.2 = (f32[1,512]{1,0:T(1,128)S(1)}, f32[1,512]{1,0:T(1,128)}, u32[]{:S(2)}) copy-start(f32[1,512]{1,0:T(1,128)} %weight_ref.1) | copy-start | bytes 6148
  4.1 2.8 %copy-start = (s32[1,512]{1,0:T(1,128)S(1)}, s32[1,512]{1,0:T(1,128)}, u32[]{:S(2)}) copy-start(s32[1,512]{1,0:T(1,128)} %cell_ref.1) | copy-start | bytes 6148
  4.2 3.8 %collective-permute-start.1 = (f32[32,128]{1,0:T(8,128)S(1)}, f32[32,128]{1,0:T(8,128)S(1)}, u32[]{:S(2)}, u32[]{:S(2)}) collective-permute-start(f32[32,128]{1,0:T(8,128)S(1)} %shard_map.66), channel_id=1, source_target_pairs={{0,24},{8,0},{16,8},{24,16},{1,25},{9,1},{17,9},{25,17},{2,26},{10... | collective-permute-start | bytes 49160 | tf_op jit(solution)/shard_map/ppermute | solution.py:405
  8.4 5.2 %collective-permute-start.2 = (f32[136,128]{1,0:T(8,128)S(1)}, f32[136,128]{1,0:T(8,128)S(1)}, u32[]{:S(2)}, u32[]{:S(2)}) collective-permute-start(f32[136,128]{1,0:T(8,128)S(1)} %shard_map.67), channel_id=1, source_target_pairs={{0,7},{1,6},{2,5},{3,4},{4,3},{5,2},{6,1},{7,0},{8,15},{9,14},{10,... | collective-permute-start | bytes 208904 | tf_op jit(solution)/shard_map/ppermute | solution.py:413
  9.5 4.9 %collective-permute-start.3 = (f32[136,128]{1,0:T(8,128)S(1)}, f32[136,128]{1,0:T(8,128)S(1)}, u32[]{:S(2)}, u32[]{:S(2)}) collective-permute-start(f32[136,128]{1,0:T(8,128)S(1)} %shard_map.67), channel_id=1, source_target_pairs={{0,2},{1,3},{2,0},{3,1},{4,6},{5,7},{6,4},{7,5},{8,10},{9,11},{10,... | collective-permute-start | bytes 208904 | tf_op jit(solution)/shard_map/ppermute | solution.py:413
  10.2 4.5 %collective-permute-start.4 = (f32[136,128]{1,0:T(8,128)S(1)}, f32[136,128]{1,0:T(8,128)S(1)}, u32[]{:S(2)}, u32[]{:S(2)}) collective-permute-start(f32[136,128]{1,0:T(8,128)S(1)} %shard_map.67), channel_id=1, source_target_pairs={{0,5},{1,4},{2,7},{3,6},{4,1},{5,0},{6,3},{7,2},{8,13},{9,12},{10,... | collective-permute-start | bytes 208904 | tf_op jit(solution)/shard_map/ppermute | solution.py:413
  13.6 2.5 %collective-permute-start.5 = (f32[272,128]{1,0:T(8,128)S(1)}, f32[272,128]{1,0:T(8,128)S(1)}, u32[]{:S(2)}, u32[]{:S(2)}) collective-permute-start(f32[272,128]{1,0:T(8,128)S(1)} %pad_maximum_fusion.2), channel_id=1, source_target_pairs={{0,1},{1,0},{2,3},{3,2},{4,5},{5,4},{6,7},{7,6},{8,9},{9,8},{10,11... | collective-permute-start | bytes 417800 | tf_op jit(solution)/shard_map/ppermute | solution.py:413
  14.4 1.3 %collective-permute-start.6 = (f32[136,128]{1,0:T(8,128)S(1)}, f32[136,128]{1,0:T(8,128)S(1)}, u32[]{:S(2)}, u32[]{:S(2)}) collective-permute-start(f32[136,128]{1,0:T(8,128)S(1)} %collective-permute-done.3), channel_id=1, source_target_pairs={{0,1},{1,0},{2,3},{3,2},{4,5},{5,4},{6,7},{7,6},{8,9},{9,8},{10,11... | collective-permute-start | bytes 208904 | tf_op jit(solution)/shard_map/ppermute | solution.py:413
  14.7 1.4 %collective-permute-start.7 = (f32[136,128]{1,0:T(8,128)S(1)}, f32[136,128]{1,0:T(8,128)S(1)}, u32[]{:S(2)}, u32[]{:S(2)}) collective-permute-start(f32[136,128]{1,0:T(8,128)S(1)} %collective-permute-done.4), channel_id=1, source_target_pairs={{0,1},{1,0},{2,3},{3,2},{4,5},{5,4},{6,7},{7,6},{8,9},{9,8},{10,11... | collective-permute-start | bytes 208904 | tf_op jit(solution)/shard_map/ppermute | solution.py:413

commit v4 on v3

--- a/solution.py
+++ b/solution.py
@@ -129,15 +129,31 @@
     return total
 
 
-def substep(x, wind3):
+def stencil(x, east, west, wind3):
     rows = x.shape[0]
     row = lax.broadcasted_iota(jnp.int32, x.shape, 0)
-    east = pltpu.roll(x, LANES - 1, 1)
-    west = pltpu.roll(x, 1, 1)
     north = jnp.where(row == rows - 1, 0.0, pltpu.roll(x, rows - 1, 0))
     south = jnp.where(row == 0, 0.0, pltpu.roll(x, 1, 0))
     speed = wind3 + 0.075 * jnp.tanh(x)
     return 0.4 * x + 0.2 * (east + west) + 0.1 * (north + south) - speed * (east - west)
+
+
+def shifted(x, by):
+    return pltpu.roll(x, -by % LANES, 1) if by else x
+
+
+def substep(x, wind3):
+    return stencil(x, shifted(x, 1), shifted(x, -1), wind3)
+
+
+def substeps(x, wind3, count):
+    at = {k: shifted(x, k) for k in range(-count, count + 1)}
+    winds = {k: shifted(wind3, k) for k in range(1 - count, count)}
+    for reach in range(count - 1, -1, -1):
+        at = {
+            k: stencil(at[k], at[k + 1], at[k - 1], winds[k]) for k in range(-reach, reach + 1)
+        }
+    return at[0]
 
 
 def pieces(x, count):
@@ -199,8 +215,7 @@
         west = pltpu.roll(west, LANES - SUBSTEPS, 1)
         east = pltpu.roll(east, SUBSTEPS, 1)
     x, wind3 = full[0], 0.3 * full[1]
-    for _ in range(SUBSTEPS):
-        x = substep(x, wind3)
+    x = substeps(x, wind3, SUBSTEPS)
     mem_here = LANES // STRIP
     stride = f_ref.shape[0] // mem_here
     for m in range(mem_here):
@@ -220,7 +235,7 @@
     return [0, *[chip + (i + 1) % 2 for i, chip in enumerate(chips)]]
 
 
-def analysis_kernel(dims, me_ref, cat_ref, sib_ref, o_ref, ob_ref, pert_ref, scaled_ref, mean_ref):
+def analysis_kernel(dims, me_ref, cat_ref, sib_ref, o_ref, ob_ref, pert_ref, scaled_ref, mean_ref, done_ref, sems):
     mem_here, rows, groups = dims
     f32, bf16 = jnp.float32, jnp.bfloat16
     order = mem_here * groups
@@ -319,32 +334,33 @@
         for p in range(per):
             mine = group == p
             total = jnp.where(mine, jnp.sum(jnp.where(mine, square, 0.0), axis=1, keepdims=True), total)
-        square = total
-        inverse.append(1.0 / jnp.sqrt(square + 1e-06))
+        inverse.append(1.0 / jnp.sqrt(total + 1e-06))
         first = grams[t] * inverse[t]
         middle.append(1.5 * ident - 0.5 * first)
-        lower.append(middle[t])
         prod.append(1.5 * first - (0.5 * inverse[t]) * (twice[t][:order] * inverse[t]))
         vec[t] = 1.5 * vec[t] - (0.5 * inverse[t]) * twice[t][order:]
+        lower.append(middle[t][0:8])
     for step in range(NS_ITERS):
+        right = [weights(middle[t]) for t in sets]
         last = step == NS_ITERS - 1
-        right = [weights(middle[t]) for t in sets]
         if step:
             for t in sets:
-                left = ([] if last else [prod[t]]) + [lower[t], vec[t]]
+                left = ([] if last else [prod[t]]) + [vec[t][0:8], lower[t]]
                 out = product(jnp.concatenate(left, axis=0), right[t])
                 if not last:
                     prod[t], out = out[:order], out[order:]
-                lower[t], vec[t] = out[:order], out[order:]
-        if not last:
-            for t in sets:
-                prod[t] = product(prod[t], right[t])
+                vec[t], lower[t] = out, out[8:16]
+        for t in sets:
+            left = [vec[t]] if last else [prod[t], vec[t]]
+            out = product(jnp.concatenate(left, axis=0), right[t])
+            if not last:
+                prod[t], out = out[:order], out[order:]
                 middle[t] = 1.5 * ident - 0.5 * prod[t]
+            vec[t] = out
     pick = lax.broadcasted_iota(jnp.int32, (groups, LANES), 0)
     tall = []
     for t in sets:
-        wbar = product(vec[t], weights(lower[t]))[0:1] * inverse[t]
-        own = lower[t][0:mem_here] * (jnp.sqrt(inverse[t]) * (order - 1.0) ** 0.5) + wbar
+        own = lower[t] * (jnp.sqrt(inverse[t]) * (order - 1.0) ** 0.5) + vec[t][0:1] * inverse[t]
         keep = pick == lax.broadcasted_iota(jnp.int32, (groups, LANES), 1) // order + per * t
         tall.append(
             jnp.concatenate(
@@ -356,15 +372,21 @@
     both = dot(jnp.concatenate([tall_high, tall_low], axis=0), pert_high, plain)
     count = groups * mem_here
     out = both[:count] + both[count:] + dot(tall_high, pert_low, plain)
+    copies = []
     for i in range(mem_here):
         for q in range(height):
             lanes = slice(q * LANES, (q + 1) * LANES)
-            o_ref[pl.ds(i * rows + q, groups, stride=height), :] = (
+            done_ref[pl.ds(i * rows + q, groups, stride=height), :] = (
                 out[i * groups : (i + 1) * groups, lanes] + mean_ref[:, lanes]
             )
-
-
-def kernel_call(body, *out_shapes, scratch=(), smem=(), work=None):
+        at = pl.ds(i * rows, rows)
+        copies.append(pltpu.make_async_copy(done_ref.at[at], o_ref.at[at], sems.at[i]))
+        copies[i].start()
+    for copy in copies:
+        copy.wait()
+
+
+def kernel_call(body, *out_shapes, scratch=(), smem=(), out_space=pltpu.VMEM):
     def call(*args):
         specs = [
             pl.BlockSpec(memory_space=pltpu.SMEM if i in smem else pltpu.VMEM)
@@ -374,11 +396,9 @@
             body,
             out_shape=[jax.ShapeDtypeStruct(shape, jnp.float32) for shape in out_shapes],
             in_specs=specs,
-            out_specs=[pl.BlockSpec(memory_space=pltpu.VMEM) for _ in out_shapes],
+            out_specs=[pl.BlockSpec(memory_space=out_space) for _ in out_shapes],
             scratch_shapes=list(scratch),
             compiler_params=pltpu.CompilerParams(vmem_limit_bytes=32 << 20),
-            cost_estimate=work
-            and pl.CostEstimate(flops=work, bytes_accessed=work, transcendentals=0),
         )(*args)
         return out[0] if len(out_shapes) == 1 else out
 
@@ -400,7 +420,7 @@
     backward = [(i, (i - 1) % count) for i in range(count)]
     eastern = kernel_call(functools.partial(edge_kernel, 0, SUBSTEPS), (rows, LANES))(both)
     western = kernel_call(
-        functools.partial(edge_kernel, STRIP - SUBSTEPS, STRIP - 2 * SUBSTEPS), (rows, LANES), work=None
+        functools.partial(edge_kernel, STRIP - SUBSTEPS, STRIP - 2 * SUBSTEPS), (rows, LANES)
     )(both)
     east = lax.ppermute(western, "space", backward)
     west = lax.ppermute(eastern, "space", forward)
@@ -425,8 +445,11 @@
             pltpu.VMEM((wide, cells), f32),
             pltpu.VMEM((wide, cells), f32),
             pltpu.VMEM((groups, cells), f32),
+            pltpu.VMEM((mem_here * rows, LANES), f32),
+            pltpu.SemaphoreType.DMA((mem_here,)),
         ],
         smem=(0,),
+        out_space=pl.ANY,
     )(me, cat, sibling)
     return out.reshape(mem_here, rows, LANES)
 

time: 19.3 us -> 19.2 us (level)
  no operation moved by 1% of the time
where the time goes in v4:
time: 19.2 us; the launch traced here: 19 us
  starting transfers between devices  9.19 us (48%)
  waiting for transfers between devices  4.22 us (22%)
  Pallas kernels  3.88 us (20%)
  other arithmetic  0.91 us (5%)
  between operations  0.73 us (4%)
    ppermute x6, starting transfers between devices, swap(): return lax.ppermute(x, 'member', [(i, i ^ k) for i in range(groups)])  4 us
    pallas_call x5, Pallas kernels, call(): pl.pallas_call(body, out_shape=[jax.ShapeDtypeStruct(shape, jnp.float32)...  3.88 us
    ppermute x6, waiting for transfers between devices, swap(): return lax.ppermute(x, 'member', [(i, i ^ k) for i in range(groups)])  3.65 us
    ppermute x1, starting transfers between devices, gathered(): west = lax.ppermute(eastern, 'space', forward)  3.08 us
    ppermute x1, starting transfers between devices, gathered(): east = lax.ppermute(western, 'space', backward)  2.11 us
    concatenate x1, other arithmetic, gathered(): both = jnp.concatenate([prior_ensemble, wind[None]], axis=0)  0.86 us
    ppermute x1, waiting for transfers between devices, gathered(): west = lax.ppermute(eastern, 'space', forward)  0.4 us
  transfers between devices with their start and end apart: 8, of which 6 were waited for; matrix products, arithmetic and copies ran while one was open for 0% of the time, Pallas kernels for 3%

profile of v4, /device:TPU:0, one launch (start us, length us, event | category | flops | bytes accessed | tf_op | source)
XLA Modules:
  0.0 19.0 jit_solution(2125451868777364224)
XLA Ops:
  0.0 0.9 %pad_maximum_fusion.3.u_ref = f32[5,32,128]{2,1,0:T(8,128)S(1)} fusion(f32[1,32,128]{2,1,0:T(8,128)} %bitcast.5, f32[4,32,128]{2,1,0:T(8,128)} %param.6), kind=kLoop, calls=%fused_computation.3 | loop fusion | flops 20480 | bytes 163840 | tf_op jit(solution)/shard_map/concatenate | solution.py:418
  0.9 0.1 shard_map.65
  1.0 3.1 %collective-permute-start = (f32[32,128]{1,0:T(8,128)S(1)}, f32[32,128]{1,0:T(8,128)S(1)}, u32[]{:S(2)}, u32[]{:S(2)}) collective-permute-start(f32[32,128]{1,0:T(8,128)S(1)} %shard_map.65), channel_id=1, source_target_pairs={{0,8},{8,16},{16,24},{24,0},{1,9},{9,17},{17,25},{25,1},{2,10},{10... | collective-permute-start | bytes 49160 | tf_op jit(solution)/shard_map/ppermute | solution.py:426
  4.0 0.0 copy-start.1
  4.0 0.0 copy-start.2
  4.0 0.1 shard_map.66
  4.1 0.0 copy-start
  4.2 2.1 %collective-permute-start.1 = (f32[32,128]{1,0:T(8,128)S(1)}, f32[32,128]{1,0:T(8,128)S(1)}, u32[]{:S(2)}, u32[]{:S(2)}) collective-permute-start(f32[32,128]{1,0:T(8,128)S(1)} %shard_map.66), channel_id=1, source_target_pairs={{0,24},{8,0},{16,8},{24,16},{1,25},{9,1},{17,9},{25,17},{2,26},{10... | collective-permute-start | bytes 49160 | tf_op jit(solution)/shard_map/ppermute | solution.py:425
  6.9 0.0 copy-done.1
  6.9 0.0 copy-done.2
  6.9 0.0 copy-done
  6.9 0.4 %shard_map.64 = (f32[136,128]{1,0:T(8,128)S(1)}, f32[64,128]{1,0:T(8,128)S(1)}) custom-call(s32[1,1]{1,0:T(1,128)} %bitcast.4.count_ref, f32[5,32,128]{2,1,0:T(8,128)S(1)} %pad_maximum_fusion.3.u_ref, s32[1,512]{1,0:T(1,128)S(1)} %copy-done, f32[1,512]{1,0:T(1,128)S(1)} %copy-done.1, f32[1,512]{1,0:T(1,128)S(1)} %copy-done.2), custom_call_target="tpu_custom_call" | custom-call | tf_op jit(solution)/shard_map/pallas_call | solution.py:395
  7.4 0.4 %collective-permute-done.west_ref = f32[32,128]{1,0:T(8,128)S(1)} collective-permute-done((f32[32,128]{1,0:T(8,128)S(1)}, f32[32,128]{1,0:T(8,128)S(1)}, u32[]{:S(2)}, u32[]{:S(2)}) %collective-permute-start) | collective-permute-done | bytes 16416 | tf_op jit(solution)/shard_map/ppermute | solution.py:426
  7.8 0.2 collective-permute-done.1.east_ref
  8.0 0.3 %shard_map.67 = f32[136,128]{1,0:T(8,128)S(1)} custom-call(f32[64,128]{1,0:T(8,128)S(1)} %get-tuple-element.7.q_ref, f32[32,128]{1,0:T(8,128)S(1)} %collective-permute-done.west_ref, f32[32,128]{1,0:T(8,128)S(1)} %collective-permute-done.1.east_ref, f32[136,128]{1,0:T(8,128)S(1)} %get-tuple-element.8.f_in_ref), custom_call_target="tpu_custom_call" | custom-call | tf_op jit(solution)/shard_map/pallas_call | solution.py:395
  8.3 1.1 %collective-permute-start.2 = (f32[136,128]{1,0:T(8,128)S(1)}, f32[136,128]{1,0:T(8,128)S(1)}, u32[]{:S(2)}, u32[]{:S(2)}) collective-permute-start(f32[136,128]{1,0:T(8,128)S(1)} %shard_map.67), channel_id=1, source_target_pairs={{0,7},{1,6},{2,5},{3,4},{4,3},{5,2},{6,1},{7,0},{8,15},{9,14},{10,... | collective-permute-start | bytes 208904 | tf_op jit(solution)/shard_map/ppermute | solution.py:433
  9.4 0.7 %collective-permute-start.3 = (f32[136,128]{1,0:T(8,128)S(1)}, f32[136,128]{1,0:T(8,128)S(1)}, u32[]{:S(2)}, u32[]{:S(2)}) collective-permute-start(f32[136,128]{1,0:T(8,128)S(1)} %shard_map.67), channel_id=1, source_target_pairs={{0,2},{1,3},{2,0},{3,1},{4,6},{5,7},{6,4},{7,5},{8,10},{9,11},{10,... | collective-permute-start | bytes 208904 | tf_op jit(solution)/shard_map/ppermute | solution.py:433
  10.1 1.2 %collective-permute-start.4 = (f32[136,128]{1,0:T(8,128)S(1)}, f32[136,128]{1,0:T(8,128)S(1)}, u32[]{:S(2)}, u32[]{:S(2)}) collective-permute-start(f32[136,128]{1,0:T(8,128)S(1)} %shard_map.67), channel_id=1, source_target_pairs={{0,5},{1,4},{2,7},{3,6},{4,1},{5,0},{6,3},{7,2},{8,13},{9,12},{10,... | collective-permute-start | bytes 208904 | tf_op jit(solution)/shard_map/ppermute | solution.py:433
  11.3 2.2 %collective-permute-done.2 = f32[136,128]{1,0:T(8,128)S(1)} collective-permute-done((f32[136,128]{1,0:T(8,128)S(1)}, f32[136,128]{1,0:T(8,128)S(1)}, u32[]{:S(2)}, u32[]{:S(2)}) %collective-permute-start.2) | collective-permute-done | bytes 69664 | tf_op jit(solution)/shard_map/ppermute | solution.py:433
  13.5 0.2 %collective-permute-start.5 = (f32[272,128]{1,0:T(8,128)S(1)}, f32[272,128]{1,0:T(8,128)S(1)}, u32[]{:S(2)}, u32[]{:S(2)}) collective-permute-start(f32[272,128]{1,0:T(8,128)S(1)} %pad_maximum_fusion.2), channel_id=1, source_target_pairs={{0,1},{1,0},{2,3},{3,2},{4,5},{5,4},{6,7},{7,6},{8,9},{9,8},{10,11... | collective-permute-start | bytes 417800 | tf_op jit(solution)/shard_map/ppermute | solution.py:433
  13.8 0.5 %collective-permute-done.3 = f32[136,128]{1,0:T(8,128)S(1)} collective-permute-done((f32[136,128]{1,0:T(8,128)S(1)}, f32[136,128]{1,0:T(8,128)S(1)}, u32[]{:S(2)}, u32[]{:S(2)}) %collective-permute-start.3) | collective-permute-done | bytes 69664 | tf_op jit(solution)/shard_map/ppermute | solution.py:433
  14.3 0.3 %collective-permute-start.6 = (f32[136,128]{1,0:T(8,128)S(1)}, f32[136,128]{1,0:T(8,128)S(1)}, u32[]{:S(2)}, u32[]{:S(2)}) collective-permute-start(f32[136,128]{1,0:T(8,128)S(1)} %collective-permute-done.3), channel_id=1, source_target_pairs={{0,1},{1,0},{2,3},{3,2},{4,5},{5,4},{6,7},{7,6},{8,9},{9,8},{10,11... | collective-permute-start | bytes 208904 | tf_op jit(solution)/shard_map/ppermute | solution.py:433
  14.6 0.0 collective-permute-done.4
  14.6 0.5 %collective-permute-start.7 = (f32[136,128]{1,0:T(8,128)S(1)}, f32[136,128]{1,0:T(8,128)S(1)}, u32[]{:S(2)}, u32[]{:S(2)}) collective-permute-start(f32[136,128]{1,0:T(8,128)S(1)} %collective-permute-done.4), channel_id=1, source_target_pairs={{0,1},{1,0},{2,3},{3,2},{4,5},{5,4},{6,7},{7,6},{8,9},{9,8},{10,11... | collective-permute-start | bytes 208904 | tf_op jit(solution)/shard_map/ppermute | solution.py:433
  15.1 0.4 %collective-permute-done.6 = f32[136,128]{1,0:T(8,128)S(1)} collective-permute-done((f32[136,128]{1,0:T(8,128)S(1)}, f32[136,128]{1,0:T(8,128)S(1)}, u32[]{:S(2)}, u32[]{:S(2)}) %collective-permute-start.6) | collective-permute-done | bytes 69664 | tf_op jit(solution)/shard_map/ppermute | solution.py:433
  15.6 0.4 %collective-permute-done.7 = f32[136,128]{1,0:T(8,128)S(1)} collective-permute-done((f32[136,128]{1,0:T(8,128)S(1)}, f32[136,128]{1,0:T(8,128)S(1)}, u32[]{:S(2)}, u32[]{:S(2)}) %collective-permute-start.7) | collective-permute-done | bytes 69664 | tf_op jit(solution)/shard_map/ppermute | solution.py:433
  16.0 0.0 collective-permute-done.5
  16.0 2.9 %shard_map.68 = f32[128,128]{1,0:T(8,128)} custom-call(s32[1]{0:T(128)} %bitcast.me_ref, f32[544,128]{1,0:T(8,128)S(1)} %pad_maximum_fusion.cat_ref, f32[544,128]{1,0:T(8,128)S(1)} %pad_maximum_fusion.1.sib_ref), custom_call_target="tpu_custom_call" | custom-call | tf_op jit(solution)/shard_map/pallas_call | solution.py:395
  (3 shorter events, 0.0 us)
Async XLA Ops:
  1.0 6.8 %collective-permute-start = (f32[32,128]{1,0:T(8,128)S(1)}, f32[32,128]{1,0:T(8,128)S(1)}, u32[]{:S(2)}, u32[]{:S(2)}) collective-permute-start(f32[32,128]{1,0:T(8,128)S(1)} %shard_map.65), channel_id=1, source_target_pairs={{0,8},{8,16},{16,24},{24,0},{1,9},{9,17},{17,25},{25,1},{2,10},{10... | collective-permute-start | bytes 49160 | tf_op jit(solution)/shard_map/ppermute | solution.py:426
  4.0 2.9 %copy-start.1 = (f32[1,512]{1,0:T(1,128)S(1)}, f32[1,512]{1,0:T(1,128)}, u32[]{:S(2)}) copy-start(f32[1,512]{1,0:T(1,128)} %value_ref.1) | copy-start | bytes 6148
  4.0 2.9 %copy-start.2 = (f32[1,512]{1,0:T(1,128)S(1)}, f32[1,512]{1,0:T(1,128)}, u32[]{:S(2)}) copy-start(f32[1,512]{1,0:T(1,128)} %weight_ref.1) | copy-start | bytes 6148
  4.1 2.8 %copy-start = (s32[1,512]{1,0:T(1,128)S(1)}, s32[1,512]{1,0:T(1,128)}, u32[]{:S(2)}) copy-start(s32[1,512]{1,0:T(1,128)} %cell_ref.1) | copy-start | bytes 6148
  4.2 3.8 %collective-permute-start.1 = (f32[32,128]{1,0:T(8,128)S(1)}, f32[32,128]{1,0:T(8,128)S(1)}, u32[]{:S(2)}, u32[]{:S(2)}) collective-permute-start(f32[32,128]{1,0:T(8,128)S(1)} %shard_map.66), channel_id=1, source_target_pairs={{0,24},{8,0},{16,8},{24,16},{1,25},{9,1},{17,9},{25,17},{2,26},{10... | collective-permute-start | bytes 49160 | tf_op jit(solution)/shard_map/ppermute | solution.py:425
  8.3 5.2 %collective-permute-start.2 = (f32[136,128]{1,0:T(8,128)S(1)}, f32[136,128]{1,0:T(8,128)S(1)}, u32[]{:S(2)}, u32[]{:S(2)}) collective-permute-start(f32[136,128]{1,0:T(8,128)S(1)} %shard_map.67), channel_id=1, source_target_pairs={{0,7},{1,6},{2,5},{3,4},{4,3},{5,2},{6,1},{7,0},{8,15},{9,14},{10,... | collective-permute-start | bytes 208904 | tf_op jit(solution)/shard_map/ppermute | solution.py:433
  9.4 4.9 %collective-permute-start.3 = (f32[136,128]{1,0:T(8,128)S(1)}, f32[136,128]{1,0:T(8,128)S(1)}, u32[]{:S(2)}, u32[]{:S(2)}) collective-permute-start(f32[136,128]{1,0:T(8,128)S(1)} %shard_map.67), channel_id=1, source_target_pairs={{0,2},{1,3},{2,0},{3,1},{4,6},{5,7},{6,4},{7,5},{8,10},{9,11},{10,... | collective-permute-start | bytes 208904 | tf_op jit(solution)/shard_map/ppermute | solution.py:433
  10.1 4.5 %collective-permute-start.4 = (f32[136,128]{1,0:T(8,128)S(1)}, f32[136,128]{1,0:T(8,128)S(1)}, u32[]{:S(2)}, u32[]{:S(2)}) collective-permute-start(f32[136,128]{1,0:T(8,128)S(1)} %shard_map.67), channel_id=1, source_target_pairs={{0,5},{1,4},{2,7},{3,6},{4,1},{5,0},{6,3},{7,2},{8,13},{9,12},{10,... | collective-permute-start | bytes 208904 | tf_op jit(solution)/shard_map/ppermute | solution.py:433
  13.5 2.5 %collective-permute-start.5 = (f32[272,128]{1,0:T(8,128)S(1)}, f32[272,128]{1,0:T(8,128)S(1)}, u32[]{:S(2)}, u32[]{:S(2)}) collective-permute-start(f32[272,128]{1,0:T(8,128)S(1)} %pad_maximum_fusion.2), channel_id=1, source_target_pairs={{0,1},{1,0},{2,3},{3,2},{4,5},{5,4},{6,7},{7,6},{8,9},{9,8},{10,11... | collective-permute-start | bytes 417800 | tf_op jit(solution)/shard_map/ppermute | solution.py:433
  14.3 1.3 %collective-permute-start.6 = (f32[136,128]{1,0:T(8,128)S(1)}, f32[136,128]{1,0:T(8,128)S(1)}, u32[]{:S(2)}, u32[]{:S(2)}) collective-permute-start(f32[136,128]{1,0:T(8,128)S(1)} %collective-permute-done.3), channel_id=1, source_target_pairs={{0,1},{1,0},{2,3},{3,2},{4,5},{5,4},{6,7},{7,6},{8,9},{9,8},{10,11... | collective-permute-start | bytes 208904 | tf_op jit(solution)/shard_map/ppermute | solution.py:433
  14.6 1.4 %collective-permute-start.7 = (f32[136,128]{1,0:T(8,128)S(1)}, f32[136,128]{1,0:T(8,128)S(1)}, u32[]{:S(2)}, u32[]{:S(2)}) collective-permute-start(f32[136,128]{1,0:T(8,128)S(1)} %collective-permute-done.4), channel_id=1, source_target_pairs={{0,1},{1,0},{2,3},{3,2},{4,5},{5,4},{6,7},{7,6},{8,9},{9,8},{10,11... | collective-permute-start | bytes 208904 | tf_op jit(solution)/shard_map/ppermute | solution.py:433

commit v5 on v4

--- a/solution.py
+++ b/solution.py
@@ -103,19 +103,23 @@
     return lax.broadcasted_iota(jnp.int32, shape, 1)
 
 
-def edge_kernel(start, wind_start, u_ref, z_ref):
+def edge_kernel(column, u_ref, z_ref):
     members, rows, _ = u_ref.shape
     members = members - 1
-    lane = lane_of((rows, LANES))
-    place = lane % STRIP
-    column = 0 if start > STRIP // 2 else LANES - SUBSTEPS
-    total = jnp.zeros((rows, LANES), jnp.float32)
+    lane = lane_of((8, LANES))
+    total = jnp.zeros((8, LANES), jnp.float32)
     for m in range(members):
-        for x, to in ((u_ref[m], start), (u_ref[members], wind_start)):
-            moved = pltpu.roll(x, (STRIP * m + to - column) % LANES, 1)
-            keep = (lane // STRIP == m) & (place >= to) & (place < to + SUBSTEPS)
-            total = jnp.where(keep, moved, total)
+        for g in range(rows // 8):
+            for x, to in ((u_ref[m], 0), (u_ref[members], SUBSTEPS)):
+                to = STRIP * m + 2 * SUBSTEPS * g + to
+                moved = pltpu.roll(x[8 * g : 8 * g + 8], (to - column) % LANES, 1)
+                total = jnp.where((lane >= to) & (lane < to + SUBSTEPS), moved, total)
     z_ref[...] = total
+
+
+def unfolded(packet, rows, to):
+    parts = [shifted(packet, 2 * SUBSTEPS * g - to) for g in range(rows // 8)]
+    return jnp.concatenate(parts, axis=0)
 
 
 def strips(block):
@@ -205,15 +209,14 @@
     rows = q_ref.shape[0] // 2
     lane = lane_of((rows, LANES))
     place = lane % STRIP
-    west, east = west_ref[...], east_ref[...]
     full = []
     for k in range(2):
         own = q_ref[k * rows : (k + 1) * rows, :]
+        west = unfolded(west_ref[...], rows, -SUBSTEPS * k)
+        east = unfolded(east_ref[...], rows, STRIP - SUBSTEPS - SUBSTEPS * k)
         full.append(
             jnp.where(place < SUBSTEPS, west, jnp.where(place >= STRIP - SUBSTEPS, east, own))
         )
-        west = pltpu.roll(west, LANES - SUBSTEPS, 1)
-        east = pltpu.roll(east, SUBSTEPS, 1)
     x, wind3 = full[0], 0.3 * full[1]
     x = substeps(x, wind3, SUBSTEPS)
     mem_here = LANES // STRIP
@@ -317,12 +320,11 @@
 
     def weights(x):
         high, low = (jnp.concatenate([part] * per, axis=0) * diag for part in split(x))
-        top = jnp.concatenate([high, low], axis=1)
-        return jnp.concatenate([top, jnp.concatenate([high, jnp.zeros_like(high)], axis=1)], axis=0)
+        return jnp.concatenate([high, high], axis=0), low
 
     def product(x, right):
-        out = dot(jnp.concatenate(split(x), axis=1), right, plain)
-        return out[:, :LANES] + out[:, LANES:]
+        xh, xl = split(x)
+        return dot(jnp.concatenate([xh, xl], axis=1), right[0], plain) + dot(xh, right[1], plain)
 
     twice = []
     for t in sets:
@@ -418,10 +420,8 @@
     both = jnp.concatenate([prior_ensemble, wind[None]], axis=0)
     forward = [(i, (i + 1) % count) for i in range(count)]
     backward = [(i, (i - 1) % count) for i in range(count)]
-    eastern = kernel_call(functools.partial(edge_kernel, 0, SUBSTEPS), (rows, LANES))(both)
-    western = kernel_call(
-        functools.partial(edge_kernel, STRIP - SUBSTEPS, STRIP - 2 * SUBSTEPS), (rows, LANES)
-    )(both)
+    eastern = kernel_call(functools.partial(edge_kernel, LANES - SUBSTEPS), (8, LANES))(both)
+    western = kernel_call(functools.partial(edge_kernel, 0), (8, LANES))(both)
     east = lax.ppermute(western, "space", backward)
     west = lax.ppermute(eastern, "space", forward)
     inside, near = kernel_call(interior_kernel, (mem_here * stride, LANES), (2 * rows, LANES))(
@@ -464,6 +464,7 @@
         and rows % groups == 0
         and 2 * (rows // groups) % mem_here == 0
         and rows % 8 == 0
+        and rows * 2 * SUBSTEPS <= 8 * STRIP
         and groups & (groups - 1) == 0
         and groups in (8, 16)
         and LANES % (mem_here * groups) == 0

time: 19.2 us -> 19 us (0.990)
  no operation moved by 1% of the time
where the time goes in v5:
time: 19 us; the launch traced here: 18.8 us
  starting transfers between devices  9.12 us (48%)
  waiting for transfers between devices  4.13 us (22%)
  Pallas kernels  3.85 us (20%)
  other arithmetic  0.91 us (5%)
  between operations  0.73 us (4%)
    ppermute x6, starting transfers between devices, swap(): return lax.ppermute(x, 'member', [(i, i ^ k) for i in range(groups)])  3.93 us
    pallas_call x5, Pallas kernels, call(): pl.pallas_call(body, out_shape=[jax.ShapeDtypeStruct(shape, jnp.float32)...  3.85 us
    ppermute x6, waiting for transfers between devices, swap(): return lax.ppermute(x, 'member', [(i, i ^ k) for i in range(groups)])  3.7 us
    ppermute x1, starting transfers between devices, gathered(): west = lax.ppermute(eastern, 'space', forward)  3.08 us
    ppermute x1, starting transfers between devices, gathered(): east = lax.ppermute(western, 'space', backward)  2.11 us
    concatenate x1, other arithmetic, gathered(): both = jnp.concatenate([prior_ensemble, wind[None]], axis=0)  0.86 us
  transfers between devices with their start and end apart: 8, of which 6 were waited for; matrix products, arithmetic and copies ran while one was open for 0% of the time, Pallas kernels for 3%

profile of v5, /device:TPU:0, one launch (start us, length us, event | category | flops | bytes accessed | tf_op | source)
XLA Modules:
  0.0 18.8 jit_solution(6849710960121373340)
XLA Ops:
  0.0 0.9 %pad_maximum_fusion.3.u_ref = f32[5,32,128]{2,1,0:T(8,128)S(1)} fusion(f32[1,32,128]{2,1,0:T(8,128)} %bitcast.5, f32[4,32,128]{2,1,0:T(8,128)} %param.6), kind=kLoop, calls=%fused_computation.3 | loop fusion | flops 20480 | bytes 163840 | tf_op jit(solution)/shard_map/concatenate | solution.py:420
  0.9 0.1 shard_map.65
  1.0 3.1 %collective-permute-start = (f32[8,128]{1,0:T(8,128)S(1)}, f32[8,128]{1,0:T(8,128)S(1)}, u32[]{:S(2)}, u32[]{:S(2)}) collective-permute-start(f32[8,128]{1,0:T(8,128)S(1)} %shard_map.65), channel_id=1, source_target_pairs={{0,8},{8,16},{16,24},{24,0},{1,9},{9,17},{17,25},{25,1},{2,10},{10... | collective-permute-start | bytes 12296 | tf_op jit(solution)/shard_map/ppermute | solution.py:426
  4.0 0.0 copy-start.1
  4.0 0.0 copy-start.2
  4.1 0.1 shard_map.66
  4.2 0.0 copy-start
  4.2 2.1 %collective-permute-start.1 = (f32[8,128]{1,0:T(8,128)S(1)}, f32[8,128]{1,0:T(8,128)S(1)}, u32[]{:S(2)}, u32[]{:S(2)}) collective-permute-start(f32[8,128]{1,0:T(8,128)S(1)} %shard_map.66), channel_id=1, source_target_pairs={{0,24},{8,0},{16,8},{24,16},{1,25},{9,1},{17,9},{25,17},{2,26},{10... | collective-permute-start | bytes 12296 | tf_op jit(solution)/shard_map/ppermute | solution.py:425
  6.9 0.0 copy-done.1
  6.9 0.0 copy-done.2
  7.0 0.0 copy-done
  7.0 0.4 %shard_map.64 = (f32[136,128]{1,0:T(8,128)S(1)}, f32[64,128]{1,0:T(8,128)S(1)}) custom-call(s32[1,1]{1,0:T(1,128)} %bitcast.4.count_ref, f32[5,32,128]{2,1,0:T(8,128)S(1)} %pad_maximum_fusion.3.u_ref, s32[1,512]{1,0:T(1,128)S(1)} %copy-done, f32[1,512]{1,0:T(1,128)S(1)} %copy-done.1, f32[1,512]{1,0:T(1,128)S(1)} %copy-done.2), custom_call_target="tpu_custom_call" | custom-call | tf_op jit(solution)/shard_map/pallas_call | solution.py:397
  7.4 0.3 %collective-permute-done.west_ref = f32[8,128]{1,0:T(8,128)S(1)} collective-permute-done((f32[8,128]{1,0:T(8,128)S(1)}, f32[8,128]{1,0:T(8,128)S(1)}, u32[]{:S(2)}, u32[]{:S(2)}) %collective-permute-start) | collective-permute-done | bytes 4128 | tf_op jit(solution)/shard_map/ppermute | solution.py:426
  7.7 0.2 collective-permute-done.1.east_ref
  7.8 0.4 %shard_map.67 = f32[136,128]{1,0:T(8,128)S(1)} custom-call(f32[64,128]{1,0:T(8,128)S(1)} %get-tuple-element.7.q_ref, f32[8,128]{1,0:T(8,128)S(1)} %collective-permute-done.west_ref, f32[8,128]{1,0:T(8,128)S(1)} %collective-permute-done.1.east_ref, f32[136,128]{1,0:T(8,128)S(1)} %get-tuple-element.8.f_in_ref), custom_call_target="tpu_custom_call" | custom-call | tf_op jit(solution)/shard_map/pallas_call | solution.py:397
  8.2 1.3 %collective-permute-start.2 = (f32[136,128]{1,0:T(8,128)S(1)}, f32[136,128]{1,0:T(8,128)S(1)}, u32[]{:S(2)}, u32[]{:S(2)}) collective-permute-start(f32[136,128]{1,0:T(8,128)S(1)} %shard_map.67), channel_id=1, source_target_pairs={{0,7},{1,6},{2,5},{3,4},{4,3},{5,2},{6,1},{7,0},{8,15},{9,14},{10,... | collective-permute-start | bytes 208904 | tf_op jit(solution)/shard_map/ppermute | solution.py:433
  9.5 0.5 %collective-permute-start.3 = (f32[136,128]{1,0:T(8,128)S(1)}, f32[136,128]{1,0:T(8,128)S(1)}, u32[]{:S(2)}, u32[]{:S(2)}) collective-permute-start(f32[136,128]{1,0:T(8,128)S(1)} %shard_map.67), channel_id=1, source_target_pairs={{0,2},{1,3},{2,0},{3,1},{4,6},{5,7},{6,4},{7,5},{8,10},{9,11},{10,... | collective-permute-start | bytes 208904 | tf_op jit(solution)/shard_map/ppermute | solution.py:433
  10.0 1.2 %collective-permute-start.4 = (f32[136,128]{1,0:T(8,128)S(1)}, f32[136,128]{1,0:T(8,128)S(1)}, u32[]{:S(2)}, u32[]{:S(2)}) collective-permute-start(f32[136,128]{1,0:T(8,128)S(1)} %shard_map.67), channel_id=1, source_target_pairs={{0,5},{1,4},{2,7},{3,6},{4,1},{5,0},{6,3},{7,2},{8,13},{9,12},{10,... | collective-permute-start | bytes 208904 | tf_op jit(solution)/shard_map/ppermute | solution.py:433
  11.2 2.3 %collective-permute-done.2 = f32[136,128]{1,0:T(8,128)S(1)} collective-permute-done((f32[136,128]{1,0:T(8,128)S(1)}, f32[136,128]{1,0:T(8,128)S(1)}, u32[]{:S(2)}, u32[]{:S(2)}) %collective-permute-start.2) | collective-permute-done | bytes 69664 | tf_op jit(solution)/shard_map/ppermute | solution.py:433
  13.6 0.1 collective-permute-start.5
  13.7 0.5 %collective-permute-done.3 = f32[136,128]{1,0:T(8,128)S(1)} collective-permute-done((f32[136,128]{1,0:T(8,128)S(1)}, f32[136,128]{1,0:T(8,128)S(1)}, u32[]{:S(2)}, u32[]{:S(2)}) %collective-permute-start.3) | collective-permute-done | bytes 69664 | tf_op jit(solution)/shard_map/ppermute | solution.py:433
  14.2 0.4 %collective-permute-start.6 = (f32[136,128]{1,0:T(8,128)S(1)}, f32[136,128]{1,0:T(8,128)S(1)}, u32[]{:S(2)}, u32[]{:S(2)}) collective-permute-start(f32[136,128]{1,0:T(8,128)S(1)} %collective-permute-done.3), channel_id=1, source_target_pairs={{0,1},{1,0},{2,3},{3,2},{4,5},{5,4},{6,7},{7,6},{8,9},{9,8},{10,11... | collective-permute-start | bytes 208904 | tf_op jit(solution)/shard_map/ppermute | solution.py:433
  14.6 0.0 collective-permute-done.4
  14.6 0.4 %collective-permute-start.7 = (f32[136,128]{1,0:T(8,128)S(1)}, f32[136,128]{1,0:T(8,128)S(1)}, u32[]{:S(2)}, u32[]{:S(2)}) collective-permute-start(f32[136,128]{1,0:T(8,128)S(1)} %collective-permute-done.4), channel_id=1, source_target_pairs={{0,1},{1,0},{2,3},{3,2},{4,5},{5,4},{6,7},{7,6},{8,9},{9,8},{10,11... | collective-permute-start | bytes 208904 | tf_op jit(solution)/shard_map/ppermute | solution.py:433
  15.0 0.5 %collective-permute-done.6 = f32[136,128]{1,0:T(8,128)S(1)} collective-permute-done((f32[136,128]{1,0:T(8,128)S(1)}, f32[136,128]{1,0:T(8,128)S(1)}, u32[]{:S(2)}, u32[]{:S(2)}) %collective-permute-start.6) | collective-permute-done | bytes 69664 | tf_op jit(solution)/shard_map/ppermute | solution.py:433
  15.5 0.4 %collective-permute-done.7 = f32[136,128]{1,0:T(8,128)S(1)} collective-permute-done((f32[136,128]{1,0:T(8,128)S(1)}, f32[136,128]{1,0:T(8,128)S(1)}, u32[]{:S(2)}, u32[]{:S(2)}) %collective-permute-start.7) | collective-permute-done | bytes 69664 | tf_op jit(solution)/shard_map/ppermute | solution.py:433
  15.9 0.0 collective-permute-done.5
  15.9 2.8 %shard_map.68 = f32[128,128]{1,0:T(8,128)} custom-call(s32[1]{0:T(128)} %bitcast.me_ref, f32[544,128]{1,0:T(8,128)S(1)} %pad_maximum_fusion.cat_ref, f32[544,128]{1,0:T(8,128)S(1)} %pad_maximum_fusion.1.sib_ref), custom_call_target="tpu_custom_call" | custom-call | tf_op jit(solution)/shard_map/pallas_call | solution.py:397
  (3 shorter events, 0.0 us)
Async XLA Ops:
  1.0 6.7 %collective-permute-start = (f32[8,128]{1,0:T(8,128)S(1)}, f32[8,128]{1,0:T(8,128)S(1)}, u32[]{:S(2)}, u32[]{:S(2)}) collective-permute-start(f32[8,128]{1,0:T(8,128)S(1)} %shard_map.65), channel_id=1, source_target_pairs={{0,8},{8,16},{16,24},{24,0},{1,9},{9,17},{17,25},{25,1},{2,10},{10... | collective-permute-start | bytes 12296 | tf_op jit(solution)/shard_map/ppermute | solution.py:426
  4.0 2.9 %copy-start.1 = (f32[1,512]{1,0:T(1,128)S(1)}, f32[1,512]{1,0:T(1,128)}, u32[]{:S(2)}) copy-start(f32[1,512]{1,0:T(1,128)} %value_ref.1) | copy-start | bytes 6148
  4.0 2.9 %copy-start.2 = (f32[1,512]{1,0:T(1,128)S(1)}, f32[1,512]{1,0:T(1,128)}, u32[]{:S(2)}) copy-start(f32[1,512]{1,0:T(1,128)} %weight_ref.1) | copy-start | bytes 6148
  4.2 2.8 %copy-start = (s32[1,512]{1,0:T(1,128)S(1)}, s32[1,512]{1,0:T(1,128)}, u32[]{:S(2)}) copy-start(s32[1,512]{1,0:T(1,128)} %cell_ref.1) | copy-start | bytes 6148
  4.2 3.7 %collective-permute-start.1 = (f32[8,128]{1,0:T(8,128)S(1)}, f32[8,128]{1,0:T(8,128)S(1)}, u32[]{:S(2)}, u32[]{:S(2)}) collective-permute-start(f32[8,128]{1,0:T(8,128)S(1)} %shard_map.66), channel_id=1, source_target_pairs={{0,24},{8,0},{16,8},{24,16},{1,25},{9,1},{17,9},{25,17},{2,26},{10... | collective-permute-start | bytes 12296 | tf_op jit(solution)/shard_map/ppermute | solution.py:425
  8.2 5.3 %collective-permute-start.2 = (f32[136,128]{1,0:T(8,128)S(1)}, f32[136,128]{1,0:T(8,128)S(1)}, u32[]{:S(2)}, u32[]{:S(2)}) collective-permute-start(f32[136,128]{1,0:T(8,128)S(1)} %shard_map.67), channel_id=1, source_target_pairs={{0,7},{1,6},{2,5},{3,4},{4,3},{5,2},{6,1},{7,0},{8,15},{9,14},{10,... | collective-permute-start | bytes 208904 | tf_op jit(solution)/shard_map/ppermute | solution.py:433
  9.5 4.7 %collective-permute-start.3 = (f32[136,128]{1,0:T(8,128)S(1)}, f32[136,128]{1,0:T(8,128)S(1)}, u32[]{:S(2)}, u32[]{:S(2)}) collective-permute-start(f32[136,128]{1,0:T(8,128)S(1)} %shard_map.67), channel_id=1, source_target_pairs={{0,2},{1,3},{2,0},{3,1},{4,6},{5,7},{6,4},{7,5},{8,10},{9,11},{10,... | collective-permute-start | bytes 208904 | tf_op jit(solution)/shard_map/ppermute | solution.py:433
  10.0 4.6 %collective-permute-start.4 = (f32[136,128]{1,0:T(8,128)S(1)}, f32[136,128]{1,0:T(8,128)S(1)}, u32[]{:S(2)}, u32[]{:S(2)}) collective-permute-start(f32[136,128]{1,0:T(8,128)S(1)} %shard_map.67), channel_id=1, source_target_pairs={{0,5},{1,4},{2,7},{3,6},{4,1},{5,0},{6,3},{7,2},{8,13},{9,12},{10,... | collective-permute-start | bytes 208904 | tf_op jit(solution)/shard_map/ppermute | solution.py:433
  13.6 2.3 %collective-permute-start.5 = (f32[272,128]{1,0:T(8,128)S(1)}, f32[272,128]{1,0:T(8,128)S(1)}, u32[]{:S(2)}, u32[]{:S(2)}) collective-permute-start(f32[272,128]{1,0:T(8,128)S(1)} %pad_maximum_fusion.2), channel_id=1, source_target_pairs={{0,1},{1,0},{2,3},{3,2},{4,5},{5,4},{6,7},{7,6},{8,9},{9,8},{10,11... | collective-permute-start | bytes 417800 | tf_op jit(solution)/shard_map/ppermute | solution.py:433
  14.2 1.3 %collective-permute-start.6 = (f32[136,128]{1,0:T(8,128)S(1)}, f32[136,128]{1,0:T(8,128)S(1)}, u32[]{:S(2)}, u32[]{:S(2)}) collective-permute-start(f32[136,128]{1,0:T(8,128)S(1)} %collective-permute-done.3), channel_id=1, source_target_pairs={{0,1},{1,0},{2,3},{3,2},{4,5},{5,4},{6,7},{7,6},{8,9},{9,8},{10,11... | collective-permute-start | bytes 208904 | tf_op jit(solution)/shard_map/ppermute | solution.py:433
  14.6 1.3 %collective-permute-start.7 = (f32[136,128]{1,0:T(8,128)S(1)}, f32[136,128]{1,0:T(8,128)S(1)}, u32[]{:S(2)}, u32[]{:S(2)}) collective-permute-start(f32[136,128]{1,0:T(8,128)S(1)} %collective-permute-done.4), channel_id=1, source_target_pairs={{0,1},{1,0},{2,3},{3,2},{4,5},{5,4},{6,7},{7,6},{8,9},{9,8},{10,11... | collective-permute-start | bytes 208904 | tf_op jit(solution)/shard_map/ppermute | solution.py:433

commit v6 on v5

--- a/solution.py
+++ b/solution.py
@@ -103,18 +103,34 @@
     return lax.broadcasted_iota(jnp.int32, shape, 1)
 
 
-def edge_kernel(column, u_ref, z_ref):
+def packet(u_ref, column):
     members, rows, _ = u_ref.shape
     members = members - 1
     lane = lane_of((8, LANES))
-    total = jnp.zeros((8, LANES), jnp.float32)
+    parts = []
     for m in range(members):
         for g in range(rows // 8):
             for x, to in ((u_ref[m], 0), (u_ref[members], SUBSTEPS)):
                 to = STRIP * m + 2 * SUBSTEPS * g + to
                 moved = pltpu.roll(x[8 * g : 8 * g + 8], (to - column) % LANES, 1)
-                total = jnp.where((lane >= to) & (lane < to + SUBSTEPS), moved, total)
-    z_ref[...] = total
+                parts.append(jnp.where((lane >= to) & (lane < to + SUBSTEPS), moved, 0.0))
+    while len(parts) > 1:
+        parts = [sum(parts[i : i + 2]) for i in range(0, len(parts), 2)]
+    return parts[0]
+
+
+def packets_kernel(u_hbm, wind_hbm, *refs):
+    obs_hbm, (east_ref, west_ref, u_ref), obs_ref, sems = refs[:3], refs[3:6], refs[6:9], refs[9]
+    members = u_hbm.shape[0]
+    pairs = [(u_hbm.at[m], u_ref.at[m]) for m in range(members)]
+    pairs += [(wind_hbm, u_ref.at[members]), *zip(obs_hbm, obs_ref)]
+    copies = [pltpu.make_async_copy(a, b, sems.at[i]) for i, (a, b) in enumerate(pairs)]
+    for copy in copies:
+        copy.start()
+    for copy in copies:
+        copy.wait()
+    east_ref[...] = packet(u_ref, LANES - SUBSTEPS)
+    west_ref[...] = packet(u_ref, 0)
 
 
 def unfolded(packet, rows, to):
@@ -218,7 +234,8 @@
             jnp.where(place < SUBSTEPS, west, jnp.where(place >= STRIP - SUBSTEPS, east, own))
         )
     x, wind3 = full[0], 0.3 * full[1]
-    x = substeps(x, wind3, SUBSTEPS)
+    for _ in range(2):
+        x = substeps(x, wind3, SUBSTEPS // 2)
     mem_here = LANES // STRIP
     stride = f_ref.shape[0] // mem_here
     for m in range(mem_here):
@@ -388,15 +405,26 @@
         copy.wait()
 
 
-def kernel_call(body, *out_shapes, scratch=(), smem=(), out_space=pltpu.VMEM):
+def typed(shape):
+    shape, dtype = shape if isinstance(shape[0], tuple) else (shape, jnp.float32)
+    return jax.ShapeDtypeStruct(shape, dtype)
+
+
+def kernel_call(body, *out_shapes, scratch=(), smem=(), far=(), out_space=pltpu.VMEM):
     def call(*args):
+        args = [
+            pltpu.with_memory_space_constraint(x, pltpu.HBM) if i in far else x
+            for i, x in enumerate(args)
+        ]
         specs = [
-            pl.BlockSpec(memory_space=pltpu.SMEM if i in smem else pltpu.VMEM)
+            pl.BlockSpec(
+                memory_space=pltpu.SMEM if i in smem else pl.ANY if i in far else pltpu.VMEM
+            )
             for i in range(len(args))
         ]
         out = pl.pallas_call(
             body,
-            out_shape=[jax.ShapeDtypeStruct(shape, jnp.float32) for shape in out_shapes],
+            out_shape=[typed(shape) for shape in out_shapes],
             in_specs=specs,
             out_specs=[pl.BlockSpec(memory_space=out_space) for _ in out_shapes],
             scratch_shapes=list(scratch),
@@ -417,15 +445,22 @@
     wide, cells = order * groups, height * LANES
     f32 = jnp.float32
 
-    both = jnp.concatenate([prior_ensemble, wind[None]], axis=0)
     forward = [(i, (i + 1) % count) for i in range(count)]
     backward = [(i, (i - 1) % count) for i in range(count)]
-    eastern = kernel_call(functools.partial(edge_kernel, LANES - SUBSTEPS), (8, LANES))(both)
-    western = kernel_call(functools.partial(edge_kernel, 0), (8, LANES))(both)
+    observed = (observed_cell_value, obs_value, obs_weight)
+    eastern, western, both, *observed = kernel_call(
+        packets_kernel,
+        (8, LANES),
+        (8, LANES),
+        (mem_here + 1, rows, LANES),
+        *[(x.shape, x.dtype) for x in observed],
+        scratch=[pltpu.SemaphoreType.DMA((mem_here + 1 + len(observed),))],
+        far=range(5),
+    )(prior_ensemble, wind, *observed)
     east = lax.ppermute(western, "space", backward)
     west = lax.ppermute(eastern, "space", forward)
     inside, near = kernel_call(interior_kernel, (mem_here * stride, LANES), (2 * rows, LANES))(
-        obs_count.reshape(1, 1), both, observed_cell_value, obs_value, obs_weight
+        obs_count.reshape(1, 1), both, *observed
     )
     payload = kernel_call(edges_kernel, (mem_here * stride, LANES))(near, west, east, inside)
 

time: 19 us -> 19 us (level)
  other arithmetic: 0.91 us -> 0.05 us
  Pallas kernels: 3.85 us -> 4.63 us
    concatenate x1 -> x0, other arithmetic: 0.86 us -> none  [gathered(): both = jnp.concatenate([prior_ensemble, wind[None]], axis=0)]
    pallas_call x5 -> x4, Pallas kernels: 3.85 us -> 4.63 us  [call(): pl.pallas_call(body, out_shape=[typed(shape) for shape in out_shapes], in...]
    ppermute x1, waiting for transfers between devices: 0.26 us -> 0.47 us  [gathered(): west = lax.ppermute(eastern, 'space', forward)]
  transfers between devices with their start and end apart: 8 -> 8, of which waited for: 6 -> 5; matrix products, arithmetic and copies ran while one was open for 0% -> 0% of each run, Pallas kernels for 3% -> 2%
where the time goes in v6:
time: 19 us; the launch traced here: 18.7 us
  starting transfers between devices  9.16 us (48%)
  Pallas kernels  4.63 us (24%)
  waiting for transfers between devices  4.15 us (22%)
  between operations  0.69 us (4%)
    pallas_call x4, Pallas kernels, call(): pl.pallas_call(body, out_shape=[typed(shape) for shape in out_shapes], in...  4.63 us
    ppermute x6, starting transfers between devices, swap(): return lax.ppermute(x, 'member', [(i, i ^ k) for i in range(groups)])  3.99 us
    ppermute x6, waiting for transfers between devices, swap(): return lax.ppermute(x, 'member', [(i, i ^ k) for i in range(groups)])  3.67 us
    ppermute x1, starting transfers between devices, gathered(): west = lax.ppermute(eastern, 'space', forward)  3.08 us
    ppermute x1, starting transfers between devices, gathered(): east = lax.ppermute(western, 'space', backward)  2.09 us
    ppermute x1, waiting for transfers between devices, gathered(): west = lax.ppermute(eastern, 'space', forward)  0.47 us
  transfers between devices with their start and end apart: 8, of which 5 were waited for; matrix products, arithmetic and copies ran while one was open for 0% of the time, Pallas kernels for 2%

profile of v6, /device:TPU:0, one launch (start us, length us, event | category | flops | bytes accessed | tf_op | source)
XLA Modules:
  0.0 18.7 jit_solution(12130721869391358369)
XLA Ops:
  0.0 1.0 %shard_map.64 = (f32[8,128]{1,0:T(8,128)S(1)}, f32[8,128]{1,0:T(8,128)S(1)}, f32[5,32,128]{2,1,0:T(8,128)S(1)}, s32[1,512]{1,0:T(1,128)S(1)}, f32[1,512]{1,0:T(1,128)S(1)}, /*index=5*/f32[1,512]{1,0:T(1,128)S(1)}) custom-call(f32[4,32,128]{2,1,0:T(8,128)} %u_hbm.1, f32[32,128]{1,0:T(8,128)} %wind_hbm.1, s32[1,512]{1,0:T(1,128)} %refs_0_.1, ...), custom_call_target="tpu_custom_call" | custom-call | tf_op jit(solution)/shard_map/pallas_call | solution.py:425
  1.0 3.1 %collective-permute-start = (f32[8,128]{1,0:T(8,128)S(1)}, f32[8,128]{1,0:T(8,128)S(1)}, u32[]{:S(2)}, u32[]{:S(2)}) collective-permute-start(f32[8,128]{1,0:T(8,128)S(1)} %get-tuple-element.18), channel_id=1, source_target_pairs={{0,8},{8,16},{16,24},{24,0},{1,9},{9,17},{17,25},{25,1},{2,10},{10... | collective-permute-start | bytes 12296 | tf_op jit(solution)/shard_map/ppermute | solution.py:461
  4.1 2.1 %collective-permute-start.1 = (f32[8,128]{1,0:T(8,128)S(1)}, f32[8,128]{1,0:T(8,128)S(1)}, u32[]{:S(2)}, u32[]{:S(2)}) collective-permute-start(f32[8,128]{1,0:T(8,128)S(1)} %get-tuple-element.19), channel_id=1, source_target_pairs={{0,24},{8,0},{16,8},{24,16},{1,25},{9,1},{17,9},{25,17},{2,26},{10... | collective-permute-start | bytes 12296 | tf_op jit(solution)/shard_map/ppermute | solution.py:460
  6.8 0.4 %shard_map.65 = (f32[136,128]{1,0:T(8,128)S(1)}, f32[64,128]{1,0:T(8,128)S(1)}) custom-call(s32[1,1]{1,0:T(1,128)} %bitcast.3.count_ref, f32[5,32,128]{2,1,0:T(8,128)S(1)} %get-tuple-element.13.u_ref, s32[1,512]{1,0:T(1,128)S(1)} %get-tuple-element.14.cell_ref, f32[1,512]{1,0:T(1,128)S(1)} %get-tuple-element.15.value_ref, ...), custom_call_target="tpu_custom_call" | custom-call | tf_op jit(solution)/shard_map/pallas_call | solution.py:425
  7.3 0.5 %collective-permute-done.west_ref = f32[8,128]{1,0:T(8,128)S(1)} collective-permute-done((f32[8,128]{1,0:T(8,128)S(1)}, f32[8,128]{1,0:T(8,128)S(1)}, u32[]{:S(2)}, u32[]{:S(2)}) %collective-permute-start) | collective-permute-done | bytes 4128 | tf_op jit(solution)/shard_map/ppermute | solution.py:461
  7.7 0.0 collective-permute-done.1.east_ref
  7.7 0.4 %shard_map.66 = f32[136,128]{1,0:T(8,128)S(1)} custom-call(f32[64,128]{1,0:T(8,128)S(1)} %get-tuple-element.17.q_ref, f32[8,128]{1,0:T(8,128)S(1)} %collective-permute-done.west_ref, f32[8,128]{1,0:T(8,128)S(1)} %collective-permute-done.1.east_ref, f32[136,128]{1,0:T(8,128)S(1)} %get-tuple-element.20.f_in_ref), custom_call_target="tpu_custom_call" | custom-call | tf_op jit(solution)/shard_map/pallas_call | solution.py:425
  8.1 1.2 %collective-permute-start.2 = (f32[136,128]{1,0:T(8,128)S(1)}, f32[136,128]{1,0:T(8,128)S(1)}, u32[]{:S(2)}, u32[]{:S(2)}) collective-permute-start(f32[136,128]{1,0:T(8,128)S(1)} %shard_map.66), channel_id=1, source_target_pairs={{0,7},{1,6},{2,5},{3,4},{4,3},{5,2},{6,1},{7,0},{8,15},{9,14},{10,... | collective-permute-start | bytes 208904 | tf_op jit(solution)/shard_map/ppermute | solution.py:468
  9.3 0.6 %collective-permute-start.3 = (f32[136,128]{1,0:T(8,128)S(1)}, f32[136,128]{1,0:T(8,128)S(1)}, u32[]{:S(2)}, u32[]{:S(2)}) collective-permute-start(f32[136,128]{1,0:T(8,128)S(1)} %shard_map.66), channel_id=1, source_target_pairs={{0,2},{1,3},{2,0},{3,1},{4,6},{5,7},{6,4},{7,5},{8,10},{9,11},{10,... | collective-permute-start | bytes 208904 | tf_op jit(solution)/shard_map/ppermute | solution.py:468
  9.9 1.2 %collective-permute-start.4 = (f32[136,128]{1,0:T(8,128)S(1)}, f32[136,128]{1,0:T(8,128)S(1)}, u32[]{:S(2)}, u32[]{:S(2)}) collective-permute-start(f32[136,128]{1,0:T(8,128)S(1)} %shard_map.66), channel_id=1, source_target_pairs={{0,5},{1,4},{2,7},{3,6},{4,1},{5,0},{6,3},{7,2},{8,13},{9,12},{10,... | collective-permute-start | bytes 208904 | tf_op jit(solution)/shard_map/ppermute | solution.py:468
  11.1 2.2 %collective-permute-done.2 = f32[136,128]{1,0:T(8,128)S(1)} collective-permute-done((f32[136,128]{1,0:T(8,128)S(1)}, f32[136,128]{1,0:T(8,128)S(1)}, u32[]{:S(2)}, u32[]{:S(2)}) %collective-permute-start.2) | collective-permute-done | bytes 69664 | tf_op jit(solution)/shard_map/ppermute | solution.py:468
  13.3 0.2 %collective-permute-start.5 = (f32[272,128]{1,0:T(8,128)S(1)}, f32[272,128]{1,0:T(8,128)S(1)}, u32[]{:S(2)}, u32[]{:S(2)}) collective-permute-start(f32[272,128]{1,0:T(8,128)S(1)} %pad_maximum_fusion.2), channel_id=1, source_target_pairs={{0,1},{1,0},{2,3},{3,2},{4,5},{5,4},{6,7},{7,6},{8,9},{9,8},{10,11... | collective-permute-start | bytes 417800 | tf_op jit(solution)/shard_map/ppermute | solution.py:468
  13.6 0.6 %collective-permute-done.3 = f32[136,128]{1,0:T(8,128)S(1)} collective-permute-done((f32[136,128]{1,0:T(8,128)S(1)}, f32[136,128]{1,0:T(8,128)S(1)}, u32[]{:S(2)}, u32[]{:S(2)}) %collective-permute-start.3) | collective-permute-done | bytes 69664 | tf_op jit(solution)/shard_map/ppermute | solution.py:468
  14.1 0.3 %collective-permute-start.6 = (f32[136,128]{1,0:T(8,128)S(1)}, f32[136,128]{1,0:T(8,128)S(1)}, u32[]{:S(2)}, u32[]{:S(2)}) collective-permute-start(f32[136,128]{1,0:T(8,128)S(1)} %collective-permute-done.3), channel_id=1, source_target_pairs={{0,1},{1,0},{2,3},{3,2},{4,5},{5,4},{6,7},{7,6},{8,9},{9,8},{10,11... | collective-permute-start | bytes 208904 | tf_op jit(solution)/shard_map/ppermute | solution.py:468
  14.4 0.0 collective-permute-done.4
  14.4 0.5 %collective-permute-start.7 = (f32[136,128]{1,0:T(8,128)S(1)}, f32[136,128]{1,0:T(8,128)S(1)}, u32[]{:S(2)}, u32[]{:S(2)}) collective-permute-start(f32[136,128]{1,0:T(8,128)S(1)} %collective-permute-done.4), channel_id=1, source_target_pairs={{0,1},{1,0},{2,3},{3,2},{4,5},{5,4},{6,7},{7,6},{8,9},{9,8},{10,11... | collective-permute-start | bytes 208904 | tf_op jit(solution)/shard_map/ppermute | solution.py:468
  14.9 0.5 %collective-permute-done.6 = f32[136,128]{1,0:T(8,128)S(1)} collective-permute-done((f32[136,128]{1,0:T(8,128)S(1)}, f32[136,128]{1,0:T(8,128)S(1)}, u32[]{:S(2)}, u32[]{:S(2)}) %collective-permute-start.6) | collective-permute-done | bytes 69664 | tf_op jit(solution)/shard_map/ppermute | solution.py:468
  15.4 0.4 %collective-permute-done.7 = f32[136,128]{1,0:T(8,128)S(1)} collective-permute-done((f32[136,128]{1,0:T(8,128)S(1)}, f32[136,128]{1,0:T(8,128)S(1)}, u32[]{:S(2)}, u32[]{:S(2)}) %collective-permute-start.7) | collective-permute-done | bytes 69664 | tf_op jit(solution)/shard_map/ppermute | solution.py:468
  15.8 0.0 collective-permute-done.5
  15.9 2.8 %shard_map.67 = f32[128,128]{1,0:T(8,128)} custom-call(s32[1]{0:T(128)} %bitcast.me_ref, f32[544,128]{1,0:T(8,128)S(1)} %pad_maximum_fusion.cat_ref, f32[544,128]{1,0:T(8,128)S(1)} %pad_maximum_fusion.1.sib_ref), custom_call_target="tpu_custom_call" | custom-call | tf_op jit(solution)/shard_map/pallas_call | solution.py:425
  (3 shorter events, 0.0 us)
Async XLA Ops:
  1.0 6.7 %collective-permute-start = (f32[8,128]{1,0:T(8,128)S(1)}, f32[8,128]{1,0:T(8,128)S(1)}, u32[]{:S(2)}, u32[]{:S(2)}) collective-permute-start(f32[8,128]{1,0:T(8,128)S(1)} %get-tuple-element.18), channel_id=1, source_target_pairs={{0,8},{8,16},{16,24},{24,0},{1,9},{9,17},{17,25},{25,1},{2,10},{10... | collective-permute-start | bytes 12296 | tf_op jit(solution)/shard_map/ppermute | solution.py:461
  4.1 3.7 %collective-permute-start.1 = (f32[8,128]{1,0:T(8,128)S(1)}, f32[8,128]{1,0:T(8,128)S(1)}, u32[]{:S(2)}, u32[]{:S(2)}) collective-permute-start(f32[8,128]{1,0:T(8,128)S(1)} %get-tuple-element.19), channel_id=1, source_target_pairs={{0,24},{8,0},{16,8},{24,16},{1,25},{9,1},{17,9},{25,17},{2,26},{10... | collective-permute-start | bytes 12296 | tf_op jit(solution)/shard_map/ppermute | solution.py:460
  8.1 5.2 %collective-permute-start.2 = (f32[136,128]{1,0:T(8,128)S(1)}, f32[136,128]{1,0:T(8,128)S(1)}, u32[]{:S(2)}, u32[]{:S(2)}) collective-permute-start(f32[136,128]{1,0:T(8,128)S(1)} %shard_map.66), channel_id=1, source_target_pairs={{0,7},{1,6},{2,5},{3,4},{4,3},{5,2},{6,1},{7,0},{8,15},{9,14},{10,... | collective-permute-start | bytes 208904 | tf_op jit(solution)/shard_map/ppermute | solution.py:468
  9.3 4.8 %collective-permute-start.3 = (f32[136,128]{1,0:T(8,128)S(1)}, f32[136,128]{1,0:T(8,128)S(1)}, u32[]{:S(2)}, u32[]{:S(2)}) collective-permute-start(f32[136,128]{1,0:T(8,128)S(1)} %shard_map.66), channel_id=1, source_target_pairs={{0,2},{1,3},{2,0},{3,1},{4,6},{5,7},{6,4},{7,5},{8,10},{9,11},{10,... | collective-permute-start | bytes 208904 | tf_op jit(solution)/shard_map/ppermute | solution.py:468
  9.9 4.5 %collective-permute-start.4 = (f32[136,128]{1,0:T(8,128)S(1)}, f32[136,128]{1,0:T(8,128)S(1)}, u32[]{:S(2)}, u32[]{:S(2)}) collective-permute-start(f32[136,128]{1,0:T(8,128)S(1)} %shard_map.66), channel_id=1, source_target_pairs={{0,5},{1,4},{2,7},{3,6},{4,1},{5,0},{6,3},{7,2},{8,13},{9,12},{10,... | collective-permute-start | bytes 208904 | tf_op jit(solution)/shard_map/ppermute | solution.py:468
  13.3 2.5 %collective-permute-start.5 = (f32[272,128]{1,0:T(8,128)S(1)}, f32[272,128]{1,0:T(8,128)S(1)}, u32[]{:S(2)}, u32[]{:S(2)}) collective-permute-start(f32[272,128]{1,0:T(8,128)S(1)} %pad_maximum_fusion.2), channel_id=1, source_target_pairs={{0,1},{1,0},{2,3},{3,2},{4,5},{5,4},{6,7},{7,6},{8,9},{9,8},{10,11... | collective-permute-start | bytes 417800 | tf_op jit(solution)/shard_map/ppermute | solution.py:468
  14.1 1.3 %collective-permute-start.6 = (f32[136,128]{1,0:T(8,128)S(1)}, f32[136,128]{1,0:T(8,128)S(1)}, u32[]{:S(2)}, u32[]{:S(2)}) collective-permute-start(f32[136,128]{1,0:T(8,128)S(1)} %collective-permute-done.3), channel_id=1, source_target_pairs={{0,1},{1,0},{2,3},{3,2},{4,5},{5,4},{6,7},{7,6},{8,9},{9,8},{10,11... | collective-permute-start | bytes 208904 | tf_op jit(solution)/shard_map/ppermute | solution.py:468
  14.4 1.4 %collective-permute-start.7 = (f32[136,128]{1,0:T(8,128)S(1)}, f32[136,128]{1,0:T(8,128)S(1)}, u32[]{:S(2)}, u32[]{:S(2)}) collective-permute-start(f32[136,128]{1,0:T(8,128)S(1)} %collective-permute-done.4), channel_id=1, source_target_pairs={{0,1},{1,0},{2,3},{3,2},{4,5},{5,4},{6,7},{7,6},{8,9},{9,8},{10,11... | collective-permute-start | bytes 208904 | tf_op jit(solution)/shard_map/ppermute | solution.py:468

commit v7 on v6

--- a/solution.py
+++ b/solution.py
@@ -103,17 +103,17 @@
     return lax.broadcasted_iota(jnp.int32, shape, 1)
 
 
-def packet(u_ref, column):
+def packet(u_ref, moved_wind, column):
     members, rows, _ = u_ref.shape
-    members = members - 1
     lane = lane_of((8, LANES))
+    beside = (lane - column) % LANES // SUBSTEPS == 1
     parts = []
-    for m in range(members):
+    for m in range(members - 1):
         for g in range(rows // 8):
-            for x, to in ((u_ref[m], 0), (u_ref[members], SUBSTEPS)):
-                to = STRIP * m + 2 * SUBSTEPS * g + to
-                moved = pltpu.roll(x[8 * g : 8 * g + 8], (to - column) % LANES, 1)
-                parts.append(jnp.where((lane >= to) & (lane < to + SUBSTEPS), moved, 0.0))
+            at, to = slice(8 * g, 8 * g + 8), STRIP * m + 2 * SUBSTEPS * g
+            both = jnp.where(beside, moved_wind[at], u_ref[m, at, :])
+            moved = pltpu.roll(both, (to - column) % LANES, 1)
+            parts.append(jnp.where(lane // (2 * SUBSTEPS) == to // (2 * SUBSTEPS), moved, 0.0))
     while len(parts) > 1:
         parts = [sum(parts[i : i + 2]) for i in range(0, len(parts), 2)]
     return parts[0]
@@ -122,15 +122,20 @@
 def packets_kernel(u_hbm, wind_hbm, *refs):
     obs_hbm, (east_ref, west_ref, u_ref), obs_ref, sems = refs[:3], refs[3:6], refs[6:9], refs[9]
     members = u_hbm.shape[0]
-    pairs = [(u_hbm.at[m], u_ref.at[m]) for m in range(members)]
-    pairs += [(wind_hbm, u_ref.at[members]), *zip(obs_hbm, obs_ref)]
+    pairs = [(wind_hbm, u_ref.at[members])]
+    pairs += [(u_hbm.at[m], u_ref.at[m]) for m in range(members)]
+    pairs += [*zip(obs_hbm, obs_ref)]
     copies = [pltpu.make_async_copy(a, b, sems.at[i]) for i, (a, b) in enumerate(pairs)]
     for copy in copies:
         copy.start()
-    for copy in copies:
+    copies[0].wait()
+    moved_wind = pltpu.roll(u_ref[members], SUBSTEPS, 1)
+    for copy in copies[1 : 1 + members]:
         copy.wait()
-    east_ref[...] = packet(u_ref, LANES - SUBSTEPS)
-    west_ref[...] = packet(u_ref, 0)
+    east_ref[...] = packet(u_ref, moved_wind, LANES - SUBSTEPS)
+    west_ref[...] = packet(u_ref, moved_wind, 0)
+    for copy in copies[1 + members :]:
+        copy.wait()
 
 
 def unfolded(packet, rows, to):
@@ -141,12 +146,12 @@
 def strips(block):
     lane = lane_of(block[0].shape)
     west = (lane % STRIP) < STRIP // 2
-    total = jnp.zeros(block[0].shape, jnp.float32)
+    parts = []
     for m, x in enumerate(block):
         low = pltpu.roll(x, (STRIP * m + SUBSTEPS) % LANES, 1)
         high = pltpu.roll(x, (STRIP * m + STRIP - SUBSTEPS) % LANES, 1)
-        total = jnp.where((lane // STRIP) == m, jnp.where(west, low, high), total)
-    return total
+        parts.append(jnp.where((lane // STRIP) == m, jnp.where(west, low, high), 0.0))
+    return sum(parts)
 
 
 def stencil(x, east, west, wind3):
@@ -192,7 +197,7 @@
     wind3 = 0.3 * u_ref[mem_here]
     slots = cell_ref.shape[1]
     slot = lax.broadcasted_iota(jnp.int32, (1, slots), 1)
-    weight = jnp.where(slot < count_ref[...], weight_ref[...], 0.0)
+    weight = jnp.where(slot < count_ref[0], weight_ref[...], 0.0)
     parts = pieces(weight, 3) + pieces(weight * value_ref[...], 3)
     sub = lax.broadcasted_iota(jnp.int32, (8, slots), 0)
     lhs = jnp.zeros((8, slots), jnp.float32)
@@ -214,10 +219,10 @@
             f_ref[at : at + 1, :] = line
     q_ref[0:rows, :] = strips([u_ref[m] for m in range(mem_here)])
     q_ref[rows : 2 * rows, :] = strips([u_ref[mem_here]] * mem_here)
-    for m in range(mem_here):
-        x = u_ref[m]
-        for _ in range(SUBSTEPS):
-            x = substep(x, wind3)
+    state = [u_ref[m] for m in range(mem_here)]
+    for _ in range(SUBSTEPS):
+        state = [substep(x, wind3) for x in state]
+    for m, x in enumerate(state):
         f_ref[m * stride : m * stride + rows, :] = x
 
 
@@ -459,9 +464,9 @@
     )(prior_ensemble, wind, *observed)
     east = lax.ppermute(western, "space", backward)
     west = lax.ppermute(eastern, "space", forward)
-    inside, near = kernel_call(interior_kernel, (mem_here * stride, LANES), (2 * rows, LANES))(
-        obs_count.reshape(1, 1), both, *observed
-    )
+    inside, near = kernel_call(
+        interior_kernel, (mem_here * stride, LANES), (2 * rows, LANES), smem=(0,)
+    )(obs_count, both, *observed)
     payload = kernel_call(edges_kernel, (mem_here * stride, LANES))(near, west, east, inside)
 
     def swap(x, k):

time: 19 us -> 18.9 us (level)
  no operation moved by 1% of the time
where the time goes in v7:
time: 18.9 us; the launch traced here: 18.7 us
  starting transfers between devices  9.16 us (48%)
  Pallas kernels  4.58 us (24%)
  waiting for transfers between devices  4.18 us (22%)
  between operations  0.7 us (4%)
    pallas_call x4, Pallas kernels, call(): pl.pallas_call(body, out_shape=[typed(shape) for shape in out_shapes], in...  4.58 us
    ppermute x6, starting transfers between devices, swap(): return lax.ppermute(x, 'member', [(i, i ^ k) for i in range(groups)])  4 us
    ppermute x6, waiting for transfers between devices, swap(): return lax.ppermute(x, 'member', [(i, i ^ k) for i in range(groups)])  3.67 us
    ppermute x1, starting transfers between devices, gathered(): west = lax.ppermute(eastern, 'space', forward)  3.08 us
    ppermute x1, starting transfers between devices, gathered(): east = lax.ppermute(western, 'space', backward)  2.09 us
    ppermute x1, waiting for transfers between devices, gathered(): west = lax.ppermute(eastern, 'space', forward)  0.5 us
  transfers between devices with their start and end apart: 8, of which 5 were waited for; matrix products, arithmetic and copies ran while one was open for 0% of the time, Pallas kernels for 2%

profile of v7, /device:TPU:0, one launch (start us, length us, event | category | flops | bytes accessed | tf_op | source)
XLA Modules:
  0.0 18.7 jit_solution(12056646637613845578)
XLA Ops:
  0.0 1.0 %shard_map.64 = (f32[8,128]{1,0:T(8,128)S(1)}, f32[8,128]{1,0:T(8,128)S(1)}, f32[5,32,128]{2,1,0:T(8,128)S(1)}, s32[1,512]{1,0:T(1,128)S(1)}, f32[1,512]{1,0:T(1,128)S(1)}, /*index=5*/f32[1,512]{1,0:T(1,128)S(1)}) custom-call(f32[4,32,128]{2,1,0:T(8,128)} %u_hbm.1, f32[32,128]{1,0:T(8,128)} %wind_hbm.1, s32[1,512]{1,0:T(1,128)} %refs_0_.1, ...), custom_call_target="tpu_custom_call" | custom-call | tf_op jit(solution)/shard_map/pallas_call | solution.py:430
  1.0 3.1 %collective-permute-start = (f32[8,128]{1,0:T(8,128)S(1)}, f32[8,128]{1,0:T(8,128)S(1)}, u32[]{:S(2)}, u32[]{:S(2)}) collective-permute-start(f32[8,128]{1,0:T(8,128)S(1)} %get-tuple-element.18), channel_id=1, source_target_pairs={{0,8},{8,16},{16,24},{24,0},{1,9},{9,17},{17,25},{25,1},{2,10},{10... | collective-permute-start | bytes 12296 | tf_op jit(solution)/shard_map/ppermute | solution.py:466
  4.1 2.1 %collective-permute-start.1 = (f32[8,128]{1,0:T(8,128)S(1)}, f32[8,128]{1,0:T(8,128)S(1)}, u32[]{:S(2)}, u32[]{:S(2)}) collective-permute-start(f32[8,128]{1,0:T(8,128)S(1)} %get-tuple-element.19), channel_id=1, source_target_pairs={{0,24},{8,0},{16,8},{24,16},{1,25},{9,1},{17,9},{25,17},{2,26},{10... | collective-permute-start | bytes 12296 | tf_op jit(solution)/shard_map/ppermute | solution.py:465
  6.8 0.4 %shard_map.65 = (f32[136,128]{1,0:T(8,128)S(1)}, f32[64,128]{1,0:T(8,128)S(1)}) custom-call(s32[1]{0:T(128)S(6)} %copy.7.count_ref, f32[5,32,128]{2,1,0:T(8,128)S(1)} %get-tuple-element.13.u_ref, s32[1,512]{1,0:T(1,128)S(1)} %get-tuple-element.14.cell_ref, f32[1,512]{1,0:T(1,128)S(1)} %get-tuple-element.15.value_ref, f32[1,512]{1,0:T(1,128)S(1)} %get-tuple-element.16.weight_ref), custom_call_target="tpu_custom_call" | custom-call | tf_op jit(solution)/shard_map/pallas_call | solution.py:430
  7.2 0.5 %collective-permute-done.west_ref = f32[8,128]{1,0:T(8,128)S(1)} collective-permute-done((f32[8,128]{1,0:T(8,128)S(1)}, f32[8,128]{1,0:T(8,128)S(1)}, u32[]{:S(2)}, u32[]{:S(2)}) %collective-permute-start) | collective-permute-done | bytes 4128 | tf_op jit(solution)/shard_map/ppermute | solution.py:466
  7.7 0.0 collective-permute-done.1.east_ref
  7.7 0.4 %shard_map.66 = f32[136,128]{1,0:T(8,128)S(1)} custom-call(f32[64,128]{1,0:T(8,128)S(1)} %get-tuple-element.17.q_ref, f32[8,128]{1,0:T(8,128)S(1)} %collective-permute-done.west_ref, f32[8,128]{1,0:T(8,128)S(1)} %collective-permute-done.1.east_ref, f32[136,128]{1,0:T(8,128)S(1)} %get-tuple-element.20.f_in_ref), custom_call_target="tpu_custom_call" | custom-call | tf_op jit(solution)/shard_map/pallas_call | solution.py:430
  8.1 1.2 %collective-permute-start.2 = (f32[136,128]{1,0:T(8,128)S(1)}, f32[136,128]{1,0:T(8,128)S(1)}, u32[]{:S(2)}, u32[]{:S(2)}) collective-permute-start(f32[136,128]{1,0:T(8,128)S(1)} %shard_map.66), channel_id=1, source_target_pairs={{0,7},{1,6},{2,5},{3,4},{4,3},{5,2},{6,1},{7,0},{8,15},{9,14},{10,... | collective-permute-start | bytes 208904 | tf_op jit(solution)/shard_map/ppermute | solution.py:473
  9.3 0.6 %collective-permute-start.3 = (f32[136,128]{1,0:T(8,128)S(1)}, f32[136,128]{1,0:T(8,128)S(1)}, u32[]{:S(2)}, u32[]{:S(2)}) collective-permute-start(f32[136,128]{1,0:T(8,128)S(1)} %shard_map.66), channel_id=1, source_target_pairs={{0,2},{1,3},{2,0},{3,1},{4,6},{5,7},{6,4},{7,5},{8,10},{9,11},{10,... | collective-permute-start | bytes 208904 | tf_op jit(solution)/shard_map/ppermute | solution.py:473
  9.9 1.2 %collective-permute-start.4 = (f32[136,128]{1,0:T(8,128)S(1)}, f32[136,128]{1,0:T(8,128)S(1)}, u32[]{:S(2)}, u32[]{:S(2)}) collective-permute-start(f32[136,128]{1,0:T(8,128)S(1)} %shard_map.66), channel_id=1, source_target_pairs={{0,5},{1,4},{2,7},{3,6},{4,1},{5,0},{6,3},{7,2},{8,13},{9,12},{10,... | collective-permute-start | bytes 208904 | tf_op jit(solution)/shard_map/ppermute | solution.py:473
  11.1 2.2 %collective-permute-done.2 = f32[136,128]{1,0:T(8,128)S(1)} collective-permute-done((f32[136,128]{1,0:T(8,128)S(1)}, f32[136,128]{1,0:T(8,128)S(1)}, u32[]{:S(2)}, u32[]{:S(2)}) %collective-permute-start.2) | collective-permute-done | bytes 69664 | tf_op jit(solution)/shard_map/ppermute | solution.py:473
  13.3 0.2 %collective-permute-start.5 = (f32[272,128]{1,0:T(8,128)S(1)}, f32[272,128]{1,0:T(8,128)S(1)}, u32[]{:S(2)}, u32[]{:S(2)}) collective-permute-start(f32[272,128]{1,0:T(8,128)S(1)} %pad_maximum_fusion.2), channel_id=1, source_target_pairs={{0,1},{1,0},{2,3},{3,2},{4,5},{5,4},{6,7},{7,6},{8,9},{9,8},{10,11... | collective-permute-start | bytes 417800 | tf_op jit(solution)/shard_map/ppermute | solution.py:473
  13.5 0.6 %collective-permute-done.3 = f32[136,128]{1,0:T(8,128)S(1)} collective-permute-done((f32[136,128]{1,0:T(8,128)S(1)}, f32[136,128]{1,0:T(8,128)S(1)}, u32[]{:S(2)}, u32[]{:S(2)}) %collective-permute-start.3) | collective-permute-done | bytes 69664 | tf_op jit(solution)/shard_map/ppermute | solution.py:473
  14.1 0.3 %collective-permute-start.6 = (f32[136,128]{1,0:T(8,128)S(1)}, f32[136,128]{1,0:T(8,128)S(1)}, u32[]{:S(2)}, u32[]{:S(2)}) collective-permute-start(f32[136,128]{1,0:T(8,128)S(1)} %collective-permute-done.3), channel_id=1, source_target_pairs={{0,1},{1,0},{2,3},{3,2},{4,5},{5,4},{6,7},{7,6},{8,9},{9,8},{10,11... | collective-permute-start | bytes 208904 | tf_op jit(solution)/shard_map/ppermute | solution.py:473
  14.4 0.0 collective-permute-done.4
  14.4 0.5 %collective-permute-start.7 = (f32[136,128]{1,0:T(8,128)S(1)}, f32[136,128]{1,0:T(8,128)S(1)}, u32[]{:S(2)}, u32[]{:S(2)}) collective-permute-start(f32[136,128]{1,0:T(8,128)S(1)} %collective-permute-done.4), channel_id=1, source_target_pairs={{0,1},{1,0},{2,3},{3,2},{4,5},{5,4},{6,7},{7,6},{8,9},{9,8},{10,11... | collective-permute-start | bytes 208904 | tf_op jit(solution)/shard_map/ppermute | solution.py:473
  14.9 0.5 %collective-permute-done.6 = f32[136,128]{1,0:T(8,128)S(1)} collective-permute-done((f32[136,128]{1,0:T(8,128)S(1)}, f32[136,128]{1,0:T(8,128)S(1)}, u32[]{:S(2)}, u32[]{:S(2)}) %collective-permute-start.6) | collective-permute-done | bytes 69664 | tf_op jit(solution)/shard_map/ppermute | solution.py:473
  15.4 0.4 %collective-permute-done.7 = f32[136,128]{1,0:T(8,128)S(1)} collective-permute-done((f32[136,128]{1,0:T(8,128)S(1)}, f32[136,128]{1,0:T(8,128)S(1)}, u32[]{:S(2)}, u32[]{:S(2)}) %collective-permute-start.7) | collective-permute-done | bytes 69664 | tf_op jit(solution)/shard_map/ppermute | solution.py:473
  15.8 0.0 collective-permute-done.5
  15.8 2.8 %shard_map.67 = f32[128,128]{1,0:T(8,128)} custom-call(s32[1]{0:T(128)} %bitcast.me_ref, f32[544,128]{1,0:T(8,128)S(1)} %pad_maximum_fusion.cat_ref, f32[544,128]{1,0:T(8,128)S(1)} %pad_maximum_fusion.1.sib_ref), custom_call_target="tpu_custom_call" | custom-call | tf_op jit(solution)/shard_map/pallas_call | solution.py:430
  (3 shorter events, 0.0 us)
Async XLA Ops:
  1.0 6.7 %collective-permute-start = (f32[8,128]{1,0:T(8,128)S(1)}, f32[8,128]{1,0:T(8,128)S(1)}, u32[]{:S(2)}, u32[]{:S(2)}) collective-permute-start(f32[8,128]{1,0:T(8,128)S(1)} %get-tuple-element.18), channel_id=1, source_target_pairs={{0,8},{8,16},{16,24},{24,0},{1,9},{9,17},{17,25},{25,1},{2,10},{10... | collective-permute-start | bytes 12296 | tf_op jit(solution)/shard_map/ppermute | solution.py:466
  4.1 3.7 %collective-permute-start.1 = (f32[8,128]{1,0:T(8,128)S(1)}, f32[8,128]{1,0:T(8,128)S(1)}, u32[]{:S(2)}, u32[]{:S(2)}) collective-permute-start(f32[8,128]{1,0:T(8,128)S(1)} %get-tuple-element.19), channel_id=1, source_target_pairs={{0,24},{8,0},{16,8},{24,16},{1,25},{9,1},{17,9},{25,17},{2,26},{10... | collective-permute-start | bytes 12296 | tf_op jit(solution)/shard_map/ppermute | solution.py:465
  8.1 5.2 %collective-permute-start.2 = (f32[136,128]{1,0:T(8,128)S(1)}, f32[136,128]{1,0:T(8,128)S(1)}, u32[]{:S(2)}, u32[]{:S(2)}) collective-permute-start(f32[136,128]{1,0:T(8,128)S(1)} %shard_map.66), channel_id=1, source_target_pairs={{0,7},{1,6},{2,5},{3,4},{4,3},{5,2},{6,1},{7,0},{8,15},{9,14},{10,... | collective-permute-start | bytes 208904 | tf_op jit(solution)/shard_map/ppermute | solution.py:473
  9.3 4.8 %collective-permute-start.3 = (f32[136,128]{1,0:T(8,128)S(1)}, f32[136,128]{1,0:T(8,128)S(1)}, u32[]{:S(2)}, u32[]{:S(2)}) collective-permute-start(f32[136,128]{1,0:T(8,128)S(1)} %shard_map.66), channel_id=1, source_target_pairs={{0,2},{1,3},{2,0},{3,1},{4,6},{5,7},{6,4},{7,5},{8,10},{9,11},{10,... | collective-permute-start | bytes 208904 | tf_op jit(solution)/shard_map/ppermute | solution.py:473
  9.9 4.5 %collective-permute-start.4 = (f32[136,128]{1,0:T(8,128)S(1)}, f32[136,128]{1,0:T(8,128)S(1)}, u32[]{:S(2)}, u32[]{:S(2)}) collective-permute-start(f32[136,128]{1,0:T(8,128)S(1)} %shard_map.66), channel_id=1, source_target_pairs={{0,5},{1,4},{2,7},{3,6},{4,1},{5,0},{6,3},{7,2},{8,13},{9,12},{10,... | collective-permute-start | bytes 208904 | tf_op jit(solution)/shard_map/ppermute | solution.py:473
  13.3 2.5 %collective-permute-start.5 = (f32[272,128]{1,0:T(8,128)S(1)}, f32[272,128]{1,0:T(8,128)S(1)}, u32[]{:S(2)}, u32[]{:S(2)}) collective-permute-start(f32[272,128]{1,0:T(8,128)S(1)} %pad_maximum_fusion.2), channel_id=1, source_target_pairs={{0,1},{1,0},{2,3},{3,2},{4,5},{5,4},{6,7},{7,6},{8,9},{9,8},{10,11... | collective-permute-start | bytes 417800 | tf_op jit(solution)/shard_map/ppermute | solution.py:473
  14.1 1.3 %collective-permute-start.6 = (f32[136,128]{1,0:T(8,128)S(1)}, f32[136,128]{1,0:T(8,128)S(1)}, u32[]{:S(2)}, u32[]{:S(2)}) collective-permute-start(f32[136,128]{1,0:T(8,128)S(1)} %collective-permute-done.3), channel_id=1, source_target_pairs={{0,1},{1,0},{2,3},{3,2},{4,5},{5,4},{6,7},{7,6},{8,9},{9,8},{10,11... | collective-permute-start | bytes 208904 | tf_op jit(solution)/shard_map/ppermute | solution.py:473
  14.4 1.4 %collective-permute-start.7 = (f32[136,128]{1,0:T(8,128)S(1)}, f32[136,128]{1,0:T(8,128)S(1)}, u32[]{:S(2)}, u32[]{:S(2)}) collective-permute-start(f32[136,128]{1,0:T(8,128)S(1)} %collective-permute-done.4), channel_id=1, source_target_pairs={{0,1},{1,0},{2,3},{3,2},{4,5},{5,4},{6,7},{7,6},{8,9},{9,8},{10,11... | collective-permute-start | bytes 208904 | tf_op jit(solution)/shard_map/ppermute | solution.py:473

commit v8 on v7

--- a/solution.py
+++ b/solution.py
@@ -256,8 +256,14 @@
 
 
 def visits(groups):
-    chips = [groups - 2, *range(2, groups - 2, 2)]
-    return [0, *[chip + (i + 1) % 2 for i, chip in enumerate(chips)]]
+    near = range(2, groups - 2, 2)
+    pairs = [(one + i % 2, two + i % 2) for i, (one, two) in enumerate(zip(near, reversed(near)))]
+    return [(groups - 1, groups - 1), *pairs]
+
+
+def sources(groups):
+    taken = [(odd, even) if even % 2 else (even, odd) for even, odd in visits(groups)]
+    return [(0, 0), *taken]
 
 
 def analysis_kernel(dims, me_ref, cat_ref, sib_ref, o_ref, ob_ref, pert_ref, scaled_ref, mean_ref, done_ref, sems):
@@ -282,7 +288,8 @@
 
     for side, ref in enumerate((cat_ref, sib_ref)):
         for k in range(groups // 2):
-            patch = me ^ (visits(groups)[k] ^ side)
+            source = sources(groups)[k]
+            patch = me ^ side ^ jnp.where(((me & 1) ^ side) == 0, source[0], source[1])
             base = k * mem_here * stride
             lines = [
                 ref[base + m * stride + rows : base + (m + 1) * stride, :] for m in range(mem_here)
@@ -472,7 +479,10 @@
     def swap(x, k):
         return lax.ppermute(x, "member", [(i, i ^ k) for i in range(groups)])
 
-    held = [payload] + [swap(payload, k) for k in visits(groups)[1:]]
+    held = [payload]
+    for visit in visits(groups):
+        move = [(i, i ^ visit[i % 2]) for i in range(groups)]
+        held.append(lax.ppermute(payload, "member", move))
     cat = jnp.concatenate(held, axis=0)
     first = jnp.concatenate(held[:2], axis=0)
     sibling = jnp.concatenate([swap(x, 1) for x in [first, *held[2:]]], axis=0)

time: 18.9 us -> 18.9 us (level)
  waiting for transfers between devices: 4.18 us -> 3.35 us
  starting transfers between devices: 9.16 us -> 9.98 us
    ppermute x0 -> x3, starting transfers between devices: none -> 4.16 us  [gathered(): held.append(lax.ppermute(payload, 'member', move))]
    ppermute x6 -> x3, starting transfers between devices: 4 us -> 0.65 us  [swap(): return lax.ppermute(x, 'member', [(i, i ^ k) for i in range(groups)])]
    ppermute x6 -> x3, waiting for transfers between devices: 3.67 us -> 0.9 us  [swap(): return lax.ppermute(x, 'member', [(i, i ^ k) for i in range(groups)])]
    ppermute x0 -> x3, waiting for transfers between devices: none -> 1.94 us  [gathered(): held.append(lax.ppermute(payload, 'member', move))]
  transfers between devices with their start and end apart: 8 -> 8, of which waited for: 5 -> 6; matrix products, arithmetic and copies ran while one was open for 0% -> 0% of each run, Pallas kernels for 2% -> 2%
where the time goes in v8:
time: 18.9 us; the launch traced here: 18.7 us
  starting transfers between devices  9.98 us (53%)
  Pallas kernels  4.59 us (24%)
  waiting for transfers between devices  3.35 us (18%)
  between operations  0.7 us (4%)
    pallas_call x4, Pallas kernels, call(): pl.pallas_call(body, out_shape=[typed(shape) for shape in out_shapes], in...  4.59 us
    ppermute x3, starting transfers between devices, gathered(): held.append(lax.ppermute(payload, 'member', move))  4.16 us
    ppermute x1, starting transfers between devices, gathered(): west = lax.ppermute(eastern, 'space', forward)  3.08 us
    ppermute x1, starting transfers between devices, gathered(): east = lax.ppermute(western, 'space', backward)  2.09 us
    ppermute x3, waiting for transfers between devices, gathered(): held.append(lax.ppermute(payload, 'member', move))  1.94 us
    ppermute x3, waiting for transfers between devices, swap(): return lax.ppermute(x, 'member', [(i, i ^ k) for i in range(groups)])  0.9 us
    ppermute x3, starting transfers between devices, swap(): return lax.ppermute(x, 'member', [(i, i ^ k) for i in range(groups)])  0.65 us
    ppermute x1, waiting for transfers between devices, gathered(): west = lax.ppermute(eastern, 'space', forward)  0.5 us
  transfers between devices with their start and end apart: 8, of which 6 were waited for; matrix products, arithmetic and copies ran while one was open for 0% of the time, Pallas kernels for 2%

profile of v8, /device:TPU:0, one launch (start us, length us, event | category | flops | bytes accessed | tf_op | source)
XLA Modules:
  0.0 18.7 jit_solution(1576368125076037547)
XLA Ops:
  0.0 1.0 %shard_map.64 = (f32[8,128]{1,0:T(8,128)S(1)}, f32[8,128]{1,0:T(8,128)S(1)}, f32[5,32,128]{2,1,0:T(8,128)S(1)}, s32[1,512]{1,0:T(1,128)S(1)}, f32[1,512]{1,0:T(1,128)S(1)}, /*index=5*/f32[1,512]{1,0:T(1,128)S(1)}) custom-call(f32[4,32,128]{2,1,0:T(8,128)} %u_hbm.1, f32[32,128]{1,0:T(8,128)} %wind_hbm.1, s32[1,512]{1,0:T(1,128)} %refs_0_.1, ...), custom_call_target="tpu_custom_call" | custom-call | tf_op jit(solution)/shard_map/pallas_call | solution.py:437
  1.0 3.1 %collective-permute-start = (f32[8,128]{1,0:T(8,128)S(1)}, f32[8,128]{1,0:T(8,128)S(1)}, u32[]{:S(2)}, u32[]{:S(2)}) collective-permute-start(f32[8,128]{1,0:T(8,128)S(1)} %get-tuple-element.18), channel_id=1, source_target_pairs={{0,8},{8,16},{16,24},{24,0},{1,9},{9,17},{17,25},{25,1},{2,10},{10... | collective-permute-start | bytes 12296 | tf_op jit(solution)/shard_map/ppermute | solution.py:473
  4.1 2.1 %collective-permute-start.1 = (f32[8,128]{1,0:T(8,128)S(1)}, f32[8,128]{1,0:T(8,128)S(1)}, u32[]{:S(2)}, u32[]{:S(2)}) collective-permute-start(f32[8,128]{1,0:T(8,128)S(1)} %get-tuple-element.19), channel_id=1, source_target_pairs={{0,24},{8,0},{16,8},{24,16},{1,25},{9,1},{17,9},{25,17},{2,26},{10... | collective-permute-start | bytes 12296 | tf_op jit(solution)/shard_map/ppermute | solution.py:472
  6.8 0.4 %shard_map.65 = (f32[136,128]{1,0:T(8,128)S(1)}, f32[64,128]{1,0:T(8,128)S(1)}) custom-call(s32[1]{0:T(128)S(6)} %copy.7.count_ref, f32[5,32,128]{2,1,0:T(8,128)S(1)} %get-tuple-element.13.u_ref, s32[1,512]{1,0:T(1,128)S(1)} %get-tuple-element.14.cell_ref, f32[1,512]{1,0:T(1,128)S(1)} %get-tuple-element.15.value_ref, f32[1,512]{1,0:T(1,128)S(1)} %get-tuple-element.16.weight_ref), custom_call_target="tpu_custom_call" | custom-call | tf_op jit(solution)/shard_map/pallas_call | solution.py:437
  7.2 0.5 %collective-permute-done.west_ref = f32[8,128]{1,0:T(8,128)S(1)} collective-permute-done((f32[8,128]{1,0:T(8,128)S(1)}, f32[8,128]{1,0:T(8,128)S(1)}, u32[]{:S(2)}, u32[]{:S(2)}) %collective-permute-start) | collective-permute-done | bytes 4128 | tf_op jit(solution)/shard_map/ppermute | solution.py:473
  7.7 0.0 collective-permute-done.1.east_ref
  7.7 0.4 %shard_map.66 = f32[136,128]{1,0:T(8,128)S(1)} custom-call(f32[64,128]{1,0:T(8,128)S(1)} %get-tuple-element.17.q_ref, f32[8,128]{1,0:T(8,128)S(1)} %collective-permute-done.west_ref, f32[8,128]{1,0:T(8,128)S(1)} %collective-permute-done.1.east_ref, f32[136,128]{1,0:T(8,128)S(1)} %get-tuple-element.20.f_in_ref), custom_call_target="tpu_custom_call" | custom-call | tf_op jit(solution)/shard_map/pallas_call | solution.py:437
  8.1 1.2 %collective-permute-start.2 = (f32[136,128]{1,0:T(8,128)S(1)}, f32[136,128]{1,0:T(8,128)S(1)}, u32[]{:S(2)}, u32[]{:S(2)}) collective-permute-start(f32[136,128]{1,0:T(8,128)S(1)} %shard_map.66), channel_id=1, source_target_pairs={{0,7},{1,6},{2,5},{3,4},{4,3},{5,2},{6,1},{7,0},{8,15},{9,14},{10,... | collective-permute-start | bytes 208904 | tf_op jit(solution)/shard_map/ppermute | solution.py:485
  9.3 0.6 %collective-permute-start.3 = (f32[136,128]{1,0:T(8,128)S(1)}, f32[136,128]{1,0:T(8,128)S(1)}, u32[]{:S(2)}, u32[]{:S(2)}) collective-permute-start(f32[136,128]{1,0:T(8,128)S(1)} %shard_map.66), channel_id=1, source_target_pairs={{0,2},{1,5},{2,0},{3,7},{4,6},{5,1},{6,4},{7,3},{8,10},{9,13},{10,... | collective-permute-start | bytes 208904 | tf_op jit(solution)/shard_map/ppermute | solution.py:485
  9.9 2.3 %collective-permute-start.4 = (f32[136,128]{1,0:T(8,128)S(1)}, f32[136,128]{1,0:T(8,128)S(1)}, u32[]{:S(2)}, u32[]{:S(2)}) collective-permute-start(f32[136,128]{1,0:T(8,128)S(1)} %shard_map.66), channel_id=1, source_target_pairs={{0,5},{1,2},{2,7},{3,0},{4,1},{5,6},{6,3},{7,4},{8,13},{9,10},{10,... | collective-permute-start | bytes 208904 | tf_op jit(solution)/shard_map/ppermute | solution.py:485
  12.3 1.0 %collective-permute-done.2 = f32[136,128]{1,0:T(8,128)S(1)} collective-permute-done((f32[136,128]{1,0:T(8,128)S(1)}, f32[136,128]{1,0:T(8,128)S(1)}, u32[]{:S(2)}, u32[]{:S(2)}) %collective-permute-start.2) | collective-permute-done | bytes 69664 | tf_op jit(solution)/shard_map/ppermute | solution.py:485
  13.3 0.2 collective-permute-start.5
  13.5 0.8 %collective-permute-done.3 = f32[136,128]{1,0:T(8,128)S(1)} collective-permute-done((f32[136,128]{1,0:T(8,128)S(1)}, f32[136,128]{1,0:T(8,128)S(1)}, u32[]{:S(2)}, u32[]{:S(2)}) %collective-permute-start.3) | collective-permute-done | bytes 69664 | tf_op jit(solution)/shard_map/ppermute | solution.py:485
  14.3 0.1 collective-permute-start.6
  14.4 0.1 collective-permute-done.4
  14.5 0.3 %collective-permute-start.7 = (f32[136,128]{1,0:T(8,128)S(1)}, f32[136,128]{1,0:T(8,128)S(1)}, u32[]{:S(2)}, u32[]{:S(2)}) collective-permute-start(f32[136,128]{1,0:T(8,128)S(1)} %collective-permute-done.4), channel_id=1, source_target_pairs={{0,1},{1,0},{2,3},{3,2},{4,5},{5,4},{6,7},{7,6},{8,9},{9,8},{10,11... | collective-permute-start | bytes 208904 | tf_op jit(solution)/shard_map/ppermute | solution.py:480
  14.9 0.6 %collective-permute-done.6 = f32[136,128]{1,0:T(8,128)S(1)} collective-permute-done((f32[136,128]{1,0:T(8,128)S(1)}, f32[136,128]{1,0:T(8,128)S(1)}, u32[]{:S(2)}, u32[]{:S(2)}) %collective-permute-start.6) | collective-permute-done | bytes 69664 | tf_op jit(solution)/shard_map/ppermute | solution.py:480
  15.5 0.3 %collective-permute-done.7 = f32[136,128]{1,0:T(8,128)S(1)} collective-permute-done((f32[136,128]{1,0:T(8,128)S(1)}, f32[136,128]{1,0:T(8,128)S(1)}, u32[]{:S(2)}, u32[]{:S(2)}) %collective-permute-start.7) | collective-permute-done | bytes 69664 | tf_op jit(solution)/shard_map/ppermute | solution.py:480
  15.8 0.0 collective-permute-done.5
  15.8 2.8 %shard_map.67 = f32[128,128]{1,0:T(8,128)} custom-call(s32[1]{0:T(128)} %bitcast.me_ref, f32[544,128]{1,0:T(8,128)S(1)} %pad_maximum_fusion.cat_ref, f32[544,128]{1,0:T(8,128)S(1)} %pad_maximum_fusion.1.sib_ref), custom_call_target="tpu_custom_call" | custom-call | tf_op jit(solution)/shard_map/pallas_call | solution.py:437
  (3 shorter events, 0.0 us)
Async XLA Ops:
  1.0 6.7 %collective-permute-start = (f32[8,128]{1,0:T(8,128)S(1)}, f32[8,128]{1,0:T(8,128)S(1)}, u32[]{:S(2)}, u32[]{:S(2)}) collective-permute-start(f32[8,128]{1,0:T(8,128)S(1)} %get-tuple-element.18), channel_id=1, source_target_pairs={{0,8},{8,16},{16,24},{24,0},{1,9},{9,17},{17,25},{25,1},{2,10},{10... | collective-permute-start | bytes 12296 | tf_op jit(solution)/shard_map/ppermute | solution.py:473
  4.1 3.7 %collective-permute-start.1 = (f32[8,128]{1,0:T(8,128)S(1)}, f32[8,128]{1,0:T(8,128)S(1)}, u32[]{:S(2)}, u32[]{:S(2)}) collective-permute-start(f32[8,128]{1,0:T(8,128)S(1)} %get-tuple-element.19), channel_id=1, source_target_pairs={{0,24},{8,0},{16,8},{24,16},{1,25},{9,1},{17,9},{25,17},{2,26},{10... | collective-permute-start | bytes 12296 | tf_op jit(solution)/shard_map/ppermute | solution.py:472
  8.1 5.2 %collective-permute-start.2 = (f32[136,128]{1,0:T(8,128)S(1)}, f32[136,128]{1,0:T(8,128)S(1)}, u32[]{:S(2)}, u32[]{:S(2)}) collective-permute-start(f32[136,128]{1,0:T(8,128)S(1)} %shard_map.66), channel_id=1, source_target_pairs={{0,7},{1,6},{2,5},{3,4},{4,3},{5,2},{6,1},{7,0},{8,15},{9,14},{10,... | collective-permute-start | bytes 208904 | tf_op jit(solution)/shard_map/ppermute | solution.py:485
  9.3 5.0 %collective-permute-start.3 = (f32[136,128]{1,0:T(8,128)S(1)}, f32[136,128]{1,0:T(8,128)S(1)}, u32[]{:S(2)}, u32[]{:S(2)}) collective-permute-start(f32[136,128]{1,0:T(8,128)S(1)} %shard_map.66), channel_id=1, source_target_pairs={{0,2},{1,5},{2,0},{3,7},{4,6},{5,1},{6,4},{7,3},{8,10},{9,13},{10,... | collective-permute-start | bytes 208904 | tf_op jit(solution)/shard_map/ppermute | solution.py:485
  9.9 4.6 %collective-permute-start.4 = (f32[136,128]{1,0:T(8,128)S(1)}, f32[136,128]{1,0:T(8,128)S(1)}, u32[]{:S(2)}, u32[]{:S(2)}) collective-permute-start(f32[136,128]{1,0:T(8,128)S(1)} %shard_map.66), channel_id=1, source_target_pairs={{0,5},{1,2},{2,7},{3,0},{4,1},{5,6},{6,3},{7,4},{8,13},{9,10},{10,... | collective-permute-start | bytes 208904 | tf_op jit(solution)/shard_map/ppermute | solution.py:485
  13.3 2.5 %collective-permute-start.5 = (f32[272,128]{1,0:T(8,128)S(1)}, f32[272,128]{1,0:T(8,128)S(1)}, u32[]{:S(2)}, u32[]{:S(2)}) collective-permute-start(f32[272,128]{1,0:T(8,128)S(1)} %pad_maximum_fusion.2), channel_id=1, source_target_pairs={{0,1},{1,0},{2,3},{3,2},{4,5},{5,4},{6,7},{7,6},{8,9},{9,8},{10,11... | collective-permute-start | bytes 417800 | tf_op jit(solution)/shard_map/ppermute | solution.py:480
  14.3 1.3 %collective-permute-start.6 = (f32[136,128]{1,0:T(8,128)S(1)}, f32[136,128]{1,0:T(8,128)S(1)}, u32[]{:S(2)}, u32[]{:S(2)}) collective-permute-start(f32[136,128]{1,0:T(8,128)S(1)} %collective-permute-done.3), channel_id=1, source_target_pairs={{0,1},{1,0},{2,3},{3,2},{4,5},{5,4},{6,7},{7,6},{8,9},{9,8},{10,11... | collective-permute-start | bytes 208904 | tf_op jit(solution)/shard_map/ppermute | solution.py:480
  14.5 1.3 %collective-permute-start.7 = (f32[136,128]{1,0:T(8,128)S(1)}, f32[136,128]{1,0:T(8,128)S(1)}, u32[]{:S(2)}, u32[]{:S(2)}) collective-permute-start(f32[136,128]{1,0:T(8,128)S(1)} %collective-permute-done.4), channel_id=1, source_target_pairs={{0,1},{1,0},{2,3},{3,2},{4,5},{5,4},{6,7},{7,6},{8,9},{9,8},{10,11... | collective-permute-start | bytes 208904 | tf_op jit(solution)/shard_map/ppermute | solution.py:480

commit v9 on v7

--- a/solution.py
+++ b/solution.py
@@ -123,18 +123,18 @@
     obs_hbm, (east_ref, west_ref, u_ref), obs_ref, sems = refs[:3], refs[3:6], refs[6:9], refs[9]
     members = u_hbm.shape[0]
     pairs = [(wind_hbm, u_ref.at[members])]
-    pairs += [(u_hbm.at[m], u_ref.at[m]) for m in range(members)]
+    pairs += [(u_hbm.at[m : m + 2], u_ref.at[m : m + 2]) for m in range(0, members, 2)]
     pairs += [*zip(obs_hbm, obs_ref)]
     copies = [pltpu.make_async_copy(a, b, sems.at[i]) for i, (a, b) in enumerate(pairs)]
     for copy in copies:
         copy.start()
     copies[0].wait()
     moved_wind = pltpu.roll(u_ref[members], SUBSTEPS, 1)
-    for copy in copies[1 : 1 + members]:
+    for copy in copies[1 : 1 + members // 2]:
         copy.wait()
     east_ref[...] = packet(u_ref, moved_wind, LANES - SUBSTEPS)
     west_ref[...] = packet(u_ref, moved_wind, 0)
-    for copy in copies[1 + members :]:
+    for copy in copies[1 + members // 2 :]:
         copy.wait()
 
 

time: 18.9 us -> 18.9 us (level)
  no operation moved by 1% of the time
where the time goes in v9:
time: 18.9 us; the launch traced here: 18.7 us
  starting transfers between devices  9.16 us (48%)
  Pallas kernels  4.58 us (24%)
  waiting for transfers between devices  4.18 us (22%)
  between operations  0.7 us (4%)
    pallas_call x4, Pallas kernels, call(): pl.pallas_call(body, out_shape=[typed(shape) for shape in out_shapes], in...  4.58 us
    ppermute x6, starting transfers between devices, swap(): return lax.ppermute(x, 'member', [(i, i ^ k) for i in range(groups)])  4 us
    ppermute x6, waiting for transfers between devices, swap(): return lax.ppermute(x, 'member', [(i, i ^ k) for i in range(groups)])  3.67 us
    ppermute x1, starting transfers between devices, gathered(): west = lax.ppermute(eastern, 'space', forward)  3.08 us
    ppermute x1, starting transfers between devices, gathered(): east = lax.ppermute(western, 'space', backward)  2.09 us
    ppermute x1, waiting for transfers between devices, gathered(): west = lax.ppermute(eastern, 'space', forward)  0.5 us
  transfers between devices with their start and end apart: 8, of which 5 were waited for; matrix products, arithmetic and copies ran while one was open for 0% of the time, Pallas kernels for 2%

profile of v9, /device:TPU:0, one launch (start us, length us, event | category | flops | bytes accessed | tf_op | source)
XLA Modules:
  0.0 18.7 jit_solution(4811095445427512842)
XLA Ops:
  0.0 1.0 %shard_map.64 = (f32[8,128]{1,0:T(8,128)S(1)}, f32[8,128]{1,0:T(8,128)S(1)}, f32[5,32,128]{2,1,0:T(8,128)S(1)}, s32[1,512]{1,0:T(1,128)S(1)}, f32[1,512]{1,0:T(1,128)S(1)}, /*index=5*/f32[1,512]{1,0:T(1,128)S(1)}) custom-call(f32[4,32,128]{2,1,0:T(8,128)} %u_hbm.1, f32[32,128]{1,0:T(8,128)} %wind_hbm.1, s32[1,512]{1,0:T(1,128)} %refs_0_.1, ...), custom_call_target="tpu_custom_call" | custom-call | tf_op jit(solution)/shard_map/pallas_call | solution.py:430
  1.0 3.1 %collective-permute-start = (f32[8,128]{1,0:T(8,128)S(1)}, f32[8,128]{1,0:T(8,128)S(1)}, u32[]{:S(2)}, u32[]{:S(2)}) collective-permute-start(f32[8,128]{1,0:T(8,128)S(1)} %get-tuple-element.18), channel_id=1, source_target_pairs={{0,8},{8,16},{16,24},{24,0},{1,9},{9,17},{17,25},{25,1},{2,10},{10... | collective-permute-start | bytes 12296 | tf_op jit(solution)/shard_map/ppermute | solution.py:466
  4.1 2.1 %collective-permute-start.1 = (f32[8,128]{1,0:T(8,128)S(1)}, f32[8,128]{1,0:T(8,128)S(1)}, u32[]{:S(2)}, u32[]{:S(2)}) collective-permute-start(f32[8,128]{1,0:T(8,128)S(1)} %get-tuple-element.19), channel_id=1, source_target_pairs={{0,24},{8,0},{16,8},{24,16},{1,25},{9,1},{17,9},{25,17},{2,26},{10... | collective-permute-start | bytes 12296 | tf_op jit(solution)/shard_map/ppermute | solution.py:465
  6.8 0.4 %shard_map.65 = (f32[136,128]{1,0:T(8,128)S(1)}, f32[64,128]{1,0:T(8,128)S(1)}) custom-call(s32[1]{0:T(128)S(6)} %copy.7.count_ref, f32[5,32,128]{2,1,0:T(8,128)S(1)} %get-tuple-element.13.u_ref, s32[1,512]{1,0:T(1,128)S(1)} %get-tuple-element.14.cell_ref, f32[1,512]{1,0:T(1,128)S(1)} %get-tuple-element.15.value_ref, f32[1,512]{1,0:T(1,128)S(1)} %get-tuple-element.16.weight_ref), custom_call_target="tpu_custom_call" | custom-call | tf_op jit(solution)/shard_map/pallas_call | solution.py:430
  7.2 0.5 %collective-permute-done.west_ref = f32[8,128]{1,0:T(8,128)S(1)} collective-permute-done((f32[8,128]{1,0:T(8,128)S(1)}, f32[8,128]{1,0:T(8,128)S(1)}, u32[]{:S(2)}, u32[]{:S(2)}) %collective-permute-start) | collective-permute-done | bytes 4128 | tf_op jit(solution)/shard_map/ppermute | solution.py:466
  7.7 0.0 collective-permute-done.1.east_ref
  7.7 0.4 %shard_map.66 = f32[136,128]{1,0:T(8,128)S(1)} custom-call(f32[64,128]{1,0:T(8,128)S(1)} %get-tuple-element.17.q_ref, f32[8,128]{1,0:T(8,128)S(1)} %collective-permute-done.west_ref, f32[8,128]{1,0:T(8,128)S(1)} %collective-permute-done.1.east_ref, f32[136,128]{1,0:T(8,128)S(1)} %get-tuple-element.20.f_in_ref), custom_call_target="tpu_custom_call" | custom-call | tf_op jit(solution)/shard_map/pallas_call | solution.py:430
  8.1 1.2 %collective-permute-start.2 = (f32[136,128]{1,0:T(8,128)S(1)}, f32[136,128]{1,0:T(8,128)S(1)}, u32[]{:S(2)}, u32[]{:S(2)}) collective-permute-start(f32[136,128]{1,0:T(8,128)S(1)} %shard_map.66), channel_id=1, source_target_pairs={{0,7},{1,6},{2,5},{3,4},{4,3},{5,2},{6,1},{7,0},{8,15},{9,14},{10,... | collective-permute-start | bytes 208904 | tf_op jit(solution)/shard_map/ppermute | solution.py:473
  9.3 0.6 %collective-permute-start.3 = (f32[136,128]{1,0:T(8,128)S(1)}, f32[136,128]{1,0:T(8,128)S(1)}, u32[]{:S(2)}, u32[]{:S(2)}) collective-permute-start(f32[136,128]{1,0:T(8,128)S(1)} %shard_map.66), channel_id=1, source_target_pairs={{0,2},{1,3},{2,0},{3,1},{4,6},{5,7},{6,4},{7,5},{8,10},{9,11},{10,... | collective-permute-start | bytes 208904 | tf_op jit(solution)/shard_map/ppermute | solution.py:473
  9.9 1.2 %collective-permute-start.4 = (f32[136,128]{1,0:T(8,128)S(1)}, f32[136,128]{1,0:T(8,128)S(1)}, u32[]{:S(2)}, u32[]{:S(2)}) collective-permute-start(f32[136,128]{1,0:T(8,128)S(1)} %shard_map.66), channel_id=1, source_target_pairs={{0,5},{1,4},{2,7},{3,6},{4,1},{5,0},{6,3},{7,2},{8,13},{9,12},{10,... | collective-permute-start | bytes 208904 | tf_op jit(solution)/shard_map/ppermute | solution.py:473
  11.1 2.2 %collective-permute-done.2 = f32[136,128]{1,0:T(8,128)S(1)} collective-permute-done((f32[136,128]{1,0:T(8,128)S(1)}, f32[136,128]{1,0:T(8,128)S(1)}, u32[]{:S(2)}, u32[]{:S(2)}) %collective-permute-start.2) | collective-permute-done | bytes 69664 | tf_op jit(solution)/shard_map/ppermute | solution.py:473
  13.3 0.2 %collective-permute-start.5 = (f32[272,128]{1,0:T(8,128)S(1)}, f32[272,128]{1,0:T(8,128)S(1)}, u32[]{:S(2)}, u32[]{:S(2)}) collective-permute-start(f32[272,128]{1,0:T(8,128)S(1)} %pad_maximum_fusion.2), channel_id=1, source_target_pairs={{0,1},{1,0},{2,3},{3,2},{4,5},{5,4},{6,7},{7,6},{8,9},{9,8},{10,11... | collective-permute-start | bytes 417800 | tf_op jit(solution)/shard_map/ppermute | solution.py:473
  13.5 0.6 %collective-permute-done.3 = f32[136,128]{1,0:T(8,128)S(1)} collective-permute-done((f32[136,128]{1,0:T(8,128)S(1)}, f32[136,128]{1,0:T(8,128)S(1)}, u32[]{:S(2)}, u32[]{:S(2)}) %collective-permute-start.3) | collective-permute-done | bytes 69664 | tf_op jit(solution)/shard_map/ppermute | solution.py:473
  14.1 0.3 %collective-permute-start.6 = (f32[136,128]{1,0:T(8,128)S(1)}, f32[136,128]{1,0:T(8,128)S(1)}, u32[]{:S(2)}, u32[]{:S(2)}) collective-permute-start(f32[136,128]{1,0:T(8,128)S(1)} %collective-permute-done.3), channel_id=1, source_target_pairs={{0,1},{1,0},{2,3},{3,2},{4,5},{5,4},{6,7},{7,6},{8,9},{9,8},{10,11... | collective-permute-start | bytes 208904 | tf_op jit(solution)/shard_map/ppermute | solution.py:473
  14.4 0.0 collective-permute-done.4
  14.4 0.5 %collective-permute-start.7 = (f32[136,128]{1,0:T(8,128)S(1)}, f32[136,128]{1,0:T(8,128)S(1)}, u32[]{:S(2)}, u32[]{:S(2)}) collective-permute-start(f32[136,128]{1,0:T(8,128)S(1)} %collective-permute-done.4), channel_id=1, source_target_pairs={{0,1},{1,0},{2,3},{3,2},{4,5},{5,4},{6,7},{7,6},{8,9},{9,8},{10,11... | collective-permute-start | bytes 208904 | tf_op jit(solution)/shard_map/ppermute | solution.py:473
  14.9 0.5 %collective-permute-done.6 = f32[136,128]{1,0:T(8,128)S(1)} collective-permute-done((f32[136,128]{1,0:T(8,128)S(1)}, f32[136,128]{1,0:T(8,128)S(1)}, u32[]{:S(2)}, u32[]{:S(2)}) %collective-permute-start.6) | collective-permute-done | bytes 69664 | tf_op jit(solution)/shard_map/ppermute | solution.py:473
  15.4 0.4 %collective-permute-done.7 = f32[136,128]{1,0:T(8,128)S(1)} collective-permute-done((f32[136,128]{1,0:T(8,128)S(1)}, f32[136,128]{1,0:T(8,128)S(1)}, u32[]{:S(2)}, u32[]{:S(2)}) %collective-permute-start.7) | collective-permute-done | bytes 69664 | tf_op jit(solution)/shard_map/ppermute | solution.py:473
  15.8 0.0 collective-permute-done.5
  15.8 2.8 %shard_map.67 = f32[128,128]{1,0:T(8,128)} custom-call(s32[1]{0:T(128)} %bitcast.me_ref, f32[544,128]{1,0:T(8,128)S(1)} %pad_maximum_fusion.cat_ref, f32[544,128]{1,0:T(8,128)S(1)} %pad_maximum_fusion.1.sib_ref), custom_call_target="tpu_custom_call" | custom-call | tf_op jit(solution)/shard_map/pallas_call | solution.py:430
  (3 shorter events, 0.0 us)
Async XLA Ops:
  1.0 6.7 %collective-permute-start = (f32[8,128]{1,0:T(8,128)S(1)}, f32[8,128]{1,0:T(8,128)S(1)}, u32[]{:S(2)}, u32[]{:S(2)}) collective-permute-start(f32[8,128]{1,0:T(8,128)S(1)} %get-tuple-element.18), channel_id=1, source_target_pairs={{0,8},{8,16},{16,24},{24,0},{1,9},{9,17},{17,25},{25,1},{2,10},{10... | collective-permute-start | bytes 12296 | tf_op jit(solution)/shard_map/ppermute | solution.py:466
  4.1 3.7 %collective-permute-start.1 = (f32[8,128]{1,0:T(8,128)S(1)}, f32[8,128]{1,0:T(8,128)S(1)}, u32[]{:S(2)}, u32[]{:S(2)}) collective-permute-start(f32[8,128]{1,0:T(8,128)S(1)} %get-tuple-element.19), channel_id=1, source_target_pairs={{0,24},{8,0},{16,8},{24,16},{1,25},{9,1},{17,9},{25,17},{2,26},{10... | collective-permute-start | bytes 12296 | tf_op jit(solution)/shard_map/ppermute | solution.py:465
  8.1 5.2 %collective-permute-start.2 = (f32[136,128]{1,0:T(8,128)S(1)}, f32[136,128]{1,0:T(8,128)S(1)}, u32[]{:S(2)}, u32[]{:S(2)}) collective-permute-start(f32[136,128]{1,0:T(8,128)S(1)} %shard_map.66), channel_id=1, source_target_pairs={{0,7},{1,6},{2,5},{3,4},{4,3},{5,2},{6,1},{7,0},{8,15},{9,14},{10,... | collective-permute-start | bytes 208904 | tf_op jit(solution)/shard_map/ppermute | solution.py:473
  9.3 4.8 %collective-permute-start.3 = (f32[136,128]{1,0:T(8,128)S(1)}, f32[136,128]{1,0:T(8,128)S(1)}, u32[]{:S(2)}, u32[]{:S(2)}) collective-permute-start(f32[136,128]{1,0:T(8,128)S(1)} %shard_map.66), channel_id=1, source_target_pairs={{0,2},{1,3},{2,0},{3,1},{4,6},{5,7},{6,4},{7,5},{8,10},{9,11},{10,... | collective-permute-start | bytes 208904 | tf_op jit(solution)/shard_map/ppermute | solution.py:473
  9.9 4.5 %collective-permute-start.4 = (f32[136,128]{1,0:T(8,128)S(1)}, f32[136,128]{1,0:T(8,128)S(1)}, u32[]{:S(2)}, u32[]{:S(2)}) collective-permute-start(f32[136,128]{1,0:T(8,128)S(1)} %shard_map.66), channel_id=1, source_target_pairs={{0,5},{1,4},{2,7},{3,6},{4,1},{5,0},{6,3},{7,2},{8,13},{9,12},{10,... | collective-permute-start | bytes 208904 | tf_op jit(solution)/shard_map/ppermute | solution.py:473
  13.3 2.5 %collective-permute-start.5 = (f32[272,128]{1,0:T(8,128)S(1)}, f32[272,128]{1,0:T(8,128)S(1)}, u32[]{:S(2)}, u32[]{:S(2)}) collective-permute-start(f32[272,128]{1,0:T(8,128)S(1)} %pad_maximum_fusion.2), channel_id=1, source_target_pairs={{0,1},{1,0},{2,3},{3,2},{4,5},{5,4},{6,7},{7,6},{8,9},{9,8},{10,11... | collective-permute-start | bytes 417800 | tf_op jit(solution)/shard_map/ppermute | solution.py:473
  14.1 1.3 %collective-permute-start.6 = (f32[136,128]{1,0:T(8,128)S(1)}, f32[136,128]{1,0:T(8,128)S(1)}, u32[]{:S(2)}, u32[]{:S(2)}) collective-permute-start(f32[136,128]{1,0:T(8,128)S(1)} %collective-permute-done.3), channel_id=1, source_target_pairs={{0,1},{1,0},{2,3},{3,2},{4,5},{5,4},{6,7},{7,6},{8,9},{9,8},{10,11... | collective-permute-start | bytes 208904 | tf_op jit(solution)/shard_map/ppermute | solution.py:473
  14.4 1.4 %collective-permute-start.7 = (f32[136,128]{1,0:T(8,128)S(1)}, f32[136,128]{1,0:T(8,128)S(1)}, u32[]{:S(2)}, u32[]{:S(2)}) collective-permute-start(f32[136,128]{1,0:T(8,128)S(1)} %collective-permute-done.4), channel_id=1, source_target_pairs={{0,1},{1,0},{2,3},{3,2},{4,5},{5,4},{6,7},{7,6},{8,9},{9,8},{10,11... | collective-permute-start | bytes 208904 | tf_op jit(solution)/shard_map/ppermute | solution.py:473
